TPU v7x, 32 devices: a whole 2x2x4 slice. The times are simulated.
32 devices in a mesh: wide: 16 (over z, y, x), narrow: 2 (over core).
Axes of the slice: x: 2, y: 2, z: 4, core: 2. Of those that a mesh axis runs over, the one named last changes fastest.
Arguments:
- layer_input: bfloat16 [8192, 2048], P(('wide', 'narrow')), may hold values from -6 to 6
- doc_lengths: int32 [16, 4], P('wide'), may hold values from 1 to 256, 512 in all within a row
- w_query: bfloat16 [2048, 2048], P('wide', 'narrow'), may hold values from -0.125 to 0.125
- w_key: bfloat16 [2048, 2048], P('wide', 'narrow'), may hold values from -0.125 to 0.125
- w_value: bfloat16 [2048, 2048], P('wide', 'narrow'), may hold values from -0.125 to 0.125
- w_gate: bfloat16 [2048, 2048], P('wide', 'narrow'), may hold values from -0.125 to 0.125
- w_output: bfloat16 [2048, 2048], P('wide', 'narrow'), may hold values from -0.125 to 0.125
- w_left: bfloat16 [2048, 5632], P('wide', 'narrow'), may hold values from -0.125 to 0.125
- w_right: bfloat16 [2048, 5632], P('wide', 'narrow'), may hold values from -0.125 to 0.125
- w_down: bfloat16 [2048, 5632], P('wide', 'narrow'), may hold values from -0.078125 to 0.078125
- cotangent: bfloat16 [8192, 2048], P(('wide', 'narrow')), may hold values from -6 to 6
Outputs:
- layer_output: bfloat16 [8192, 2048], P(('wide', 'narrow'))
- input_grad: float32 [8192, 2048], P(('wide', 'narrow'))
- grad_query: float32 [2048, 2048], P('wide', 'narrow')
- grad_key: float32 [2048, 2048], P('wide', 'narrow')
- grad_value: float32 [2048, 2048], P('wide', 'narrow')
- grad_gate: float32 [2048, 2048], P('wide', 'narrow')
- grad_output: float32 [2048, 2048], P('wide', 'narrow')
- grad_left: float32 [2048, 5632], P('wide', 'narrow')
- grad_right: float32 [2048, 5632], P('wide', 'narrow')
- grad_down: float32 [2048, 5632], P('wide', 'narrow')
Inputs may be any that keep to these rules, and one draw needn't show every extreme that they name: `doc_lengths`: in each packed row the 4 lengths add up to 512, the documents lying along the row in this order; the longest of every row has 256 tokens.
All inputs are finite; a program needn't handle non-finite values.
Results may differ from a plain program's by a relative error of at most 0.014.
Values may be sent and summed in bfloat16 or wider, within the bound.
A program may use at most 256 MiB of HBM per device.

v0:
```python
from functools import partial

import jax
import jax.numpy as jnp
from jax import lax
from jax.sharding import PartitionSpec as P

D = 2048
HEADS = 16
HEAD_DIM = 128
ROWS_GRP = 1
ROW_LEN = 512
GRP_TOK = 512


epsilon = 1e-06
decay_scale = 2.0


def norm_parts(values):
    norm_scale = lax.rsqrt(jnp.mean(values * values, axis=-1, keepdims=True) + epsilon)
    return (values * norm_scale, norm_scale)


def norm_back(values, norm_scale, gradient):
    inner_mean = jnp.mean(gradient * values, axis=-1, keepdims=True)
    return norm_scale * gradient - values * (norm_scale * norm_scale * norm_scale) * inner_mean


def silu_slope(values):
    sigmoid_val = jax.nn.sigmoid(values)
    return sigmoid_val * (1.0 + values * (1.0 - sigmoid_val))


def contract_rows(left_side, right_side):
    return lax.dot_general(
        left_side, right_side, (((0,), (0,)), ((), ())), preferred_element_type=jnp.float32
    )


def contract_cols(left_side, right_side):
    return lax.dot_general(
        left_side, right_side, (((1,), (1,)), ((), ())), preferred_element_type=jnp.float32
    )


def fetch_attention(w_query, w_key, w_value, w_gate, w_output):
    return (
        lax.all_gather(w_query, "wide", axis=0, tiled=True),
        lax.all_gather(w_key, "wide", axis=0, tiled=True),
        lax.all_gather(w_value, "wide", axis=0, tiled=True),
        lax.all_gather(w_gate, "wide", axis=0, tiled=True),
        lax.all_gather(w_output, "wide", axis=0, tiled=True),
    )


def fetch_feed(w_left, w_right, w_down):
    return (
        lax.all_gather(w_left, "wide", axis=0, tiled=True),
        lax.all_gather(w_right, "wide", axis=0, tiled=True),
        lax.all_gather(w_down, "wide", axis=0, tiled=True),
    )


def decay_mask(lengths, head_ids):
    starts = jnp.cumsum(lengths) - lengths
    places = jnp.arange(ROW_LEN, dtype=jnp.int32)
    doc_ids = jnp.sum((places[:, None] >= starts[None, :]).astype(jnp.int32), axis=1)
    causal = places[:, None] >= places[None, :]
    allowed = causal & (doc_ids[:, None] == doc_ids[None, :])
    spread = jnp.where(
        causal, (places[:, None] - places[None, :]).astype(jnp.float32), jnp.float32(0.0)
    )
    head_rates = decay_scale * head_ids.astype(jnp.float32) / HEADS
    weights = jnp.exp(-head_rates[:, None, None] * spread[None, :, :])
    return jnp.where(allowed[None, :, :], weights, jnp.float32(0.0))


def attend_row(row_parts, head_ids):
    queries, keys_row, values_row, lengths = row_parts
    decay_masks = decay_mask(lengths, head_ids)
    scores = jnp.einsum("ihd,jhd->hij", queries, keys_row, preferred_element_type=jnp.float32)
    attn_probs = (scores * decay_masks).astype(jnp.bfloat16)
    return jnp.einsum("hij,jhd->ihd", attn_probs, values_row, preferred_element_type=jnp.float32)


def attend_back(row_parts, head_ids):
    queries, keys_row, values_row, lengths, grad_mixed = row_parts
    decay_masks = decay_mask(lengths, head_ids)
    scores = jnp.einsum("ihd,jhd->hij", queries, keys_row, preferred_element_type=jnp.float32)
    attn_probs = (scores * decay_masks).astype(jnp.bfloat16)
    grad_probs = jnp.einsum(
        "ihd,jhd->hij", grad_mixed, values_row, preferred_element_type=jnp.float32
    )
    grad_values = jnp.einsum(
        "hij,ihd->jhd", attn_probs, grad_mixed, preferred_element_type=jnp.float32
    )
    grad_scores = (grad_probs * decay_masks).astype(jnp.bfloat16)
    grad_queries = jnp.einsum(
        "hij,jhd->ihd", grad_scores, keys_row, preferred_element_type=jnp.float32
    )
    grad_keys = jnp.einsum("hij,ihd->jhd", grad_scores, queries, preferred_element_type=jnp.float32)
    return (grad_queries, grad_keys, grad_values)


def on_device(
    layer_input,
    doc_lengths,
    w_query,
    w_key,
    w_value,
    w_gate,
    w_output,
    w_left,
    w_right,
    w_down,
    cotangent,
):
    inputs = layer_input.astype(jnp.float32)
    normed_local, norm_one = norm_parts(inputs)
    normed_all = lax.all_gather(normed_local.astype(jnp.bfloat16), "narrow", axis=0, tiled=True)
    query_full, key_full, value_full, gate_full, output_full = fetch_attention(
        w_query, w_key, w_value, w_gate, w_output
    )
    left_full, right_full, down_full = fetch_feed(w_left, w_right, w_down)
    query_pre = jnp.dot(normed_all, query_full, preferred_element_type=jnp.float32)
    key_pre = jnp.dot(normed_all, key_full, preferred_element_type=jnp.float32)
    queries = jax.nn.silu(query_pre).astype(jnp.bfloat16)
    keys_all = jax.nn.silu(key_pre).astype(jnp.bfloat16)
    values_all = jnp.dot(normed_all, value_full, preferred_element_type=jnp.float32).astype(
        jnp.bfloat16
    )
    gate_all = jnp.dot(normed_all, gate_full, preferred_element_type=jnp.float32)
    local_heads = query_full.shape[1] // HEAD_DIM
    width_local = local_heads * HEAD_DIM
    head_ids = lax.axis_index("narrow") * local_heads + jnp.arange(local_heads, dtype=jnp.int32)
    split_shape = (ROWS_GRP, ROW_LEN, local_heads, HEAD_DIM)
    query_rows = queries.reshape(split_shape)
    key_rows = keys_all.reshape(split_shape)
    value_rows = values_all.reshape(split_shape)
    mixed_out = lax.map(
        partial(attend_row, head_ids=head_ids), (query_rows, key_rows, value_rows, doc_lengths)
    )
    mixed_out = mixed_out.reshape(GRP_TOK, width_local)
    square_sum = lax.psum(jnp.sum(mixed_out * mixed_out, axis=1), "narrow")
    attn_scale = lax.rsqrt(square_sum / D + epsilon)[:, None]
    scaled = mixed_out * attn_scale
    blended = (gate_all * scaled).astype(jnp.bfloat16)
    row_block = blended
    middle = inputs + lax.psum_scatter(
        contract_cols(row_block, output_full), "narrow", scatter_dimension=0, tiled=True
    )
    mid_local, norm_two = norm_parts(middle)
    mid_all = lax.all_gather(mid_local.astype(jnp.bfloat16), "narrow", axis=0, tiled=True)
    left_all = jnp.dot(mid_all, left_full, preferred_element_type=jnp.float32)
    right_all = jnp.dot(mid_all, right_full, preferred_element_type=jnp.float32)
    product = (left_all * right_all).astype(jnp.bfloat16)
    row_block = product
    layer_output = (
        middle
        + lax.psum_scatter(
            contract_cols(row_block, down_full).astype(jnp.bfloat16),
            "narrow",
            scatter_dimension=0,
            tiled=True,
        ).astype(jnp.float32)
    ).astype(jnp.bfloat16)
    left_full, right_full, down_full = fetch_feed(w_left, w_right, w_down)
    query_full, key_full, value_full, gate_full, output_full = fetch_attention(
        w_query, w_key, w_value, w_gate, w_output
    )
    cot_all = lax.all_gather(cotangent, "narrow", axis=0, tiled=True)
    grad_product = jnp.dot(cot_all, down_full, preferred_element_type=jnp.float32)
    grad_left_pre = (grad_product * right_all).astype(jnp.bfloat16)
    grad_right_pre = (grad_product * left_all).astype(jnp.bfloat16)
    grad_mid = lax.psum_scatter(
        contract_cols(grad_left_pre, left_full) + contract_cols(grad_right_pre, right_full),
        "narrow",
        scatter_dimension=0,
        tiled=True,
    )
    grad_middle = cotangent.astype(jnp.float32) + norm_back(middle, norm_two, grad_mid)
    grad_down = contract_rows(cot_all, product)
    grad_left = contract_rows(mid_all, grad_left_pre)
    grad_right = contract_rows(mid_all, grad_right_pre)
    ffn_sums = (
        lax.psum_scatter(grad_left, "wide", scatter_dimension=0, tiled=True),
        lax.psum_scatter(grad_right, "wide", scatter_dimension=0, tiled=True),
        lax.psum_scatter(grad_down, "wide", scatter_dimension=0, tiled=True),
    )
    branch_grad = lax.all_gather(grad_middle.astype(jnp.bfloat16), "narrow", axis=0, tiled=True)
    grad_blended = jnp.dot(branch_grad, output_full, preferred_element_type=jnp.float32)
    grad_gate_pre = (grad_blended * scaled).astype(jnp.bfloat16)
    grad_scaled = grad_blended * gate_all
    inner_sum = lax.psum(jnp.sum(grad_scaled * mixed_out, axis=1), "narrow")
    scale_cube = attn_scale * attn_scale * attn_scale
    grad_mixed = (
        attn_scale * grad_scaled - mixed_out * scale_cube * (inner_sum / D)[:, None]
    ).astype(jnp.bfloat16)
    grad_query_rows, grad_key_rows, grad_value_rows = lax.map(
        partial(attend_back, head_ids=head_ids),
        (query_rows, key_rows, value_rows, doc_lengths, grad_mixed.reshape(split_shape)),
    )
    grad_query_pre = (grad_query_rows.reshape(GRP_TOK, width_local) * silu_slope(query_pre)).astype(
        jnp.bfloat16
    )
    grad_key_pre = (grad_key_rows.reshape(GRP_TOK, width_local) * silu_slope(key_pre)).astype(
        jnp.bfloat16
    )
    grad_value_pre = grad_value_rows.reshape(GRP_TOK, width_local).astype(jnp.bfloat16)
    total = contract_cols(grad_query_pre, query_full)
    total = total + contract_cols(grad_key_pre, key_full)
    total = total + contract_cols(grad_value_pre, value_full)
    grad_normed = lax.psum_scatter(
        (total + contract_cols(grad_gate_pre, gate_full)).astype(jnp.bfloat16),
        "narrow",
        scatter_dimension=0,
        tiled=True,
    ).astype(jnp.float32)
    input_grad = grad_middle + norm_back(inputs, norm_one, grad_normed)
    grad_output = contract_rows(branch_grad, blended)
    grad_query = contract_rows(normed_all, grad_query_pre)
    grad_key = contract_rows(normed_all, grad_key_pre)
    grad_value = contract_rows(normed_all, grad_value_pre)
    grad_gate = contract_rows(normed_all, grad_gate_pre)
    attn_sums = (
        lax.psum_scatter(grad_query, "wide", scatter_dimension=0, tiled=True),
        lax.psum_scatter(grad_key, "wide", scatter_dimension=0, tiled=True),
        lax.psum_scatter(grad_value, "wide", scatter_dimension=0, tiled=True),
        lax.psum_scatter(grad_gate, "wide", scatter_dimension=0, tiled=True),
        lax.psum_scatter(grad_output, "wide", scatter_dimension=0, tiled=True),
    )
    return (
        layer_output,
        input_grad,
        attn_sums[0],
        attn_sums[1],
        attn_sums[2],
        attn_sums[3],
        attn_sums[4],
        ffn_sums[0],
        ffn_sums[1],
        ffn_sums[2],
    )


def solution(mesh):
    in_specs = (
        P(("wide", "narrow"), None),
        P("wide", None),
        P("wide", "narrow"),
        P("wide", "narrow"),
        P("wide", "narrow"),
        P("wide", "narrow"),
        P("wide", "narrow"),
        P("wide", "narrow"),
        P("wide", "narrow"),
        P("wide", "narrow"),
        P(("wide", "narrow"), None),
    )
    out_specs = (
        P(("wide", "narrow"), None),
        P(("wide", "narrow"), None),
        P("wide", "narrow"),
        P("wide", "narrow"),
        P("wide", "narrow"),
        P("wide", "narrow"),
        P("wide", "narrow"),
        P("wide", "narrow"),
        P("wide", "narrow"),
        P("wide", "narrow"),
    )
    return jax.shard_map(
        on_device, mesh=mesh, in_specs=in_specs, out_specs=out_specs, check_vma=False
    )
```

profile of v0, /device:TPU:25, one launch (start us, length us, event | category | flops | bytes accessed | tf_op | source)
XLA Modules:
  0.0 3396.8 jit_solution(8083809339045837947)
XLA Ops:
  15.8 8.5 all-gather.13.cloned.1.call-done
  24.3 77.9 %all-gather.21.cloned.1.call-done = bf16[2048,1024]{1,0:T(8,128)(2,1)} async-done(((bf16[128,1024]{1,0:T(8,128)(2,1)}), bf16[2048,1024]{1,0:T(8,128)(2,1)}) %all-gather.21.cloned.1.call-update) | async-done | bytes 4194320 | tf_op jit(solution)/shard_map/all_gather | solution.py:50
  102.2 6.7 multiply_convert_fusion.10
  109.4 70.3 %all-gather.19.cloned.1.call-done = bf16[2048,1024]{1,0:T(8,128)(2,1)} async-done(((bf16[128,1024]{1,0:T(8,128)(2,1)}), bf16[2048,1024]{1,0:T(8,128)(2,1)}) %all-gather.19.cloned.1.call-update) | async-done | bytes 4194320 | tf_op jit(solution)/shard_map/all_gather | solution.py:49
  179.7 7.0 multiply_convert_fusion.11
  188.2 4.5 multiply_convert_fusion.1
  192.7 64.4 %all-gather.17.cloned.1.call-done = bf16[2048,1024]{1,0:T(8,128)(2,1)} async-done(((bf16[128,1024]{1,0:T(8,128)(2,1)}), bf16[2048,1024]{1,0:T(8,128)(2,1)}) %all-gather.17.cloned.1.call-update) | async-done | bytes 4194320 | tf_op jit(solution)/shard_map/all_gather | solution.py:51
  257.0 5.3 fusion.7
  270.1 64.3 %all-gather.15.cloned.1.call-done = bf16[2048,1024]{1,0:T(8,128)(2,1)} async-done(((bf16[128,1024]{1,0:T(8,128)(2,1)}), bf16[2048,1024]{1,0:T(8,128)(2,1)}) %all-gather.15.cloned.1.call-update) | async-done | bytes 4194320 | tf_op jit(solution)/shard_map/all_gather | solution.py:52
  334.4 6.6 multiply_convert_fusion.9
  341.0 70.7 %all-gather.23.cloned.1.call-done = bf16[2048,1024]{1,0:T(8,128)(2,1)} async-done(((bf16[128,1024]{1,0:T(8,128)(2,1)}), bf16[2048,1024]{1,0:T(8,128)(2,1)}) %all-gather.23.cloned.1.call-update) | async-done | bytes 4194320 | tf_op jit(solution)/shard_map/all_gather | solution.py:53
  411.7 6.5 fusion.15
  418.3 12.9 reduce-scatter.13.cloned.1.call-done
  437.4 9.3 all-gather.25.cloned.1.call-done
  446.7 144.1 %all-gather.29.cloned.1.call-done = bf16[2048,2816]{1,0:T(8,128)(2,1)} async-done(((bf16[128,2816]{1,0:T(8,128)(2,1)}), bf16[2048,2816]{1,0:T(8,128)(2,1)}) %all-gather.29.cloned.1.call-update) | async-done | bytes 11534352 | tf_op jit(solution)/shard_map/all_gather | solution.py:60
  590.8 12.5 fusion.17
  603.3 130.8 %all-gather.27.cloned.1.call-done = bf16[2048,2816]{1,0:T(8,128)(2,1)} async-done(((bf16[128,2816]{1,0:T(8,128)(2,1)}), bf16[2048,2816]{1,0:T(8,128)(2,1)}) %all-gather.27.cloned.1.call-update) | async-done | bytes 11534352 | tf_op jit(solution)/shard_map/all_gather | solution.py:59
  734.1 12.5 fusion.16
  747.0 143.9 %all-gather.31.cloned.1.call-done = bf16[2048,2816]{1,0:T(8,128)(2,1)} async-done(((bf16[128,2816]{1,0:T(8,128)(2,1)}), bf16[2048,2816]{1,0:T(8,128)(2,1)}) %all-gather.31.cloned.1.call-update) | async-done | bytes 11534352 | tf_op jit(solution)/shard_map/all_gather | solution.py:61
  890.9 15.1 multiply_convert_fusion.2
  906.0 11.4 fusion.18
  917.4 10.1 convolution_add_fusion
  927.8 11.0 convolution_convert_fusion
  942.3 11.1 reduce-scatter.15.cloned.1.call-done
  953.4 5.0 fusion.14
  958.5 11.9 all-gather.35.cloned.1.call-done
  970.3 7.9 multiply_reduce_fusion
  980.6 4.2 multiply_convert_fusion.5
  986.3 4.0 convolution_convert_fusion.1
  1002.4 3.1 multiply_convert_fusion.7
  1016.1 3.9 add_convert_fusion
  1020.1 13.9 convolution_bitcast_fusion
  1034.0 7.8 fusion.28
  1041.9 7.5 fusion.27
  1050.7 7.3 fusion.25
  1058.3 7.4 fusion.24
  1066.9 7.4 fusion.26
  1075.9 12.7 fusion.30
  1088.9 12.8 fusion.29
  1103.6 3.1 fusion.1
  1106.7 402.3 %reduce-scatter.35.cloned.1.call-done = f32[128,2816]{0,1:T(8,128)} async-done(((f32[2048,2816]{0,1:T(8,128)}), f32[128,2816]{0,1:T(8,128)}) %reduce-scatter.35.cloned.1.call-update) | async-done | bytes 1441808 | tf_op jit(solution)/shard_map/reduce_scatter | solution.py:189
  1511.9 182.8 %reduce-scatter.29.cloned.1.call-done = f32[128,1024]{1,0:T(8,128)} async-done(((f32[2048,1024]{1,0:T(8,128)}), f32[128,1024]{1,0:T(8,128)}) %reduce-scatter.29.cloned.1.call-update) | async-done | bytes 524304 | tf_op jit(solution)/shard_map/reduce_scatter | solution.py:231
  1694.7 183.1 %reduce-scatter.27.cloned.1.call-done = f32[128,1024]{1,0:T(8,128)} async-done(((f32[2048,1024]{1,0:T(8,128)}), f32[128,1024]{1,0:T(8,128)}) %reduce-scatter.27.cloned.1.call-update) | async-done | bytes 524304 | tf_op jit(solution)/shard_map/reduce_scatter | solution.py:230
  1877.9 183.0 %reduce-scatter.23.cloned.1.call-done = f32[128,1024]{1,0:T(8,128)} async-done(((f32[2048,1024]{1,0:T(8,128)}), f32[128,1024]{1,0:T(8,128)}) %reduce-scatter.23.cloned.1.call-update) | async-done | bytes 524304 | tf_op jit(solution)/shard_map/reduce_scatter | solution.py:228
  2060.9 183.1 %reduce-scatter.21.cloned.1.call-done = f32[128,1024]{1,0:T(8,128)} async-done(((f32[2048,1024]{1,0:T(8,128)}), f32[128,1024]{1,0:T(8,128)}) %reduce-scatter.21.cloned.1.call-update) | async-done | bytes 524304 | tf_op jit(solution)/shard_map/reduce_scatter | solution.py:227
  2244.0 183.1 %reduce-scatter.25.cloned.1.call-done = f32[128,1024]{1,0:T(8,128)} async-done(((f32[2048,1024]{1,0:T(8,128)}), f32[128,1024]{1,0:T(8,128)}) %reduce-scatter.25.cloned.1.call-update) | async-done | bytes 524304 | tf_op jit(solution)/shard_map/reduce_scatter | solution.py:229
  2427.2 479.9 %reduce-scatter.33.cloned.1.call-done = f32[128,2816]{1,0:T(8,128)} async-done(((f32[2048,2816]{1,0:T(8,128)}), f32[128,2816]{1,0:T(8,128)}) %reduce-scatter.33.cloned.1.call-update) | async-done | bytes 1441808 | tf_op jit(solution)/shard_map/reduce_scatter | solution.py:188
  2907.1 482.6 %reduce-scatter.31.cloned.1.call-done = f32[128,2816]{1,0:T(8,128)} async-done(((f32[2048,2816]{1,0:T(8,128)}), f32[128,2816]{1,0:T(8,128)}) %reduce-scatter.31.cloned.1.call-update) | async-done | bytes 1441808 | tf_op jit(solution)/shard_map/reduce_scatter | solution.py:187
  (157 shorter events, 64.6 us)
Async XLA Ops:
  7.2 17.1 all-gather.13.cloned.1.call-start
  9.3 5.1 copy-start.22
  9.3 5.8 copy-start.29
  11.8 90.4 %all-gather.21.cloned.1.call-start = ((), (), s32[]{:S(2)}) async-start(), calls=%async_computation.16 | async-start | bytes 4456448 | tf_op jit(solution)/shard_map/all_gather | solution.py:50
  12.6 167.1 %all-gather.19.cloned.1.call-start = ((), (), s32[]{:S(2)}) async-start(), calls=%async_computation.15 | async-start | bytes 4456448 | tf_op jit(solution)/shard_map/all_gather | solution.py:49
  13.3 243.7 %all-gather.17.cloned.1.call-start = ((), (), s32[]{:S(2)}) async-start(), calls=%async_computation.14 | async-start | bytes 4456448 | tf_op jit(solution)/shard_map/all_gather | solution.py:51
  13.9 320.5 %all-gather.15.cloned.1.call-start = ((), (), s32[]{:S(2)}) async-start(), calls=%async_computation.13 | async-start | bytes 4456448 | tf_op jit(solution)/shard_map/all_gather | solution.py:52
  14.5 397.2 %all-gather.23.cloned.1.call-start = ((), (), s32[]{:S(2)}) async-start(), calls=%async_computation.17 | async-start | bytes 4456448 | tf_op jit(solution)/shard_map/all_gather | solution.py:53
  15.1 416.1 %reduce-scatter.13.cloned.1.call-start = ((), (), s32[]{:S(2)}) async-start(), calls=%async_computation.18 | async-start | bytes 6291456 | tf_op jit(solution)/shard_map/reduce_scatter | solution.py:150
  15.5 172.6 %copy-start.16 = (f32[512,512]{1,0:T(8,128)}, f32[512,512]{1,0:T(8,128)S(1)}, u32[]{:S(2)}) copy-start(f32[512,512]{1,0:T(8,128)S(1)} %convert_select_fusion) | copy-start | bytes 3145732
  109.4 78.8 %copy-start.9 = (bf16[512,1024]{0,1:T(8,128)(2,1)}, bf16[512,1024]{0,1:T(8,128)(2,1)S(1)}, u32[]{:S(2)}) copy-start(bf16[512,1024]{0,1:T(8,128)(2,1)S(1)} %copy.49) | copy-start | bytes 3145732
  188.2 4.5 copy-start.11
  257.0 5.3 copy-start.2
  262.3 2.9 copy-start.18
  267.1 73.8 %copy-start.5 = (f32[512,1024]{1,0:T(8,128)}, f32[512,1024]{1,0:T(8,128)S(1)}, u32[]{:S(2)}) copy-start(f32[512,1024]{1,0:T(8,128)S(1)} %copy.45) | copy-start | bytes 6291460
  341.0 77.3 %copy-start.30 = (bf16[512,1024]{1,0:T(8,128)(2,1)}, bf16[512,1024]{1,0:T(8,128)(2,1)S(1)}, u32[]{:S(2)}) copy-start(bf16[512,1024]{1,0:T(8,128)(2,1)S(1)} %get-tuple-element.101) | copy-start | bytes 3145732
  418.2 13.0 copy-start
  418.3 28.4 all-gather.25.cloned.1.call-start
  434.7 156.1 %all-gather.29.cloned.1.call-start = ((), (), s32[]{:S(2)}) async-start(), calls=%async_computation.21 | async-start | bytes 12255232 | tf_op jit(solution)/shard_map/all_gather | solution.py:60
  435.4 298.7 %all-gather.27.cloned.1.call-start = ((), (), s32[]{:S(2)}) async-start(), calls=%async_computation.20 | async-start | bytes 12255232 | tf_op jit(solution)/shard_map/all_gather | solution.py:59
  436.0 311.0 %all-gather.33.cloned.1.call-start = ((), (), s32[]{:S(2)}) async-start(), calls=%async_computation.24 | async-start | bytes 3145728 | tf_op jit(solution)/shard_map/all_gather | solution.py:172
  436.8 454.1 %all-gather.31.cloned.1.call-start = ((), (), s32[]{:S(2)}) async-start(), calls=%async_computation.22 | async-start | bytes 12255232 | tf_op jit(solution)/shard_map/all_gather | solution.py:61
  437.3 503.0 %reduce-scatter.17.cloned.1.call-start = ((), (), s32[]{:S(2)}) async-start(), calls=%async_computation.25 | async-start | bytes 6291456 | tf_op jit(solution)/shard_map/reduce_scatter | solution.py:176
  890.9 26.5 slice-start
  890.9 26.5 slice-start.1
  906.0 11.4 copy-start.31
  906.0 11.4 slice-start.2
  927.5 25.9 reduce-scatter.15.cloned.1.call-start
  938.8 31.5 all-gather.35.cloned.1.call-start
  958.4 143.3 %reduce-scatter.19.cloned.1.call-start = ((), (), s32[]{:S(2)}) async-start(), calls=%async_computation.27 | async-start | bytes 3145728 | tf_op jit(solution)/shard_map/reduce_scatter | solution.py:214
  970.3 10.3 copy-start.6
  986.3 4.1 copy-start.17
  986.3 4.0 copy-start.19
  990.4 2.9 copy-start.12
  1002.4 3.1 copy-start.4
  1002.4 3.5 copy-start.13
  1005.9 2.9 copy-start.27
  1006.7 6.9 copy-start.14
  1011.2 2.4 copy-start.25
  1013.6 2.5 copy-start.8
  1020.0 489.0 %reduce-scatter.35.cloned.1.call-start = ((), (), s32[]{:S(2)}) async-start(), calls=%async_computation.35 | async-start | bytes 24510464 | tf_op jit(solution)/shard_map/reduce_scatter | solution.py:189
  1033.9 660.8 %reduce-scatter.29.cloned.1.call-start = ((), (), s32[]{:S(2)}) async-start(), calls=%async_computation.32 | async-start | bytes 8912896 | tf_op jit(solution)/shard_map/reduce_scatter | solution.py:231
  1041.8 836.0 %reduce-scatter.27.cloned.1.call-start = ((), (), s32[]{:S(2)}) async-start(), calls=%async_computation.31 | async-start | bytes 8912896 | tf_op jit(solution)/shard_map/reduce_scatter | solution.py:230
  1049.5 1011.4 %reduce-scatter.23.cloned.1.call-start = ((), (), s32[]{:S(2)}) async-start(), calls=%async_computation.29 | async-start | bytes 8912896 | tf_op jit(solution)/shard_map/reduce_scatter | solution.py:228
  1058.0 1186.0 %reduce-scatter.21.cloned.1.call-start = ((), (), s32[]{:S(2)}) async-start(), calls=%async_computation.28 | async-start | bytes 8912896 | tf_op jit(solution)/shard_map/reduce_scatter | solution.py:227
  1065.7 1361.4 %reduce-scatter.25.cloned.1.call-start = ((), (), s32[]{:S(2)}) async-start(), calls=%async_computation.30 | async-start | bytes 8912896 | tf_op jit(solution)/shard_map/reduce_scatter | solution.py:229
  1074.3 1832.8 %reduce-scatter.33.cloned.1.call-start = ((), (), s32[]{:S(2)}) async-start(), calls=%async_computation.34 | async-start | bytes 24510464 | tf_op jit(solution)/shard_map/reduce_scatter | solution.py:188
  1088.6 2301.1 %reduce-scatter.31.cloned.1.call-start = ((), (), s32[]{:S(2)}) async-start(), calls=%async_computation.33 | async-start | bytes 24510464 | tf_op jit(solution)/shard_map/reduce_scatter | solution.py:187
  (11 other events, 19.2 us)
Sparse Core Ops, SparseCore 0:
  11.9 12.2 all-gather.12
  27.0 75.1 all-gather.20
  105.0 74.6 all-gather.18
  182.3 74.6 all-gather.16
  259.6 74.6 all-gather.14
  337.0 74.6 all-gather.22
  418.4 12.7 reduce-scatter.12
  434.8 11.8 all-gather.24
  449.8 140.8 all-gather.28
  593.7 140.3 all-gather.26
  735.7 11.1 all-gather.32
  750.0 140.8 all-gather.30
  927.7 12.6 reduce-scatter.16
  942.5 10.8 reduce-scatter.14
  958.5 11.7 all-gather.34
  1020.1 10.7 reduce-scatter.18
  1034.1 474.8 reduce-scatter.34
  1511.7 182.9 reduce-scatter.28
  1697.6 180.2 reduce-scatter.26
  1880.6 180.2 reduce-scatter.22
  2063.7 180.2 reduce-scatter.20
  2246.9 180.2 reduce-scatter.24
  2430.0 477.0 reduce-scatter.32
  2909.8 479.7 reduce-scatter.30
where the time goes:
time: 3410 us; the launch traced here: 3400 us
  waiting for transfers between devices  3110 us (91%)
  matrix products  218 us (6%)
    reduce_scatter x1, waiting for transfers between devices, on_device(): lax.psum_scatter(grad_left, 'wide', scatter_dimension=0, tiled=True)  483 us
    reduce_scatter x1, waiting for transfers between devices, on_device(): lax.psum_scatter(grad_right, 'wide', scatter_dimension=0, tiled=True)  480 us
    reduce_scatter x1, waiting for transfers between devices, on_device(): lax.psum_scatter(grad_down, 'wide', scatter_dimension=0, tiled=True)  402 us
    reduce_scatter x1, waiting for transfers between devices, on_device(): lax.psum_scatter(grad_query, 'wide', scatter_dimension=0, tiled=True)  183 us
    reduce_scatter x1, waiting for transfers between devices, on_device(): lax.psum_scatter(grad_gate, 'wide', scatter_dimension=0, tiled=True)  183 us
    reduce_scatter x1, waiting for transfers between devices, on_device(): lax.psum_scatter(grad_value, 'wide', scatter_dimension=0, tiled=True)  183 us
    reduce_scatter x1, waiting for transfers between devices, on_device(): lax.psum_scatter(grad_key, 'wide', scatter_dimension=0, tiled=True)  183 us
    reduce_scatter x1, waiting for transfers between devices, on_device(): lax.psum_scatter(grad_output, 'wide', scatter_dimension=0, tiled=True)  183 us
  transfers between devices with their start and end apart: 24, of which 23 were waited for; matrix products, arithmetic and copies ran while one was open for 5% of the time, Pallas kernels for 0%

commit v1 on v0

v1 whole, which is shorter than its diff:
```python
import jax
import jax.numpy as jnp
from jax import lax
from jax.sharding import PartitionSpec as P

HEAD_DIM = 128
LINE = 4
EPS = 1e-06
DECAY = 2.0
F32 = jnp.float32
BF16 = jnp.bfloat16


def mm(a, b, out=F32):
    return lax.dot_general(a, b, (((1,), (0,)), ((), ())), preferred_element_type=F32).astype(out)


def mm_t(a, b, out=F32):
    return lax.dot_general(a, b, (((1,), (1,)), ((), ())), preferred_element_type=F32).astype(out)


def t_mm(a, b, out=F32):
    return lax.dot_general(a, b, (((0,), (0,)), ((), ())), preferred_element_type=F32).astype(out)


def norm_scale_of(values):
    return lax.rsqrt(jnp.mean(values * values, axis=-1, keepdims=True) + EPS)


def norm_back(values, scale, gradient):
    inner = jnp.mean(gradient * values, axis=-1, keepdims=True)
    return scale * gradient - values * (scale * scale * scale) * inner


def after(value, *deps):
    return lax.optimization_barrier((value,) + deps)[0]


class Net:
    def __init__(self, wide):
        self.wide = wide
        self.me = lax.axis_index("wide")
        bits = wide.bit_length() - 1
        self.plane = [0, 1] + list(range(4, bits))
        self.n_plane = wide // LINE
        self.lines = [
            [base + 4 * k for k in range(LINE)] for base in range(wide) if not base & 12
        ]

    def flip(self, value, bit):
        return lax.ppermute(value, "wide", [(w, w ^ (1 << bit)) for w in range(self.wide)])

    def core(self, value):
        return lax.ppermute(value, "narrow", [(0, 1), (1, 0)])

    def line(self, value):
        return lax.all_to_all(
            value, "wide", 0, 0, axis_index_groups=self.lines, tiled=True
        )

    def permute(self, value):
        size = value.shape[1] // self.wide
        blocks = [value[:, i * size : (i + 1) * size] for i in range(self.wide)]
        blocks = self.swap(blocks)
        order = [self.index(m, z) for m in range(self.n_plane) for z in range(LINE)]
        return jnp.concatenate([blocks[i] for i in order], axis=1)

    def restore(self, value):
        size = value.shape[1] // self.wide
        blocks = [None] * self.wide
        for m in range(self.n_plane):
            for z in range(LINE):
                at = (m * LINE + z) * size
                blocks[self.index(m, z)] = value[:, at : at + size]
        return jnp.concatenate(self.swap(blocks), axis=1)

    def index(self, m, z):
        return z * 4 + sum(((m >> j) & 1) << bit for j, bit in enumerate(self.plane))

    def swap(self, blocks):
        for bit in self.plane:
            mine = ((self.me >> bit) & 1) == 1
            blocks = [
                jnp.where(mine, blocks[i ^ (1 << bit)], blocks[i])
                for i in range(len(blocks))
            ]
        return blocks

    def scatter_line(self, weight):
        rows, cols = weight.shape
        halves = [weight[:, : cols // 2], weight[:, cols // 2 :]]
        return self.line(jnp.stack([halves[z & 1] for z in range(LINE)]))

    def spread(self, block, turn):
        order = list(range(len(self.plane)))
        if turn:
            order = [1, 0] + order[2:]
        held = {0: block}
        for j in order:
            held.update({m | (1 << j): self.flip(b, self.plane[j]) for m, b in held.items()})
        return [held[m] for m in range(self.n_plane)]

    def gather(self, lined, turn, split):
        _, size, cols = lined.shape
        if split:
            cut = [self.spread(lined[:2], turn), self.spread(lined[2:], not turn)]
            parts = [p for pair in zip(*cut) for p in pair]
        else:
            parts = self.spread(lined, turn)
        return jnp.concatenate([p.reshape(-1, cols) for p in parts], axis=0)

    def fold(self, blocks, turn):
        order = list(range(len(self.plane)))
        if turn:
            order = [1, 0] + order[2:]
        held = {m: blocks[m] for m in range(self.n_plane)}
        for j in reversed(order):
            keep = [m for m in held if not (m >> j) & 1]
            sent = jnp.stack([held[m | (1 << j)] for m in keep])
            got = self.flip(sent, self.plane[j])
            held = {
                m: (held[m].astype(F32) + got[i].astype(F32)).astype(BF16)
                for i, m in enumerate(keep)
            }
        return held[0]

    def reduce(self, grad, turn, split):
        rows, cols = grad.shape
        size = rows // self.wide
        blocks = grad.reshape(self.n_plane, LINE, size, cols)
        if split:
            lined = jnp.concatenate(
                [self.fold(blocks[:, :2], turn), self.fold(blocks[:, 2:], not turn)]
            )
        else:
            lined = self.fold(blocks, turn)
        got = self.line(lined).astype(F32)
        return jnp.concatenate([got[0] + got[2], got[1] + got[3]], axis=1)

    def group_gather(self, value):
        near = self.core(value)
        far = self.flip(value, 2)
        return jnp.concatenate([value, near, far, self.core(far)], axis=0)

    def group_sum(self, value):
        quarter = value.shape[0] // 4
        b = value.reshape(4, quarter)
        got = self.core(b)
        b = b + jnp.concatenate([got[1:2], got[0:1], got[3:4], got[2:3]])
        got = self.flip(b, 2)
        return (b + jnp.concatenate([got[2:], got[:2]])).reshape(-1)

    def group_scatter(self, value):
        quarter = value.shape[0] // 4
        b = [value[i * quarter : (i + 1) * quarter] for i in range(4)]
        got = self.core(jnp.concatenate([b[1], b[3]]))
        far = (b[2].astype(F32) + got[quarter:].astype(F32)).astype(BF16)
        own = b[0].astype(F32) + got[:quarter].astype(F32)
        return own + self.flip(far, 2).astype(F32)


def masks(lengths, places, rates):
    starts, total = [], 0
    for c in range(lengths.shape[1] - 1):
        total = total + lengths[:, c]
        starts.append(total)
    starts = jnp.stack(starts, axis=1)
    docs = jnp.sum((places[None, :, None] >= starts[:, None, :]).astype(jnp.int32), axis=2)
    gap = places[:, None] - places[None, :]
    allowed = (gap >= 0)[None] & (docs[:, :, None] == docs[:, None, :])
    spread = jnp.maximum(gap, 0).astype(F32)
    weights = jnp.exp(-rates[:, None, None] * spread[None])
    return jnp.where(allowed[:, None], weights[None], 0.0)


def sigmoid(z):
    return 1.0 / (1.0 + jnp.exp(-z))


def on_device(
    layer_input, doc_lengths, w_query, w_key, w_value, w_gate, w_output, w_left, w_right, w_down, cotangent, *, wide
):
    net = Net(wide)
    core = lax.axis_index("narrow")
    half = (net.me >> 2) & 1
    features = layer_input.shape[1]

    weights = [w_query, w_key, w_value, w_gate, w_output, w_left, w_right, w_down]
    turns = [0, 1, 0, 1, 0, 0, 1, 0]
    splits = [0, 0, 0, 0, 0, 1, 1, 1]
    lined = []
    for i, w in enumerate(weights):
        if i >= 2:
            w = after(w, lined[i - 2])
        lined.append(net.scatter_line(w))
    full = [net.gather(x, t, s) for x, t, s in zip(lined, turns, splits)]
    query_w, key_w, value_w, gate_w, output_w, left_w, right_w, down_w = full

    inputs = net.permute(layer_input).astype(F32)
    norm_one = norm_scale_of(inputs)
    normed = net.group_gather((inputs * norm_one).astype(BF16))
    cot = net.permute(cotangent)
    cot_all = net.group_gather(cot)

    quarter = inputs.shape[0]
    tokens = 4 * quarter
    row_len = 2 * quarter
    width = query_w.shape[1]
    heads = width // HEAD_DIM
    all_heads = features // HEAD_DIM
    head_ids = (core * 2 + half) * heads + jnp.arange(heads, dtype=jnp.int32)
    rates = DECAY * head_ids.astype(F32) / all_heads
    own = jnp.arange(quarter, dtype=jnp.int32)
    places = jnp.concatenate([own + core * quarter, own + (1 - core) * quarter])
    lengths = jnp.concatenate([doc_lengths, net.flip(doc_lengths, 2)])
    decay = masks(lengths, places, rates)

    query_pre = mm(normed, query_w)
    key_pre = mm(normed, key_w)
    values = mm(normed, value_w, BF16)
    gate = mm(normed, gate_w)
    query_sig, key_sig = sigmoid(query_pre), sigmoid(key_pre)
    queries = (query_pre * query_sig).astype(BF16)
    keys = (key_pre * key_sig).astype(BF16)
    shape = (2, row_len, heads, HEAD_DIM)
    q4, k4, v4 = (a.reshape(shape) for a in (queries, keys, values))
    scores = jnp.einsum("rihd,rjhd->rhij", q4, k4, preferred_element_type=F32)
    probs = (scores * decay).astype(BF16)
    mixed = jnp.einsum("rhij,rjhd->rihd", probs, v4, preferred_element_type=F32)
    mixed = mixed.reshape(tokens, width)
    squares = net.group_sum(jnp.sum(mixed * mixed, axis=1))
    attn_scale = lax.rsqrt(squares / features + EPS)[:, None]
    scaled = mixed * attn_scale
    blended = (gate * scaled).astype(BF16)
    middle = inputs + net.group_scatter(mm_t(blended, output_w, BF16))
    norm_two = norm_scale_of(middle)
    mid = net.group_gather((middle * norm_two).astype(BF16))
    left = mm(mid, left_w)
    right = mm(mid, right_w)
    product = (left * right).astype(BF16)
    grad_down = net.reduce(t_mm(cot_all, product, BF16), 0, 1)

    layer_output = middle + net.group_scatter(mm_t(product, down_w, BF16))
    layer_output = net.restore(layer_output.astype(BF16))

    grad_product = mm(cot_all, down_w)
    grad_left_pre = (grad_product * right).astype(BF16)
    grad_right_pre = (grad_product * left).astype(BF16)
    grad_mid = net.group_scatter(
        (mm_t(grad_left_pre, left_w) + mm_t(grad_right_pre, right_w)).astype(BF16)
    )
    grad_left = net.reduce(t_mm(mid, grad_left_pre, BF16), 0, 1)
    grad_right = net.reduce(t_mm(mid, grad_right_pre, BF16), 1, 1)
    grad_middle = cot.astype(F32) + norm_back(middle, norm_two, grad_mid)
    branch = net.group_gather(grad_middle.astype(BF16))
    grad_blended = mm(branch, output_w)
    grad_output = net.reduce(t_mm(branch, blended, BF16), 0, 0)
    grad_gate_pre = (grad_blended * scaled).astype(BF16)
    grad_gate = net.reduce(t_mm(normed, grad_gate_pre, BF16), 1, 0)
    grad_scaled = grad_blended * gate
    inner = net.group_sum(jnp.sum(grad_scaled * mixed, axis=1)) / features
    grad_mixed = (
        attn_scale * grad_scaled - mixed * (attn_scale * attn_scale * attn_scale) * inner[:, None]
    ).astype(BF16)
    g4 = grad_mixed.reshape(shape)
    grad_probs = jnp.einsum("rihd,rjhd->rhij", g4, v4, preferred_element_type=F32)
    grad_values = jnp.einsum("rhij,rihd->rjhd", probs, g4, preferred_element_type=F32)
    grad_value_pre = grad_values.astype(BF16).reshape(tokens, width)
    grad_value = net.reduce(t_mm(normed, grad_value_pre, BF16), 0, 0)
    grad_scores = (grad_probs * decay).astype(BF16)
    grad_queries = jnp.einsum("rhij,rjhd->rihd", grad_scores, k4, preferred_element_type=F32)
    grad_keys = jnp.einsum("rhij,rihd->rjhd", grad_scores, q4, preferred_element_type=F32)
    grad_query_pre = (
        grad_queries.reshape(tokens, width) * (query_sig * (1.0 + query_pre * (1.0 - query_sig)))
    ).astype(BF16)
    grad_key_pre = (
        grad_keys.reshape(tokens, width) * (key_sig * (1.0 + key_pre * (1.0 - key_sig)))
    ).astype(BF16)
    grad_query = net.reduce(t_mm(normed, grad_query_pre, BF16), 1, 0)
    grad_key = net.reduce(t_mm(normed, grad_key_pre, BF16), 0, 0)
    total = mm_t(grad_gate_pre, gate_w) + mm_t(grad_value_pre, value_w)
    total = total + mm_t(grad_query_pre, query_w) + mm_t(grad_key_pre, key_w)
    grad_normed = net.group_scatter(total.astype(BF16))
    input_grad = net.restore(grad_middle + norm_back(inputs, norm_one, grad_normed))
    return (
        layer_output,
        input_grad,
        grad_query,
        grad_key,
        grad_value,
        grad_gate,
        grad_output,
        grad_left,
        grad_right,
        grad_down,
    )


def solution(mesh):
    both, weight = P(("wide", "narrow"), None), P("wide", "narrow")
    wide = mesh.shape["wide"]

    def body(*args):
        return on_device(*args, wide=wide)

    return jax.shard_map(
        body,
        mesh=mesh,
        in_specs=(both, P("wide", None)) + (weight,) * 8 + (both,),
        out_specs=(both, both) + (weight,) * 8,
        check_vma=False,
    )
```

time: 3410 us -> 957 us (0.28)
  waiting for transfers between devices: 3110 us -> 317 us
  starting transfers between devices: 1.64 us -> 211 us
  other arithmetic: 28.4 us -> 138 us
  local copies, waits for them, and re-layouts: 20.6 us -> 69 us
    reduce_scatter x12 -> x0, waiting for transfers between devices: 2310 us -> none  [the longest x1 483 us: on_device(): lax.psum_scatter(grad_left, 'wide', scatter_dimension=0, tiled=True)]
    all_gather x12 -> x0, waiting for transfers between devices: 796 us -> none  [the longest x1 144 us: fetch_feed(): lax.all_gather(w_right, 'wide', axis=0, tiled=True)]
    ppermute x0 -> x80, waiting for transfers between devices: none -> 206 us  [the longest x66 206 us: flip(): lax.ppermute(value, 'wide', [(w, w ^ 1 << bit) for w in range(self.wide)])]
    ppermute x0 -> x80, starting transfers between devices: none -> 122 us  [the longest x14 66.1 us: core(): return lax.ppermute(value, 'narrow', [(0, 1), (1, 0)])]
    all_to_all x0 -> x16, waiting for transfers between devices: none -> 112 us  [line(): lax.all_to_all(value, 'wide', 0, 0, axis_index_groups=self.lines, tiled=T...]
    all_to_all x0 -> x16, starting transfers between devices: none -> 88.8 us  [line(): lax.all_to_all(value, 'wide', 0, 0, axis_index_groups=self.lines, tiled=T...]
    convert_element_type x6 -> x38, other arithmetic: 16.7 us -> 72.4 us  [the longest x19 37 us: fold(): (held[m].astype(F32) + got[i].astype(F32)).astype(BF16)]
  transfers between devices with their start and end apart: 24 -> 96, of which waited for: 23 -> 35; matrix products, arithmetic and copies ran while one was open for 5% -> 37% of each run, Pallas kernels for 0% -> 0%
where the time goes in v1:
time: 957 us; the launch traced here: 945 us
  waiting for transfers between devices  317 us (33%)
  starting transfers between devices  211 us (22%)
  matrix products  207 us (22%)
  other arithmetic  138 us (14%)
  local copies, waits for them, and re-layouts  69 us (7%)
    ppermute x66, waiting for transfers between devices, flip(): lax.ppermute(value, 'wide', [(w, w ^ 1 << bit) for w in range(self.wide)])  206 us
    all_to_all x16, waiting for transfers between devices, line(): lax.all_to_all(value, 'wide', 0, 0, axis_index_groups=self.lines, tiled=T...  112 us
    all_to_all x16, starting transfers between devices, line(): lax.all_to_all(value, 'wide', 0, 0, axis_index_groups=self.lines, tiled=T...  88.8 us
    dot_general x8, matrix products, mm(): lax.dot_general(a, b, (((1,), (0,)), ((), ())), preferred_element_type=F32)  73.4 us
    ppermute x14, starting transfers between devices, core(): return lax.ppermute(value, 'narrow', [(0, 1), (1, 0)])  66.1 us
    dot_general x8, matrix products, mm_t(): lax.dot_general(a, b, (((1,), (1,)), ((), ())), preferred_element_type=F32)  65 us
    ppermute x66, starting transfers between devices, flip(): lax.ppermute(value, 'wide', [(w, w ^ 1 << bit) for w in range(self.wide)])  56.2 us
    dot_general x8, matrix products, t_mm(): lax.dot_general(a, b, (((0,), (0,)), ((), ())), preferred_element_type=F32)  49.1 us
  transfers between devices with their start and end apart: 96, of which 35 were waited for; matrix products, arithmetic and copies ran while one was open for 37% of the time, Pallas kernels for 0%

profile of v1, /device:TPU:25, one launch (start us, length us, event | category | flops | bytes accessed | tf_op | source)
XLA Modules:
  0.0 945.1 jit_solution(14762847086686754798)
XLA Ops:
  23.1 22.0 %all-to-all-done.2 = bf16[4,128,512]{2,1,0:T(8,128)(2,1)} async-done(((bf16[4,128,512]{2,1,0:T(8,128)(2,1)}), bf16[4,128,512]{2,1,0:T(8,128)(2,1)}, u32[]{:S(2)}, u32[]{:S(2)}) %all-to-all-start.2) | async-done | bytes 524320 | tf_op jit(solution)/shard_map/all_to_all | solution.py:57
  53.1 8.9 all-to-all-done
  62.0 5.8 all-to-all-start.3
  71.7 7.5 all-to-all-done.3
  79.2 6.9 all-to-all-start.1
  97.3 7.1 all-to-all-start.4
  113.2 8.7 collective-permute-done.14
  123.3 6.4 multiply_convert_fusion.6
  134.5 6.9 multiply_convert_fusion.7
  152.7 5.9 fusion
  168.8 5.4 multiply_reduce_fusion.3
  174.3 5.8 collective-permute-start.16
  187.3 8.9 collective-permute-done.18
  197.4 6.5 multiply_convert_fusion.5
  229.3 11.2 %collective-permute-done.26 = bf16[2,128,1408]{2,1,0:T(8,128)(2,1)} collective-permute-done((bf16[2,128,1408]{2,1,0:T(8,128)(2,1)S(1)}, bf16[2,128,1408]{2,1,0:T(8,128)(2,1)}, u32[]{:S(2)}, u32[]{:S(2)}) %collective-permute-start.26) | collective-permute-done | bytes 720928 | tf_op jit(solution)/shard_map/ppermute | solution.py:51
  242.6 13.4 %collective-permute-done.27 = bf16[2,128,1408]{2,1,0:T(8,128)(2,1)S(1)} collective-permute-done((bf16[2,128,1408]{2,1,0:T(8,128)(2,1)S(1)}, bf16[2,128,1408]{2,1,0:T(8,128)(2,1)S(1)}, u32[]{:S(2)}, u32[]{:S(2)}) %collective-permute-start.27) | collective-permute-done | bytes 720928 | tf_op jit(solution)/shard_map/ppermute | solution.py:51
  279.1 12.0 %collective-permute-done.32 = bf16[2,128,1408]{2,1,0:T(8,128)(2,1)S(1)} collective-permute-done((bf16[2,128,1408]{2,1,0:T(8,128)(2,1)S(1)}, bf16[2,128,1408]{2,1,0:T(8,128)(2,1)S(1)}, u32[]{:S(2)}, u32[]{:S(2)}) %collective-permute-start.32) | collective-permute-done | bytes 720928 | tf_op jit(solution)/shard_map/ppermute | solution.py:51
  294.3 12.2 %collective-permute-done.33 = bf16[2,128,1408]{2,1,0:T(8,128)(2,1)} collective-permute-done((bf16[2,128,1408]{2,1,0:T(8,128)(2,1)S(1)}, bf16[2,128,1408]{2,1,0:T(8,128)(2,1)}, u32[]{:S(2)}, u32[]{:S(2)}) %collective-permute-start.33) | collective-permute-done | bytes 720928 | tf_op jit(solution)/shard_map/ppermute | solution.py:51
  313.5 7.7 collective-permute-done.22
  330.4 9.0 collective-permute-done.38
  342.8 12.1 %collective-permute-done.39 = bf16[2,128,1408]{2,1,0:T(8,128)(2,1)S(1)} collective-permute-done((bf16[2,128,1408]{2,1,0:T(8,128)(2,1)S(1)}, bf16[2,128,1408]{2,1,0:T(8,128)(2,1)S(1)}, u32[]{:S(2)}, u32[]{:S(2)}) %collective-permute-start.39) | collective-permute-done | bytes 720928 | tf_op jit(solution)/shard_map/ppermute | solution.py:51
  360.5 8.8 collective-permute-done.47
  379.9 14.6 %fusion.83 = f32[1024,1408]{1,0:T(8,128)} fusion(bf16[2048,1408]{1,0:T(8,128)(2,1)} %constant_dynamic-update-slice_fusion.16, bf16[256,2048]{1,0:T(8,128)(2,1)S(1)} %collective-permute-done.25, bf16[256,2048]{1,0:T(8,128)(2,1)S(1)} %collective-permute-done.24, bf16[256,2048]{1,0:T(8,128)(2,1)S(1)} %collective-permute-done.23, ...), kind=kOutput, calls=%fused_computation.420 | convolution fusion | flops 5922357248 | bytes 15728640 | tf_op jit(solution)/shard_map/dot_general | solution.py:15
  394.6 14.1 %fusion.82 = f32[1024,1408]{1,0:T(8,128)} fusion(bf16[2048,1408]{1,0:T(8,128)(2,1)} %constant_dynamic-update-slice_fusion.24, bf16[256,2048]{1,0:T(8,128)(2,1)S(1)} %collective-permute-done.25, bf16[256,2048]{1,0:T(8,128)(2,1)S(1)} %collective-permute-done.24, bf16[256,2048]{1,0:T(8,128)(2,1)S(1)} %collective-permute-done.23, ...), kind=kOutput, calls=%fused_computation.419 | convolution fusion | flops 5922357248 | bytes 15728640 | tf_op jit(solution)/shard_map/dot_general | solution.py:15
  409.6 13.6 %multiply_convert_fusion.1 = (bf16[1024,1408]{1,0:T(8,128)(2,1)}, bf16[1024,1408]{1,0:T(8,128)(2,1)}, bf16[1024,1408]{1,0:T(8,128)(2,1)}) fusion(f32[1024,1408]{1,0:T(8,128)} %fusion.82, f32[1024,1408]{1,0:T(8,128)} %fusion.83, bf16[2048,1408]{1,0:T(8,128)(2,1)S(1)} %copy-done.68, bf16[256,2048]{1,0:T(8,128)(2,1)} %collective-permute-done.48, ...), kind=kOutput, calls=%fused_computation.10 | convolution fusion | flops 5931008000 | bytes 30146560 | tf_op jit(solution)/shard_map/dot_general | solution.py:15
  423.2 9.2 convolution_convert_fusion
  434.8 6.9 convolution_convert_fusion.3
  445.5 10.9 %fusion.104 = f32[1024,2048]{1,0:T(8,128)} fusion(bf16[1024,1408]{1,0:T(8,128)(2,1)S(1)} %copy-done.99, bf16[2048,1408]{1,0:T(8,128)(2,1)} %constant_dynamic-update-slice_fusion.24), kind=kOutput, calls=%fused_computation.441 | convolution fusion | flops 5905580032 | bytes 17039360 | tf_op jit(solution)/shard_map/dot_general | solution.py:19
  456.5 7.3 convolution_convert_fusion.1
  465.8 9.8 %convolution_convert_fusion.2 = bf16[2048,1408]{1,0:T(8,128)(2,1)S(1)} fusion(bf16[1024,1408]{1,0:T(8,128)(2,1)} %get-tuple-element.42, bf16[256,2048]{1,0:T(8,128)(2,1)} %copy-done.82, bf16[256,2048]{1,0:T(8,128)(2,1)S(1)} %copy-done.79, bf16[256,2048]{1,0:T(8,128)(2,1)S(1)} %copy-done.81, bf16[256,2048]{1,0:T(8,128)(2,1)S(1)} %copy-done.54), kind=kOutput, calls=%fused_computation.8 | convolution fusion | flops 5925240832 | bytes 12845056 | tf_op jit(solution)/shard_map/dot_general | solution.py:23
  480.4 11.2 %add_convert_fusion.1 = bf16[1024,2048]{1,0:T(8,128)(2,1)S(1)} fusion(f32[1024,2048]{1,0:T(8,128)} %fusion.104, bf16[1024,1408]{1,0:T(8,128)(2,1)} %get-tuple-element.42, bf16[2048,1408]{1,0:T(8,128)(2,1)} %constant_dynamic-update-slice_fusion.16), kind=kOutput, calls=%fused_computation.5 | convolution fusion | flops 5909774336 | bytes 21233664 | tf_op jit(solution)/shard_map/dot_general | solution.py:19
  494.4 11.6 %collective-permute-done.72 = bf16[2,2,128,1408]{3,2,1,0:T(8,128)(2,1)} collective-permute-done((bf16[2,2,128,1408]{3,2,1,0:T(8,128)(2,1)}, bf16[2,2,128,1408]{3,2,1,0:T(8,128)(2,1)}, u32[]{:S(2)}, u32[]{:S(2)}) %collective-permute-start.72) | collective-permute-done | bytes 1441824 | tf_op jit(solution)/shard_map/ppermute | solution.py:51
  518.0 36.0 %collective-permute-done.77 = bf16[1,2,128,1408]{3,2,1,0:T(8,128)(2,1)S(1)} collective-permute-done((bf16[1,2,128,1408]{3,2,1,0:T(8,128)(2,1)S(1)}, bf16[1,2,128,1408]{3,2,1,0:T(8,128)(2,1)S(1)}, u32[]{:S(2)}, u32[]{:S(2)}) %collective-permute-start.77) | collective-permute-done | bytes 720928 | tf_op jit(solution)/shard_map/ppermute | solution.py:51
  563.0 6.5 collective-permute-done.69
  591.1 5.3 collective-permute-done.50
  602.8 30.7 %collective-permute-start.51 = (bf16[256,2048]{1,0:T(8,128)(2,1)}, bf16[256,2048]{1,0:T(8,128)(2,1)}, u32[]{:S(2)}, u32[]{:S(2)}) collective-permute-start(bf16[256,2048]{1,0:T(8,128)(2,1)} %get-tuple-element.24), channel_id=1, source_target_pairs={{0,1},{1,0},{2,3},{3,2},{4,5},{5,4},{6,7},{7,6},{8,9},{9,8},{10,11... | collective-permute-start | bytes 3145736 | tf_op jit(solution)/shard_map/ppermute | solution.py:54
  639.2 23.5 %all-to-all-done.14 = bf16[4,128,1408]{2,1,0:T(8,128)(2,1)S(1)} async-done(((bf16[4,128,1408]{2,1,0:T(8,128)(2,1)}), bf16[4,128,1408]{2,1,0:T(8,128)(2,1)S(1)}, u32[]{:S(2)}, u32[]{:S(2)}) %all-to-all-start.14) | async-done | bytes 1441824 | tf_op jit(solution)/shard_map/all_to_all | solution.py:57
  662.6 9.9 %all-to-all-start.13 = ((bf16[4,128,1408]{2,1,0:T(8,128)(2,1)}), bf16[4,128,1408]{2,1,0:T(8,128)(2,1)}, u32[]{:S(2)}, u32[]{:S(2)}) async-start(bf16[4,128,1408]{2,1,0:T(8,128)(2,1)} %pad_maximum_fusion.17), calls=%async_computation.13 | async-start | bytes 2883584 | tf_op jit(solution)/shard_map/all_to_all | solution.py:57
  673.0 7.8 collective-permute-start.53
  685.3 16.2 %all-to-all-done.13 = bf16[4,128,1408]{2,1,0:T(8,128)(2,1)} async-done(((bf16[4,128,1408]{2,1,0:T(8,128)(2,1)}), bf16[4,128,1408]{2,1,0:T(8,128)(2,1)}, u32[]{:S(2)}, u32[]{:S(2)}) %all-to-all-start.13) | async-done | bytes 1441824 | tf_op jit(solution)/shard_map/all_to_all | solution.py:57
  707.2 6.2 multiply_reduce_fusion
  739.3 7.2 fusion.52
  755.1 7.5 fusion.13
  788.6 6.8 fusion.50
  803.7 10.8 %add_convert_fusion = bf16[1024,2048]{1,0:T(8,128)(2,1)S(1)} fusion(f32[1024,2048]{1,0:T(8,128)} %fusion.50, f32[1024,2048]{1,0:T(8,128)} %fusion.52, f32[1024,2048]{1,0:T(8,128)} %fusion.13, bf16[1024,512]{1,0:T(8,128)(2,1)S(1)} %fusion.8, bf16[512,512]{1,0:T(8,128)(2,1)S(1)} %bitcast.336, bf16[512,512]{1,0:T(8,128)(2,1)S(1)} %bitcast.332, ...), kind=kOutput, calls=%fused_computation.4 | convolution fusion | flops 2164260864 | bytes 32505856 | tf_op jit(solution)/shard_map/dot_general | solution.py:19
  819.3 17.0 %collective-permute-done.67 = bf16[1,4,128,512]{3,2,1,0:T(8,128)(2,1)S(1)} collective-permute-done((bf16[1,4,128,512]{3,2,1,0:T(8,128)(2,1)S(1)}, bf16[1,4,128,512]{3,2,1,0:T(8,128)(2,1)S(1)}, u32[]{:S(2)}, u32[]{:S(2)}) %collective-permute-start.67) | collective-permute-done | bytes 524320 | tf_op jit(solution)/shard_map/ppermute | solution.py:51
  838.4 6.2 all-to-all-start.12
  915.4 17.3 %all-to-all-done.8 = bf16[4,128,512]{2,1,0:T(8,128)(2,1)} async-done(((bf16[4,128,512]{2,1,0:T(8,128)(2,1)}), bf16[4,128,512]{2,1,0:T(8,128)(2,1)}, u32[]{:S(2)}, u32[]{:S(2)}) %all-to-all-start.8) | async-done | bytes 524320 | tf_op jit(solution)/shard_map/all_to_all | solution.py:57
  (616 shorter events, 419.2 us)
Async XLA Ops:
  12.3 76.6 %collective-permute-start.1 = (bf16[256,2048]{1,0:T(8,128)(2,1)}, bf16[256,2048]{1,0:T(8,128)(2,1)}, u32[]{:S(2)}, u32[]{:S(2)}) collective-permute-start(bf16[256,2048]{1,0:T(8,128)(2,1)} %fusion.3), channel_id=1, source_target_pairs={{0,8},{2,10},{4,12},{6,14},{8,0},{10,2},{12,4},{14,6},{16,24},{18,... | collective-permute-start | bytes 3145736 | tf_op jit(solution)/shard_map/ppermute | solution.py:51
  12.5 93.3 %collective-permute-start = (bf16[256,2048]{1,0:T(8,128)(2,1)}, bf16[256,2048]{1,0:T(8,128)(2,1)}, u32[]{:S(2)}, u32[]{:S(2)}) collective-permute-start(bf16[256,2048]{1,0:T(8,128)(2,1)} %fusion.3), channel_id=1, source_target_pairs={{0,1},{1,0},{2,3},{3,2},{4,5},{5,4},{6,7},{7,6},{8,9},{9,8},{10,11... | collective-permute-start | bytes 3145736 | tf_op jit(solution)/shard_map/ppermute | solution.py:54
  19.5 49.0 %collective-permute-start.15 = (s32[1,4]{1,0:T(1,128)S(1)}, s32[1,4]{1,0:T(1,128)S(1)}, u32[]{:S(2)}, u32[]{:S(2)}) collective-permute-start(s32[1,4]{1,0:T(1,128)S(1)} %copy-done.77), channel_id=1, source_target_pairs={{0,8},{2,10},{4,12},{6,14},{8,0},{10,2},{12,4},{14,6},{16,24},{18,... | collective-permute-start | bytes 56 | tf_op jit(solution)/shard_map/ppermute | solution.py:51
  89.0 34.1 %collective-permute-start.2 = (bf16[256,2048]{1,0:T(8,128)(2,1)}, bf16[256,2048]{1,0:T(8,128)(2,1)}, u32[]{:S(2)}, u32[]{:S(2)}) collective-permute-start(bf16[256,2048]{1,0:T(8,128)(2,1)} %collective-permute-done.1), channel_id=1, source_target_pairs={{0,1},{1,0},{2,3},{3,2},{4,5},{5,4},{6,7},{7,6},{8,9},{9,8},{10,11... | collective-permute-start | bytes 3145736 | tf_op jit(solution)/shard_map/ppermute | solution.py:54
  97.3 61.2 %all-to-all-start.4 = ((bf16[4,128,512]{2,1,0:T(8,128)(2,1)}), bf16[4,128,512]{2,1,0:T(8,128)(2,1)}, u32[]{:S(2)}, u32[]{:S(2)}) async-start(bf16[4,128,512]{2,1,0:T(8,128)(2,1)} %pad_maximum_fusion.38), calls=%async_computation.4 | async-start | bytes 1048576 | tf_op jit(solution)/shard_map/all_to_all | solution.py:57
  121.9 41.5 %collective-permute-start.7 = (bf16[4,128,512]{2,1,0:T(8,128)(2,1)}, bf16[4,128,512]{2,1,0:T(8,128)(2,1)}, u32[]{:S(2)}, u32[]{:S(2)}) collective-permute-start(bf16[4,128,512]{2,1,0:T(8,128)(2,1)} %all-to-all-done.3), channel_id=1, source_target_pairs={{0,4},{2,6},{4,0},{6,2},{8,12},{10,14},{12,8},{14,10},{16,20},{18,... | collective-permute-start | bytes 1572872 | tf_op jit(solution)/shard_map/ppermute | solution.py:51
  129.8 67.6 %collective-permute-start.3 = (bf16[4,128,512]{2,1,0:T(8,128)(2,1)}, bf16[4,128,512]{2,1,0:T(8,128)(2,1)}, u32[]{:S(2)}, u32[]{:S(2)}) collective-permute-start(bf16[4,128,512]{2,1,0:T(8,128)(2,1)} %all-to-all-done.1), channel_id=1, source_target_pairs={{0,2},{2,0},{4,6},{6,4},{8,10},{10,8},{12,14},{14,12},{16,18},{18,... | collective-permute-start | bytes 1572872 | tf_op jit(solution)/shard_map/ppermute | solution.py:51
  151.5 45.9 %collective-permute-start.5 = (bf16[4,128,512]{2,1,0:T(8,128)(2,1)}, bf16[4,128,512]{2,1,0:T(8,128)(2,1)}, u32[]{:S(2)}, u32[]{:S(2)}) collective-permute-start(bf16[4,128,512]{2,1,0:T(8,128)(2,1)} %collective-permute-done.4), channel_id=1, source_target_pairs={{0,2},{2,0},{4,6},{6,4},{8,10},{10,8},{12,14},{14,12},{16,18},{18,... | collective-permute-start | bytes 1572872 | tf_op jit(solution)/shard_map/ppermute | solution.py:51
  158.6 58.2 %all-to-all-start.5 = ((bf16[4,128,1408]{2,1,0:T(8,128)(2,1)}), bf16[4,128,1408]{2,1,0:T(8,128)(2,1)}, u32[]{:S(2)}, u32[]{:S(2)}) async-start(bf16[4,128,1408]{2,1,0:T(8,128)(2,1)} %pad_maximum_fusion.13), calls=%async_computation.5 | async-start | bytes 2883584 | tf_op jit(solution)/shard_map/all_to_all | solution.py:57
  214.6 77.4 %collective-permute-start.21 = (bf16[512,2048]{1,0:T(8,128)(2,1)}, bf16[512,2048]{1,0:T(8,128)(2,1)}, u32[]{:S(2)}, u32[]{:S(2)}) collective-permute-start(bf16[512,2048]{1,0:T(8,128)(2,1)} %pad_maximum_fusion.9), channel_id=1, source_target_pairs={{0,1},{1,0},{2,3},{3,2},{4,5},{5,4},{6,7},{7,6},{8,9},{9,8},{10,11... | collective-permute-start | bytes 6291464 | tf_op jit(solution)/shard_map/ppermute | solution.py:54
  216.8 44.6 %all-to-all-start.6 = ((bf16[4,128,1408]{2,1,0:T(8,128)(2,1)}), bf16[4,128,1408]{2,1,0:T(8,128)(2,1)S(1)}, u32[]{:S(2)}, u32[]{:S(2)}) async-start(bf16[4,128,1408]{2,1,0:T(8,128)(2,1)} %pad_maximum_fusion.14), calls=%async_computation.6 | async-start | bytes 2883584 | tf_op jit(solution)/shard_map/all_to_all | solution.py:57
  223.4 33.5 %collective-permute-start.28 = (bf16[2,128,1408]{2,1,0:T(8,128)(2,1)S(1)}, bf16[2,128,1408]{2,1,0:T(8,128)(2,1)S(1)}, u32[]{:S(2)}, u32[]{:S(2)}) collective-permute-start(bf16[2,128,1408]{2,1,0:T(8,128)(2,1)S(1)} %get-tuple-element.87), channel_id=1, source_target_pairs={{0,4},{2,6},{4,0},{6,2},{8,12},{10,14},{12,8},{14,10},{16,20},{18,... | collective-permute-start | bytes 2162696 | tf_op jit(solution)/shard_map/ppermute | solution.py:51
  224.6 31.3 %collective-permute-start.27 = (bf16[2,128,1408]{2,1,0:T(8,128)(2,1)S(1)}, bf16[2,128,1408]{2,1,0:T(8,128)(2,1)S(1)}, u32[]{:S(2)}, u32[]{:S(2)}) collective-permute-start(bf16[2,128,1408]{2,1,0:T(8,128)(2,1)S(1)} %get-tuple-element.86), channel_id=1, source_target_pairs={{0,2},{2,0},{4,6},{6,4},{8,10},{10,8},{12,14},{14,12},{16,18},{18,... | collective-permute-start | bytes 2162696 | tf_op jit(solution)/shard_map/ppermute | solution.py:51
  225.9 33.3 %collective-permute-start.29 = (bf16[2,128,1408]{2,1,0:T(8,128)(2,1)S(1)}, bf16[2,128,1408]{2,1,0:T(8,128)(2,1)}, u32[]{:S(2)}, u32[]{:S(2)}) collective-permute-start(bf16[2,128,1408]{2,1,0:T(8,128)(2,1)S(1)} %get-tuple-element.86), channel_id=1, source_target_pairs={{0,4},{2,6},{4,0},{6,2},{8,12},{10,14},{12,8},{14,10},{16,20},{18,... | collective-permute-start | bytes 2162696 | tf_op jit(solution)/shard_map/ppermute | solution.py:51
  262.5 49.5 %all-to-all-start.7 = ((bf16[4,128,1408]{2,1,0:T(8,128)(2,1)}), bf16[4,128,1408]{2,1,0:T(8,128)(2,1)S(1)}, u32[]{:S(2)}, u32[]{:S(2)}) async-start(bf16[4,128,1408]{2,1,0:T(8,128)(2,1)} %pad_maximum_fusion.15), calls=%async_computation.7 | async-start | bytes 2883584 | tf_op jit(solution)/shard_map/all_to_all | solution.py:57
  270.2 36.3 %collective-permute-start.33 = (bf16[2,128,1408]{2,1,0:T(8,128)(2,1)S(1)}, bf16[2,128,1408]{2,1,0:T(8,128)(2,1)}, u32[]{:S(2)}, u32[]{:S(2)}) collective-permute-start(bf16[2,128,1408]{2,1,0:T(8,128)(2,1)S(1)} %get-tuple-element.84), channel_id=1, source_target_pairs={{0,2},{2,0},{4,6},{6,4},{8,10},{10,8},{12,14},{14,12},{16,18},{18,... | collective-permute-start | bytes 2162696 | tf_op jit(solution)/shard_map/ppermute | solution.py:51
  274.7 34.1 %collective-permute-start.34 = (bf16[2,128,1408]{2,1,0:T(8,128)(2,1)S(1)}, bf16[2,128,1408]{2,1,0:T(8,128)(2,1)}, u32[]{:S(2)}, u32[]{:S(2)}) collective-permute-start(bf16[2,128,1408]{2,1,0:T(8,128)(2,1)S(1)} %get-tuple-element.85), channel_id=1, source_target_pairs={{0,4},{2,6},{4,0},{6,2},{8,12},{10,14},{12,8},{14,10},{16,20},{18,... | collective-permute-start | bytes 2162696 | tf_op jit(solution)/shard_map/ppermute | solution.py:51
  277.9 33.1 %collective-permute-start.35 = (bf16[2,128,1408]{2,1,0:T(8,128)(2,1)S(1)}, bf16[2,128,1408]{2,1,0:T(8,128)(2,1)S(1)}, u32[]{:S(2)}, u32[]{:S(2)}) collective-permute-start(bf16[2,128,1408]{2,1,0:T(8,128)(2,1)S(1)} %get-tuple-element.84), channel_id=1, source_target_pairs={{0,4},{2,6},{4,0},{6,2},{8,12},{10,14},{12,8},{14,10},{16,20},{18,... | collective-permute-start | bytes 2162696 | tf_op jit(solution)/shard_map/ppermute | solution.py:51
  324.0 35.7 %collective-permute-start.24 = (bf16[256,2048]{1,0:T(8,128)(2,1)S(1)}, bf16[256,2048]{1,0:T(8,128)(2,1)S(1)}, u32[]{:S(2)}, u32[]{:S(2)}) collective-permute-start(bf16[256,2048]{1,0:T(8,128)(2,1)S(1)} %multiply_convert_fusion.4), channel_id=1, source_target_pairs={{0,8},{2,10},{4,12},{6,14},{8,0},{10,2},{12,4},{14,6},{16,24},{18,... | collective-permute-start | bytes 3145736 | tf_op jit(solution)/shard_map/ppermute | solution.py:51
  326.5 31.9 %collective-permute-start.40 = (bf16[2,128,1408]{2,1,0:T(8,128)(2,1)S(1)}, bf16[2,128,1408]{2,1,0:T(8,128)(2,1)S(1)}, u32[]{:S(2)}, u32[]{:S(2)}) collective-permute-start(bf16[2,128,1408]{2,1,0:T(8,128)(2,1)S(1)} %get-tuple-element.83), channel_id=1, source_target_pairs={{0,4},{2,6},{4,0},{6,2},{8,12},{10,14},{12,8},{14,10},{16,20},{18,... | collective-permute-start | bytes 2162696 | tf_op jit(solution)/shard_map/ppermute | solution.py:51
  328.9 40.4 %collective-permute-start.47 = (bf16[256,2048]{1,0:T(8,128)(2,1)S(1)}, bf16[256,2048]{1,0:T(8,128)(2,1)S(1)}, u32[]{:S(2)}, u32[]{:S(2)}) collective-permute-start(bf16[256,2048]{1,0:T(8,128)(2,1)S(1)} %copy-done.50), channel_id=1, source_target_pairs={{0,8},{2,10},{4,12},{6,14},{8,0},{10,2},{12,4},{14,6},{16,24},{18,... | collective-permute-start | bytes 3145736 | tf_op jit(solution)/shard_map/ppermute | solution.py:51
  369.3 39.3 %collective-permute-start.46 = (bf16[256,2048]{1,0:T(8,128)(2,1)S(1)}, bf16[256,2048]{1,0:T(8,128)(2,1)S(1)}, u32[]{:S(2)}, u32[]{:S(2)}) collective-permute-start(bf16[256,2048]{1,0:T(8,128)(2,1)S(1)} %copy-done.50), channel_id=1, source_target_pairs={{0,1},{1,0},{2,3},{3,2},{4,5},{5,4},{6,7},{7,6},{8,9},{9,8},{10,11... | collective-permute-start | bytes 3145736 | tf_op jit(solution)/shard_map/ppermute | solution.py:54
  376.2 33.4 %collective-permute-start.48 = (bf16[256,2048]{1,0:T(8,128)(2,1)S(1)}, bf16[256,2048]{1,0:T(8,128)(2,1)}, u32[]{:S(2)}, u32[]{:S(2)}) collective-permute-start(bf16[256,2048]{1,0:T(8,128)(2,1)S(1)} %collective-permute-done.47), channel_id=1, source_target_pairs={{0,1},{1,0},{2,3},{3,2},{4,5},{5,4},{6,7},{7,6},{8,9},{9,8},{10,11... | collective-permute-start | bytes 3145736 | tf_op jit(solution)/shard_map/ppermute | solution.py:54
  443.1 74.9 %collective-permute-start.78 = (bf16[2,2,128,1408]{3,2,1,0:T(8,128)(2,1)}, bf16[2,2,128,1408]{3,2,1,0:T(8,128)(2,1)}, u32[]{:S(2)}, u32[]{:S(2)}) collective-permute-start(bf16[2,2,128,1408]{3,2,1,0:T(8,128)(2,1)} %pad_maximum_fusion.22), channel_id=1, source_target_pairs={{0,2},{2,0},{4,6},{6,4},{8,10},{10,8},{12,14},{14,12},{16,18},{18,... | collective-permute-start | bytes 4325384 | tf_op jit(solution)/shard_map/ppermute | solution.py:51
  443.4 49.0 %collective-permute-start.76 = (bf16[2,2,128,1408]{3,2,1,0:T(8,128)(2,1)}, bf16[2,2,128,1408]{3,2,1,0:T(8,128)(2,1)}, u32[]{:S(2)}, u32[]{:S(2)}) collective-permute-start(bf16[2,2,128,1408]{3,2,1,0:T(8,128)(2,1)} %stack.175), channel_id=1, source_target_pairs={{0,4},{2,6},{4,0},{6,2},{8,12},{10,14},{12,8},{14,10},{16,20},{18,... | collective-permute-start | bytes 4325384 | tf_op jit(solution)/shard_map/ppermute | solution.py:51
  465.2 40.9 %collective-permute-start.72 = (bf16[2,2,128,1408]{3,2,1,0:T(8,128)(2,1)}, bf16[2,2,128,1408]{3,2,1,0:T(8,128)(2,1)}, u32[]{:S(2)}, u32[]{:S(2)}) collective-permute-start(bf16[2,2,128,1408]{3,2,1,0:T(8,128)(2,1)} %pad_maximum_fusion.19), channel_id=1, source_target_pairs={{0,2},{2,0},{4,6},{6,4},{8,10},{10,8},{12,14},{14,12},{16,18},{18,... | collective-permute-start | bytes 4325384 | tf_op jit(solution)/shard_map/ppermute | solution.py:51
  476.9 32.2 %collective-permute-start.68 = (bf16[2,2,128,1408]{3,2,1,0:T(8,128)(2,1)}, bf16[2,2,128,1408]{3,2,1,0:T(8,128)(2,1)}, u32[]{:S(2)}, u32[]{:S(2)}) collective-permute-start(bf16[2,2,128,1408]{3,2,1,0:T(8,128)(2,1)} %stack.173), channel_id=1, source_target_pairs={{0,4},{2,6},{4,0},{6,2},{8,12},{10,14},{12,8},{14,10},{16,20},{18,... | collective-permute-start | bytes 4325384 | tf_op jit(solution)/shard_map/ppermute | solution.py:51
  479.6 31.1 %collective-permute-start.44 = (bf16[512,2048]{1,0:T(8,128)(2,1)}, bf16[512,2048]{1,0:T(8,128)(2,1)}, u32[]{:S(2)}, u32[]{:S(2)}) collective-permute-start(bf16[512,2048]{1,0:T(8,128)(2,1)} %pad_maximum_fusion.10), channel_id=1, source_target_pairs={{0,1},{1,0},{2,3},{3,2},{4,5},{5,4},{6,7},{7,6},{8,9},{9,8},{10,11... | collective-permute-start | bytes 6291464 | tf_op jit(solution)/shard_map/ppermute | solution.py:54
  506.1 50.1 %collective-permute-start.74 = (bf16[2,2,128,1408]{3,2,1,0:T(8,128)(2,1)S(1)}, bf16[2,2,128,1408]{3,2,1,0:T(8,128)(2,1)S(1)}, u32[]{:S(2)}, u32[]{:S(2)}) collective-permute-start(bf16[2,2,128,1408]{3,2,1,0:T(8,128)(2,1)S(1)} %stack.174), channel_id=1, source_target_pairs={{0,4},{2,6},{4,0},{6,2},{8,12},{10,14},{12,8},{14,10},{16,20},{18,... | collective-permute-start | bytes 4325384 | tf_op jit(solution)/shard_map/ppermute | solution.py:51
  509.1 53.9 %collective-permute-start.70 = (bf16[2,2,128,1408]{3,2,1,0:T(8,128)(2,1)S(1)}, bf16[2,2,128,1408]{3,2,1,0:T(8,128)(2,1)S(1)}, u32[]{:S(2)}, u32[]{:S(2)}) collective-permute-start(bf16[2,2,128,1408]{3,2,1,0:T(8,128)(2,1)S(1)} %pad_maximum_fusion.16), channel_id=1, source_target_pairs={{0,2},{2,0},{4,6},{6,4},{8,10},{10,8},{12,14},{14,12},{16,18},{18,... | collective-permute-start | bytes 4325384 | tf_op jit(solution)/shard_map/ppermute | solution.py:51
  510.7 43.3 %collective-permute-start.77 = (bf16[1,2,128,1408]{3,2,1,0:T(8,128)(2,1)S(1)}, bf16[1,2,128,1408]{3,2,1,0:T(8,128)(2,1)S(1)}, u32[]{:S(2)}, u32[]{:S(2)}) collective-permute-start(bf16[1,2,128,1408]{3,2,1,0:T(8,128)(2,1)S(1)} %add_convert_fusion.15), channel_id=1, source_target_pairs={{0,2},{2,0},{4,6},{6,4},{8,10},{10,8},{12,14},{14,12},{16,18},{18,... | collective-permute-start | bytes 2162696 | tf_op jit(solution)/shard_map/ppermute | solution.py:51
  515.0 42.4 %collective-permute-start.73 = (bf16[1,2,128,1408]{3,2,1,0:T(8,128)(2,1)S(1)}, bf16[1,2,128,1408]{3,2,1,0:T(8,128)(2,1)S(1)}, u32[]{:S(2)}, u32[]{:S(2)}) collective-permute-start(bf16[1,2,128,1408]{3,2,1,0:T(8,128)(2,1)S(1)} %add_convert_fusion.19), channel_id=1, source_target_pairs={{0,4},{2,6},{4,0},{6,2},{8,12},{10,14},{12,8},{14,10},{16,20},{18,... | collective-permute-start | bytes 2162696 | tf_op jit(solution)/shard_map/ppermute | solution.py:51
  518.0 51.5 %collective-permute-start.69 = (bf16[1,2,128,1408]{3,2,1,0:T(8,128)(2,1)S(1)}, bf16[1,2,128,1408]{3,2,1,0:T(8,128)(2,1)S(1)}, u32[]{:S(2)}, u32[]{:S(2)}) collective-permute-start(bf16[1,2,128,1408]{3,2,1,0:T(8,128)(2,1)S(1)} %add_convert_fusion.23), channel_id=1, source_target_pairs={{0,2},{2,0},{4,6},{6,4},{8,10},{10,8},{12,14},{14,12},{16,18},{18,... | collective-permute-start | bytes 2162696 | tf_op jit(solution)/shard_map/ppermute | solution.py:51
  554.0 44.3 %collective-permute-start.45 = (bf16[256,2048]{1,0:T(8,128)(2,1)}, bf16[256,2048]{1,0:T(8,128)(2,1)}, u32[]{:S(2)}, u32[]{:S(2)}) collective-permute-start(bf16[256,2048]{1,0:T(8,128)(2,1)} %add_convert_fusion.5), channel_id=1, source_target_pairs={{0,8},{2,10},{4,12},{6,14},{8,0},{10,2},{12,4},{14,6},{16,24},{18,... | collective-permute-start | bytes 3145736 | tf_op jit(solution)/shard_map/ppermute | solution.py:51
  556.2 40.2 %collective-permute-start.50 = (bf16[256,2048]{1,0:T(8,128)(2,1)}, bf16[256,2048]{1,0:T(8,128)(2,1)}, u32[]{:S(2)}, u32[]{:S(2)}) collective-permute-start(bf16[256,2048]{1,0:T(8,128)(2,1)} %add_convert_fusion.3), channel_id=1, source_target_pairs={{0,8},{2,10},{4,12},{6,14},{8,0},{10,2},{12,4},{14,6},{16,24},{18,... | collective-permute-start | bytes 3145736 | tf_op jit(solution)/shard_map/ppermute | solution.py:51
  577.6 55.9 %all-to-all-start.15 = ((bf16[4,128,1408]{2,1,0:T(8,128)(2,1)}), bf16[4,128,1408]{2,1,0:T(8,128)(2,1)}, u32[]{:S(2)}, u32[]{:S(2)}) async-start(bf16[4,128,1408]{2,1,0:T(8,128)(2,1)} %pad_maximum_fusion.23), calls=%async_computation.15 | async-start | bytes 2883584 | tf_op jit(solution)/shard_map/all_to_all | solution.py:57
  602.8 70.1 %collective-permute-start.52 = (bf16[256,2048]{1,0:T(8,128)(2,1)}, bf16[256,2048]{1,0:T(8,128)(2,1)}, u32[]{:S(2)}, u32[]{:S(2)}) collective-permute-start(bf16[256,2048]{1,0:T(8,128)(2,1)} %get-tuple-element.24), channel_id=1, source_target_pairs={{0,8},{2,10},{4,12},{6,14},{8,0},{10,2},{12,4},{14,6},{16,24},{18,... | collective-permute-start | bytes 3145736 | tf_op jit(solution)/shard_map/ppermute | solution.py:51
  602.8 102.8 %collective-permute-start.51 = (bf16[256,2048]{1,0:T(8,128)(2,1)}, bf16[256,2048]{1,0:T(8,128)(2,1)}, u32[]{:S(2)}, u32[]{:S(2)}) collective-permute-start(bf16[256,2048]{1,0:T(8,128)(2,1)} %get-tuple-element.24), channel_id=1, source_target_pairs={{0,1},{1,0},{2,3},{3,2},{4,5},{5,4},{6,7},{7,6},{8,9},{9,8},{10,11... | collective-permute-start | bytes 3145736 | tf_op jit(solution)/shard_map/ppermute | solution.py:54
  662.6 38.8 %all-to-all-start.13 = ((bf16[4,128,1408]{2,1,0:T(8,128)(2,1)}), bf16[4,128,1408]{2,1,0:T(8,128)(2,1)}, u32[]{:S(2)}, u32[]{:S(2)}) async-start(bf16[4,128,1408]{2,1,0:T(8,128)(2,1)} %pad_maximum_fusion.17), calls=%async_computation.13 | async-start | bytes 2883584 | tf_op jit(solution)/shard_map/all_to_all | solution.py:57
  673.0 32.7 %collective-permute-start.53 = (bf16[256,2048]{1,0:T(8,128)(2,1)}, bf16[256,2048]{1,0:T(8,128)(2,1)}, u32[]{:S(2)}, u32[]{:S(2)}) collective-permute-start(bf16[256,2048]{1,0:T(8,128)(2,1)} %collective-permute-done.52), channel_id=1, source_target_pairs={{0,1},{1,0},{2,3},{3,2},{4,5},{5,4},{6,7},{7,6},{8,9},{9,8},{10,11... | collective-permute-start | bytes 3145736 | tf_op jit(solution)/shard_map/ppermute | solution.py:54
  725.1 89.3 %collective-permute-start.66 = (bf16[2,4,128,512]{3,2,1,0:T(8,128)(2,1)}, bf16[2,4,128,512]{3,2,1,0:T(8,128)(2,1)}, u32[]{:S(2)}, u32[]{:S(2)}) collective-permute-start(bf16[2,4,128,512]{3,2,1,0:T(8,128)(2,1)} %pad_maximum_fusion.29), channel_id=1, source_target_pairs={{0,4},{2,6},{4,0},{6,2},{8,12},{10,14},{12,8},{14,10},{16,20},{18,... | collective-permute-start | bytes 3145736 | tf_op jit(solution)/shard_map/ppermute | solution.py:51
  753.3 63.1 %collective-permute-start.64 = (bf16[2,4,128,512]{3,2,1,0:T(8,128)(2,1)}, bf16[2,4,128,512]{3,2,1,0:T(8,128)(2,1)}, u32[]{:S(2)}, u32[]{:S(2)}) collective-permute-start(bf16[2,4,128,512]{3,2,1,0:T(8,128)(2,1)} %pad_maximum_fusion.28), channel_id=1, source_target_pairs={{0,2},{2,0},{4,6},{6,4},{8,10},{10,8},{12,14},{14,12},{16,18},{18,... | collective-permute-start | bytes 3145736 | tf_op jit(solution)/shard_map/ppermute | solution.py:51
  769.4 79.8 %collective-permute-start.62 = (bf16[2,4,128,512]{3,2,1,0:T(8,128)(2,1)}, bf16[2,4,128,512]{3,2,1,0:T(8,128)(2,1)}, u32[]{:S(2)}, u32[]{:S(2)}) collective-permute-start(bf16[2,4,128,512]{3,2,1,0:T(8,128)(2,1)} %pad_maximum_fusion.27), channel_id=1, source_target_pairs={{0,4},{2,6},{4,0},{6,2},{8,12},{10,14},{12,8},{14,10},{16,20},{18,... | collective-permute-start | bytes 3145736 | tf_op jit(solution)/shard_map/ppermute | solution.py:51
  782.9 78.7 %collective-permute-start.60 = (bf16[2,4,128,512]{3,2,1,0:T(8,128)(2,1)}, bf16[2,4,128,512]{3,2,1,0:T(8,128)(2,1)}, u32[]{:S(2)}, u32[]{:S(2)}) collective-permute-start(bf16[2,4,128,512]{3,2,1,0:T(8,128)(2,1)} %pad_maximum_fusion.26), channel_id=1, source_target_pairs={{0,4},{2,6},{4,0},{6,2},{8,12},{10,14},{12,8},{14,10},{16,20},{18,... | collective-permute-start | bytes 3145736 | tf_op jit(solution)/shard_map/ppermute | solution.py:51
  802.2 73.9 %collective-permute-start.58 = (bf16[2,4,128,512]{3,2,1,0:T(8,128)(2,1)}, bf16[2,4,128,512]{3,2,1,0:T(8,128)(2,1)}, u32[]{:S(2)}, u32[]{:S(2)}) collective-permute-start(bf16[2,4,128,512]{3,2,1,0:T(8,128)(2,1)} %pad_maximum_fusion.25), channel_id=1, source_target_pairs={{0,2},{2,0},{4,6},{6,4},{8,10},{10,8},{12,14},{14,12},{16,18},{18,... | collective-permute-start | bytes 3145736 | tf_op jit(solution)/shard_map/ppermute | solution.py:51
  818.4 33.6 %collective-permute-start.65 = (bf16[1,4,128,512]{3,2,1,0:T(8,128)(2,1)}, bf16[1,4,128,512]{3,2,1,0:T(8,128)(2,1)}, u32[]{:S(2)}, u32[]{:S(2)}) collective-permute-start(bf16[1,4,128,512]{3,2,1,0:T(8,128)(2,1)} %fusion.19), channel_id=1, source_target_pairs={{0,4},{2,6},{4,0},{6,2},{8,12},{10,14},{12,8},{14,10},{16,20},{18,... | collective-permute-start | bytes 1572872 | tf_op jit(solution)/shard_map/ppermute | solution.py:51
  846.0 48.0 %collective-permute-start.56 = (bf16[512,2048]{1,0:T(8,128)(2,1)}, bf16[512,2048]{1,0:T(8,128)(2,1)S(1)}, u32[]{:S(2)}, u32[]{:S(2)}) collective-permute-start(bf16[512,2048]{1,0:T(8,128)(2,1)} %pad_maximum_fusion.12), channel_id=1, source_target_pairs={{0,1},{1,0},{2,3},{3,2},{4,5},{5,4},{6,7},{7,6},{8,9},{9,8},{10,11... | collective-permute-start | bytes 6291464 | tf_op jit(solution)/shard_map/ppermute | solution.py:54
  896.6 42.9 %collective-permute-start.57 = (bf16[256,2048]{1,0:T(8,128)(2,1)}, bf16[256,2048]{1,0:T(8,128)(2,1)S(1)}, u32[]{:S(2)}, u32[]{:S(2)}) collective-permute-start(bf16[256,2048]{1,0:T(8,128)(2,1)} %add_convert_fusion.2), channel_id=1, source_target_pairs={{0,8},{2,10},{4,12},{6,14},{8,0},{10,2},{12,4},{14,6},{16,24},{18,... | collective-permute-start | bytes 3145736 | tf_op jit(solution)/shard_map/ppermute | solution.py:51
  (149 other events, 2395.3 us)

commit v2 on v1

v2 whole, which is shorter than its diff:
```python
import functools

import jax
import jax.numpy as jnp
from jax import lax
from jax.experimental import pallas as pl
from jax.experimental.pallas import tpu as pltpu
from jax.sharding import PartitionSpec as P

HEAD_DIM = 128
LINE = 4
EPS = 1e-06
DECAY = 2.0
F32 = jnp.float32
BF16 = jnp.bfloat16


def mm(a, b, out=F32):
    return lax.dot_general(a, b, (((1,), (0,)), ((), ())), preferred_element_type=F32).astype(out)


def mm_t(a, b, out=F32):
    return lax.dot_general(a, b, (((1,), (1,)), ((), ())), preferred_element_type=F32).astype(out)


def t_mm(a, b, out=F32):
    return lax.dot_general(a, b, (((0,), (0,)), ((), ())), preferred_element_type=F32).astype(out)


def norm_scale_of(values):
    return lax.rsqrt(jnp.mean(values * values, axis=-1, keepdims=True) + EPS)


def norm_back(values, scale, gradient):
    inner = jnp.mean(gradient * values, axis=-1, keepdims=True)
    return scale * gradient - values * (scale * scale * scale) * inner


def after(value, *deps):
    return lax.optimization_barrier((value,) + deps)[0]


class Net:
    def __init__(self, wide):
        self.wide = wide
        self.me = lax.axis_index("wide")
        self.n_plane = wide // LINE
        self.lines = [
            [base + 4 * k for k in range(LINE)] for base in range(wide) if not base & 12
        ]
        self.planes = [[w for w in range(wide) if (w >> 2) % LINE == z] for z in range(LINE)]

    def flip(self, value, bit):
        return lax.ppermute(value, "wide", [(w, w ^ (1 << bit)) for w in range(self.wide)])

    def core(self, value):
        return lax.ppermute(value, "narrow", [(0, 1), (1, 0)])

    def line(self, value):
        return lax.all_to_all(
            value, "wide", 0, 0, axis_index_groups=self.lines, tiled=True
        )

    def permute(self, value):
        tokens, cols = value.shape
        value = value.reshape(tokens, self.n_plane // 4, LINE, 4, cols // self.wide)
        return value.transpose(0, 1, 3, 2, 4).reshape(tokens, cols)

    def restore(self, value):
        tokens, cols = value.shape
        value = value.reshape(tokens, self.n_plane // 4, 4, LINE, cols // self.wide)
        return value.transpose(0, 1, 3, 2, 4).reshape(tokens, cols)

    def gather(self, lined):
        return lax.all_gather(lined, "wide", axis=0, axis_index_groups=self.planes, tiled=True)

    def reduce(self, grad):
        lined = lax.psum_scatter(
            grad, "wide", scatter_dimension=0, axis_index_groups=self.planes, tiled=True
        )
        got = self.line(lined.reshape(LINE, -1, grad.shape[1])).astype(F32)
        return jnp.concatenate([got[0] + got[2], got[1] + got[3]], axis=1)

    def group_gather(self, value):
        near = self.core(value)
        far = self.flip(value, 2)
        return jnp.concatenate([value, near, far, self.core(far)], axis=0)

    def group_sum(self, value):
        quarter = value.shape[0] // 4
        b = value.reshape(4, quarter)
        got = self.core(b)
        b = b + jnp.concatenate([got[1:2], got[0:1], got[3:4], got[2:3]])
        got = self.flip(b, 2)
        return (b + jnp.concatenate([got[2:], got[:2]])).reshape(-1)

    def group_scatter(self, value):
        quarter = value.shape[0] // 4
        b = [value[i * quarter : (i + 1) * quarter] for i in range(4)]
        got = self.core(jnp.concatenate([b[1], b[3]]))
        far = (b[2].astype(F32) + got[quarter:].astype(F32)).astype(BF16)
        own = b[0].astype(F32) + got[:quarter].astype(F32)
        return own + self.flip(far, 2).astype(F32)


def place_of(wide):
    me = lax.axis_index("wide")
    z = (me // 4) % LINE

    def on_line(k):
        there = (z + k) % LINE
        return me + (there - z) * 4, there

    def flip(bit):
        return me + (1 - 2 * ((me >> bit) & 1)) * (1 << bit)

    return me, lax.axis_index("narrow"), z, on_line, flip


def meet(devices):
    barrier = pltpu.get_barrier_semaphore()
    for device in devices:
        pl.semaphore_signal(
            barrier, inc=1, device_id=device, device_id_type=pl.DeviceIdType.MESH
        )
    pl.semaphore_wait(barrier, len(devices))


def gather_kernel(wide, chunks, n_in, n_out, *refs):
    ins, outs = refs[: n_in + 2], refs[n_in + 2 : n_in + n_out + 4]
    line_send, line_recv, own_sem, plane_send, plane_recv, token_sem, token_send, token_recv = refs[
        n_in + n_out + 4 :
    ]
    me, core, z, on_line, flip = place_of(wide)
    extra = list(range(4, wide.bit_length() - 1))
    plane_at = (me // 16) * 4 + me % 4
    others = [on_line(k)[0] for k in (1, 2, 3)] + [flip(b) for b in [0, 1] + extra]
    meet([(other, core) for other in others] + [(me, 1 - core)])
    rb = ins[0].shape[0]

    def token_copies(i):
        source, out = ins[n_in + i], outs[n_out + i]
        size = source.shape[0]

        def send(j, source, device):
            return pltpu.make_async_remote_copy(
                src_ref=source, dst_ref=out.at[pl.ds((j + 1) * size, size)],
                send_sem=token_send.at[i, j], recv_sem=token_recv.at[i, j],
                device_id=device, device_id_type=pl.DeviceIdType.MESH,
            )

        return (
            pltpu.make_async_copy(source, out.at[pl.ds(0, size)], token_sem.at[i]),
            send(0, source, (me, 1 - core)),
            send(1, source, (flip(2), core)),
            send(2, out.at[pl.ds(2 * size, size)], (me, 1 - core)),
        )

    def part(i, start, size):
        source, out, col, _ = chunks[i]
        width = ins[source].shape[1] // 2
        return outs[out].at[pl.ds(pl.multiple_of(start, min(size, rb)), size), pl.ds(col, width)]

    def block(m):
        return (plane_at ^ m) * (LINE * rb)

    def mine(i, there):
        source = chunks[i][0]
        width = ins[source].shape[1] // 2
        return ins[source].at[:, pl.ds(pl.multiple_of((there % 2) * width, HEAD_DIM), width)]

    def landing(i):
        return part(i, (block(0) if chunks[i][3] else 0) + z * rb, rb)

    def line_copy(i, k):
        device, there = on_line(k)
        return pltpu.make_async_remote_copy(
            src_ref=mine(i, there), dst_ref=landing(i),
            send_sem=line_send.at[i, k - 1], recv_sem=line_recv.at[i, k - 1],
            device_id=(device, core), device_id_type=pl.DeviceIdType.MESH,
        )

    def own_copy(i):
        return pltpu.make_async_copy(mine(i, z), landing(i), own_sem.at[i])

    def plane(i, j, start, size, bit):
        return pltpu.make_async_remote_copy(
            src_ref=part(i, start, size), dst_ref=part(i, start, size),
            send_sem=plane_send.at[i, j], recv_sem=plane_recv.at[i, j],
            device_id=(flip(bit), core), device_id_type=pl.DeviceIdType.MESH,
        )

    q = LINE * rb
    h = q // 2

    def first(i):
        return plane(i, 0, block(0), q, 0), plane(i, 1, block(0), q, 1)

    def second(i):
        return plane(i, 2, block(1), h, 1), plane(i, 3, block(2) + h, h, 0)

    def start_line(i):
        own_copy(i).start()
        for k in (1, 2, 3):
            line_copy(i, k).start()

    count = len(chunks)
    spread = [c[3] for c in chunks]
    tokens = [token_copies(0), token_copies(1)]
    for copy in tokens[0][:3]:
        copy.start()
    for i in range(2):
        start_line(i)
    for i in range(count + 1):
        if i == 2:
            for copy in tokens[1][:3]:
                copy.start()
            tokens[0][2].wait_recv()
            tokens[0][3].start()
        if i < count:
            own_copy(i).wait()
            for k in (1, 2, 3):
                line_copy(i, k).wait_recv()
            if spread[i]:
                for copy in first(i):
                    copy.start()
            if i + 2 < count:
                start_line(i + 2)
        if i > 0 and spread[i - 1]:
            for got, onward in zip(first(i - 1), second(i - 1)):
                got.wait_recv()
                onward.start()
    tokens[1][2].wait_recv()
    tokens[1][3].start()
    for own, near, far, onward in tokens:
        own.wait()
        near.wait()
        far.wait_send()
        onward.wait()
    for i in range(count):
        for k in (1, 2, 3):
            line_copy(i, k).wait_send()
        if spread[i]:
            for copy in first(i):
                copy.wait_send()
            for copy in second(i):
                copy.wait()
    for e, bit in enumerate(extra):
        size = q << (2 + e)
        start = (plane_at >> (2 + e)) * size
        copies = [plane(i, 4 + e, start, size, bit) for i in range(count) if spread[i]]
        for copy in copies:
            copy.start()
        for copy in copies:
            copy.wait()


def gather_weights(wide, weights, chunks, outs, tokens):
    count = len(chunks)
    steps = wide.bit_length() - 1
    anywhere = pl.BlockSpec(memory_space=pl.ANY)
    dma = pltpu.SemaphoreType.DMA
    return pl.pallas_call(
        functools.partial(gather_kernel, wide, chunks, len(weights), len(outs)),
        out_shape=[jax.ShapeDtypeStruct(o, BF16) for o in outs]
        + [jax.ShapeDtypeStruct((4 * t.shape[0], t.shape[1]), BF16) for t in tokens],
        in_specs=[anywhere] * (len(weights) + 2),
        out_specs=[anywhere] * (len(outs) + 2),
        scratch_shapes=[dma((count, 3)), dma((count, 3)), dma((count,)), dma((count, steps)), dma((count, steps))]
        + [dma((2,)), dma((2, 3)), dma((2, 3))],
        compiler_params=pltpu.CompilerParams(
            has_side_effects=True, collective_id=1, vmem_limit_bytes=1 << 20
        ),
        cost_estimate=pl.CostEstimate(flops=0, bytes_accessed=300 << 20, transcendentals=0),
    )(*weights, *tokens)


def reduce_kernel(wide, count, *refs):
    grads, outs = refs[:count], refs[count : 2 * count]
    held, near, far, line, more, load_sem, send, recv, line_send, line_recv, more_send, more_recv = refs[2 * count :]
    me, core, z, on_line, flip = place_of(wide)
    extra = list(range(4, wide.bit_length() - 1))
    plane_at = (me // 16) * 4 + me % 4
    others = [on_line(k)[0] for k in (1, 2, 3)] + [flip(b) for b in [0, 1] + extra]
    rows, cols = grads[0].shape
    rb = rows // wide
    q = LINE * rb
    h = q // 2

    def rows_at(i, start, size):
        return held.at[i, pl.ds(pl.multiple_of(start, min(size, h)), size)]

    def block(m):
        return (plane_at ^ m) * q

    def remote(source, target, send_sem, recv_sem, device):
        return pltpu.make_async_remote_copy(
            src_ref=source, dst_ref=target, send_sem=send_sem, recv_sem=recv_sem,
            device_id=(device, core), device_id_type=pl.DeviceIdType.MESH,
        )

    def step(i, j, start, size, target, bit):
        return remote(rows_at(i, start, size), target, send.at[i, j], recv.at[i, j], flip(bit))

    def copies(i):
        return (
            step(i, 0, block(3), h, near.at[i, 0], 1),
            step(i, 1, block(3) + h, h, near.at[i, 1], 0),
            step(i, 2, block(1) + h, h, far.at[i, 0, pl.ds(h, h)], 0),
            step(i, 3, block(2), h, far.at[i, 1, pl.ds(0, h)], 1),
            step(i, 4, block(1), h, far.at[i, 0, pl.ds(0, h)], 0),
            step(i, 5, block(2) + h, h, far.at[i, 1, pl.ds(h, h)], 1),
        )

    def line_copy(i, k):
        device, there = on_line(k)
        return remote(
            rows_at(i, block(0) + there * rb, rb), line.at[i, k - 1],
            line_send.at[i, k - 1], line_recv.at[i, k - 1], device,
        )

    def load(i):
        return pltpu.make_async_copy(grads[i], held.at[i], load_sem.at[i])

    def add(i, start, size, *sources):
        tile = min(64, size)

        def body(n, carry):
            at = pl.ds(pl.multiple_of(start + n * tile, tile), tile)
            total = held[i, at].astype(F32)
            for source in sources:
                total = total + source[pl.ds(n * tile, tile)].astype(F32)
            held[i, at] = total.astype(BF16)
            return carry

        lax.fori_loop(0, size // tile, body, 0)

    for i in range(count):
        load(i).start()
    meet([(other, core) for other in others])

    def begin(i):
        load(i).wait()
        for e in reversed(range(len(extra))):
            size = q << (2 + e)
            half = plane_at >> (2 + e)
            copy = remote(
                rows_at(i, (half ^ 1) * size, size), more.at[i, e, pl.ds(0, size)],
                more_send.at[i, e], more_recv.at[i, e], flip(extra[e]),
            )
            copy.start()
            copy.wait()
            add(i, half * size, size, more.at[i, e])
        for copy in copies(i)[:4]:
            copy.start()

    def fold(i):
        c = copies(i)
        c[0].wait_recv()
        add(i, block(1), h, near.at[i, 0])
        c[4].start()
        c[1].wait_recv()
        add(i, block(2) + h, h, near.at[i, 1])
        c[5].start()

    def to_line(i):
        for copy in copies(i)[2:]:
            copy.wait_recv()
        add(i, block(0), q, far.at[i, 0], far.at[i, 1])
        for k in (1, 2, 3):
            line_copy(i, k).start()

    def finish(i):
        for k in (1, 2, 3):
            line_copy(i, k).wait_recv()
        own = held[i, pl.ds(pl.multiple_of(block(0) + z * rb, rb), rb)].astype(F32) + line[i, 1].astype(F32)
        other = line[i, 0].astype(F32) + line[i, 2].astype(F32)
        lower = z % 2 == 0

        @pl.when(lower)
        def _():
            outs[i][:, pl.ds(0, cols)] = own
            outs[i][:, pl.ds(cols, cols)] = other

        @pl.when(jnp.logical_not(lower))
        def _():
            outs[i][:, pl.ds(0, cols)] = other
            outs[i][:, pl.ds(cols, cols)] = own

    for n in range(count + 3):
        if n < count:
            begin(n)
        if 0 <= n - 1 < count:
            fold(n - 1)
        if 0 <= n - 2 < count:
            to_line(n - 2)
        if 0 <= n - 3 < count:
            finish(n - 3)
    for i in range(count):
        for copy in copies(i):
            copy.wait_send()
        for k in (1, 2, 3):
            line_copy(i, k).wait_send()


def reduce_weights(wide, grads):
    count = len(grads)
    rows, cols = grads[0].shape
    rb = rows // wide
    q = LINE * rb
    extra = max(1, wide.bit_length() - 5)
    dma = pltpu.SemaphoreType.DMA
    return pl.pallas_call(
        functools.partial(reduce_kernel, wide, count),
        out_shape=[jax.ShapeDtypeStruct((rb, 2 * cols), F32)] * count,
        in_specs=[pl.BlockSpec(memory_space=pl.ANY)] * count,
        out_specs=[pl.BlockSpec(memory_space=pltpu.VMEM)] * count,
        scratch_shapes=[
            pltpu.VMEM((count, rows, cols), BF16),
            pltpu.VMEM((count, 2, q // 2, cols), BF16),
            pltpu.VMEM((count, 2, q, cols), BF16),
            pltpu.VMEM((count, 3, rb, cols), BF16),
            pltpu.VMEM((count, extra, rows // 2 if wide > 16 else 16, cols), BF16),
            dma((count,)),
            dma((count, 6)),
            dma((count, 6)),
            dma((count, 3)),
            dma((count, 3)),
            dma((count, extra)),
            dma((count, extra)),
        ],
        compiler_params=pltpu.CompilerParams(
            has_side_effects=True, collective_id=2, vmem_limit_bytes=48 << 20
        ),
        cost_estimate=pl.CostEstimate(flops=0, bytes_accessed=300 << 20, transcendentals=0),
    )(*grads)


def masks(lengths, places, rates):
    starts, total = [], 0
    for c in range(lengths.shape[1] - 1):
        total = total + lengths[:, c]
        starts.append(total)
    starts = jnp.stack(starts, axis=1)
    docs = jnp.sum((places[None, :, None] >= starts[:, None, :]).astype(jnp.int32), axis=2)
    gap = places[:, None] - places[None, :]
    allowed = (gap >= 0)[None] & (docs[:, :, None] == docs[:, None, :])
    spread = jnp.maximum(gap, 0).astype(F32)
    weights = jnp.exp(-rates[:, None, None] * spread[None])
    return jnp.where(allowed[:, None], weights[None], 0.0)


def sigmoid(z):
    return 1.0 / (1.0 + jnp.exp(-z))


def on_device(
    layer_input, doc_lengths, w_query, w_key, w_value, w_gate, w_output, w_left, w_right, w_down, cotangent, *, wide
):
    net = Net(wide)
    core = lax.axis_index("narrow")
    half = (net.me >> 2) & 1
    features = layer_input.shape[1]

    inputs = net.permute(layer_input).astype(F32)
    norm_one = norm_scale_of(inputs)
    cot = net.permute(cotangent)
    rows, small, large = features, w_query.shape[1] // 2, w_left.shape[1] // 2
    qk_w, vg_w, output_w, left_lined, right_lined, down_lined, normed, cot_all = gather_weights(
        wide,
        [w_query, w_key, w_value, w_gate, w_output, w_left, w_right, w_down],
        [(0, 0, 0, 1), (1, 0, small, 1), (2, 1, 0, 1), (3, 1, small, 1), (4, 2, 0, 1), (5, 3, 0, 0), (6, 4, 0, 0), (7, 5, 0, 0)],
        [(rows, 2 * small), (rows, 2 * small), (rows, small), *[(LINE * w_left.shape[0], large)] * 3],
        [(inputs * norm_one).astype(BF16), cot],
    )
    left_w = net.gather(left_lined)
    right_w = net.gather(right_lined)
    down_w = net.gather(down_lined)

    quarter = inputs.shape[0]
    tokens = 4 * quarter
    row_len = 2 * quarter
    width = output_w.shape[1]
    heads = width // HEAD_DIM
    all_heads = features // HEAD_DIM
    head_ids = (core * 2 + half) * heads + jnp.arange(heads, dtype=jnp.int32)
    rates = DECAY * head_ids.astype(F32) / all_heads
    own = jnp.arange(quarter, dtype=jnp.int32)
    places = jnp.concatenate([own + core * quarter, own + (1 - core) * quarter])
    lengths = jnp.concatenate([doc_lengths, net.flip(doc_lengths, 2)])
    decay = masks(lengths, places, rates)

    qk_pre = mm(normed, qk_w)
    query_pre, key_pre = qk_pre[:, :width], qk_pre[:, width:]
    vg = mm(normed, vg_w)
    values, gate = vg[:, :width].astype(BF16), vg[:, width:]
    query_sig, key_sig = sigmoid(query_pre), sigmoid(key_pre)
    queries = (query_pre * query_sig).astype(BF16)
    keys = (key_pre * key_sig).astype(BF16)
    shape = (2, row_len, heads, HEAD_DIM)
    q4, k4, v4 = (a.reshape(shape) for a in (queries, keys, values))
    scores = jnp.einsum("rihd,rjhd->rhij", q4, k4, preferred_element_type=F32)
    probs = (scores * decay).astype(BF16)
    mixed = jnp.einsum("rhij,rjhd->rihd", probs, v4, preferred_element_type=F32)
    mixed = mixed.reshape(tokens, width)
    squares = net.group_sum(jnp.sum(mixed * mixed, axis=1))
    attn_scale = lax.rsqrt(squares / features + EPS)[:, None]
    scaled = mixed * attn_scale
    blended = (gate * scaled).astype(BF16)
    middle = inputs + net.group_scatter(mm_t(blended, output_w, BF16))
    norm_two = norm_scale_of(middle)
    mid = net.group_gather((middle * norm_two).astype(BF16))
    left = mm(mid, left_w)
    right = mm(mid, right_w)
    product = (left * right).astype(BF16)
    grad_down = t_mm(cot_all, product, BF16)
    output_part = mm_t(product, down_w, BF16)
    layer_output = middle + net.group_scatter(output_part)
    layer_output = net.restore(layer_output.astype(BF16))

    grad_product = mm(cot_all, down_w)
    grad_left_pre = (grad_product * right).astype(BF16)
    grad_right_pre = (grad_product * left).astype(BF16)
    grad_mid = net.group_scatter(
        (mm_t(grad_left_pre, left_w) + mm_t(grad_right_pre, right_w)).astype(BF16)
    )
    grad_left = t_mm(mid, grad_left_pre, BF16)
    grad_right = t_mm(mid, grad_right_pre, BF16)
    grad_mid = after(grad_mid, grad_left, grad_right)
    grad_middle = cot.astype(F32) + norm_back(middle, norm_two, grad_mid)
    branch = net.group_gather(grad_middle.astype(BF16))
    branch = after(branch, output_part, grad_down)
    grad_left, grad_right, grad_down = (net.reduce(g) for g in (grad_left, grad_right, grad_down))
    grad_blended = mm(branch, output_w)
    grad_output = t_mm(branch, blended, BF16)
    grad_gate_pre = (grad_blended * scaled).astype(BF16)
    grad_gate = t_mm(normed, grad_gate_pre, BF16)
    grad_scaled = grad_blended * gate
    inner = net.group_sum(jnp.sum(grad_scaled * mixed, axis=1)) / features
    grad_mixed = (
        attn_scale * grad_scaled - mixed * (attn_scale * attn_scale * attn_scale) * inner[:, None]
    ).astype(BF16)
    g4 = grad_mixed.reshape(shape)
    grad_probs = jnp.einsum("rihd,rjhd->rhij", g4, v4, preferred_element_type=F32)
    grad_values = jnp.einsum("rhij,rihd->rjhd", probs, g4, preferred_element_type=F32)
    grad_value_pre = grad_values.astype(BF16).reshape(tokens, width)
    grad_value = t_mm(normed, grad_value_pre, BF16)
    grad_scores = (grad_probs * decay).astype(BF16)
    grad_queries = jnp.einsum("rhij,rjhd->rihd", grad_scores, k4, preferred_element_type=F32)
    grad_keys = jnp.einsum("rhij,rihd->rjhd", grad_scores, q4, preferred_element_type=F32)
    grad_query_pre = (
        grad_queries.reshape(tokens, width) * (query_sig * (1.0 + query_pre * (1.0 - query_sig)))
    ).astype(BF16)
    grad_key_pre = (
        grad_keys.reshape(tokens, width) * (key_sig * (1.0 + key_pre * (1.0 - key_sig)))
    ).astype(BF16)
    grad_query = t_mm(normed, grad_query_pre, BF16)
    grad_key = t_mm(normed, grad_key_pre, BF16)
    grad_output, grad_gate, grad_value, grad_query, grad_key = reduce_weights(
        wide, [grad_output, grad_gate, grad_value, grad_query, grad_key]
    )
    total = mm_t(jnp.concatenate([grad_value_pre, grad_gate_pre], axis=1), vg_w)
    total = total + mm_t(jnp.concatenate([grad_query_pre, grad_key_pre], axis=1), qk_w)
    grad_normed = net.group_scatter(total.astype(BF16))
    input_grad = net.restore(grad_middle + norm_back(inputs, norm_one, grad_normed))
    return (
        layer_output,
        input_grad,
        grad_query,
        grad_key,
        grad_value,
        grad_gate,
        grad_output,
        grad_left,
        grad_right,
        grad_down,
    )


def solution(mesh):
    both, weight = P(("wide", "narrow"), None), P("wide", "narrow")
    wide = mesh.shape["wide"]

    def body(*args):
        return on_device(*args, wide=wide)

    return jax.shard_map(
        body,
        mesh=mesh,
        in_specs=(both, P("wide", None)) + (weight,) * 8 + (both,),
        out_specs=(both, both) + (weight,) * 8,
        check_vma=False,
    )
```

time: 957 us -> 838 us (0.88)
  Pallas kernels: 0 us -> 276 us
  starting transfers between devices: 211 us -> 33.4 us
  waiting for transfers between devices: 317 us -> 193 us
  other arithmetic: 138 us -> 61.8 us
  matrix products: 207 us -> 171 us
  between operations: 2.67 us -> 15.6 us
    pallas_call x0 -> x2, Pallas kernels: none -> 276 us  [the longest x1 173 us: gather_weights(): pl.pallas_call(functools.partial(gather_kernel, wide, chunks, len(weights...]
    ppermute x66 -> x9, waiting for transfers between devices: 206 us -> 101 us  [flip(): lax.ppermute(value, 'wide', [(w, w ^ 1 << bit) for w in range(self.wide)])]
    all_to_all x16 -> x3, waiting for transfers between devices: 112 us -> 22.7 us  [line(): lax.all_to_all(value, 'wide', 0, 0, axis_index_groups=self.lines, tiled=T...]
    all_to_all x16 -> x3, starting transfers between devices: 88.8 us -> 17.6 us  [line(): lax.all_to_all(value, 'wide', 0, 0, axis_index_groups=self.lines, tiled=T...]
    all_gather x0 -> x3, waiting for transfers between devices: none -> 58.9 us  [gather(): lax.all_gather(lined, 'wide', axis=0, axis_index_groups=self.planes, tile...]
    ppermute x14 -> x10, starting transfers between devices: 66.1 us -> 10.6 us  [core(): return lax.ppermute(value, 'narrow', [(0, 1), (1, 0)])]
    ppermute x66 -> x9, starting transfers between devices: 56.2 us -> 4.67 us  [flip(): lax.ppermute(value, 'wide', [(w, w ^ 1 << bit) for w in range(self.wide)])]
    convert_element_type x30 -> x7, other arithmetic: 55.6 us -> 16.5 us  [the longest x1 4.75 us: on_device(): grad_mixed = (attn_scale * grad_scaled - mixed * (attn_scale * attn_scale...]
  transfers between devices with their start and end apart: 96 -> 28, of which waited for: 35 -> 15; matrix products, arithmetic and copies ran while one was open for 37% -> 28% of each run, Pallas kernels for 0% -> 12%
where the time goes in v2:
time: 838 us; the launch traced here: 826 us
  Pallas kernels  276 us (33%)
  waiting for transfers between devices  193 us (23%)
  matrix products  171 us (20%)
  local copies, waits for them, and re-layouts  75.2 us (9%)
  other arithmetic  61.8 us (7%)
  starting transfers between devices  33.4 us (4%)
  between operations  15.6 us (2%)
    pallas_call x1, Pallas kernels, gather_weights(): pl.pallas_call(functools.partial(gather_kernel, wide, chunks, len(weights...  173 us
    pallas_call x1, Pallas kernels, reduce_weights(): pl.pallas_call(functools.partial(reduce_kernel, wide, count), out_shape=[...  103 us
    ppermute x9, waiting for transfers between devices, flip(): lax.ppermute(value, 'wide', [(w, w ^ 1 << bit) for w in range(self.wide)])  101 us
    dot_general x6, matrix products, mm(): lax.dot_general(a, b, (((1,), (0,)), ((), ())), preferred_element_type=F32)  59.5 us
    all_gather x3, waiting for transfers between devices, gather(): lax.all_gather(lined, 'wide', axis=0, axis_index_groups=self.planes, tile...  58.9 us
    dot_general x8, matrix products, t_mm(): lax.dot_general(a, b, (((0,), (0,)), ((), ())), preferred_element_type=F32)  53.1 us
    dot_general x6, matrix products, mm_t(): lax.dot_general(a, b, (((1,), (1,)), ((), ())), preferred_element_type=F32)  43.4 us
    unnamed x176, local copies, waits for them, and re-layouts  32.4 us
  transfers between devices with their start and end apart: 28, of which 15 were waited for; matrix products, arithmetic and copies ran while one was open for 28% of the time, Pallas kernels for 12%

profile of v2, /device:TPU:25, one launch (start us, length us, event | category | flops | bytes accessed | tf_op | source)
XLA Modules:
  0.0 825.9 jit_solution(5030447360575850432)
XLA Ops:
  8.7 2.8 reshape.268
  19.1 3.3 reshape.267
  24.3 173.1 %shard_map.186 = (bf16[2048,1024]{1,0:T(8,128)(2,1)S(1)}, bf16[2048,1024]{1,0:T(8,128)(2,1)S(1)}, bf16[2048,512]{1,0:T(8,128)(2,1)S(1)}, bf16[512,1408]{1,0:T(8,...) custom-call(bf16[128,1024]{1,0:T(8,128)(2,1)S(1)} %copy-done.9, ...), custom_call_target="tpu_custom_call" | custom-call | bytes 314572800 | tf_op jit(solution)/shard_map/pallas_call | solution.py:263
  207.8 10.2 %fusion.39 = f32[1024,1024]{0,1:T(8,128)} fusion(bf16[1024,2048]{1,0:T(8,128)(2,1)} %copy-done.14, bf16[2048,1024]{1,0:T(8,128)(2,1)} %copy-done.21), kind=kOutput, calls=%fused_computation.132 | convolution fusion | flops 4294967296 | bytes 12582912 | tf_op jit(solution)/shard_map/dot_general | solution.py:19
  218.1 6.1 fusion.40
  227.7 4.7 multiply_convert_fusion.8
  240.2 5.0 fusion
  245.3 2.8 multiply_reduce_fusion.4
  250.0 3.2 copy.43
  262.7 4.0 collective-permute-done.3
  269.5 23.7 %collective-permute-done.4 = bf16[256,2048]{1,0:T(8,128)(2,1)S(1)} collective-permute-done((bf16[256,2048]{1,0:T(8,128)(2,1)S(1)}, bf16[256,2048]{1,0:T(8,128)(2,1)S(1)}, u32[]{:S(2)}, u32[]{:S(2)}) %collective-permute-start.4) | collective-permute-done | bytes 1048608 | tf_op jit(solution)/shard_map/ppermute | solution.py:54
  299.1 21.5 %collective-permute-done.6 = bf16[256,2048]{1,0:T(8,128)(2,1)S(1)} collective-permute-done((bf16[256,2048]{1,0:T(8,128)(2,1)S(1)}, bf16[256,2048]{1,0:T(8,128)(2,1)S(1)}, u32[]{:S(2)}, u32[]{:S(2)}) %collective-permute-start.6) | collective-permute-done | bytes 1048608 | tf_op jit(solution)/shard_map/ppermute | solution.py:54
  325.0 12.9 %fusion.28 = f32[1024,1408]{1,0:T(8,128)} fusion(bf16[2048,1408]{1,0:T(8,128)(2,1)} %all-gather.6.cloned.1.call-done, bf16[256,2048]{1,0:T(8,128)(2,1)} %collective-permute-done.7, bf16[256,2048]{1,0:T(8,128)(2,1)} %copy-done.72, bf16[256,2048]{1,0:T(8,128)(2,1)} %copy-done.74, bf16[256,2048]{1,0:T(8,128)(2,1)} %copy-done.60), kind=kOutput, calls=%fused_computation.121 | convolution fusion | flops 5922357248 | bytes 15728640 | tf_op jit(solution)/shard_map/dot_general | solution.py:19
  337.9 3.0 all-gather.8.cloned.1.call-done
  340.9 11.8 %fusion.41 = f32[1024,1408]{1,0:T(8,128)} fusion(bf16[1024,2048]{1,0:T(8,128)(2,1)} %copy-done.23, bf16[2048,1408]{1,0:T(8,128)(2,1)} %all-gather.8.cloned.1.call-done), kind=kOutput, calls=%fused_computation.134 | convolution fusion | flops 5905580032 | bytes 15728640 | tf_op jit(solution)/shard_map/dot_general | solution.py:19
  352.7 55.9 %all-gather.4.cloned.1.call-done = bf16[2048,1408]{1,0:T(8,128)(2,1)} async-done(((bf16[512,1408]{1,0:T(8,128)(2,1)}), bf16[2048,1408]{1,0:T(8,128)(2,1)}) %all-gather.4.cloned.1.call-update) | async-done | bytes 5767184 | tf_op jit(solution)/shard_map/all_gather | solution.py:75
  408.6 14.7 %multiply_convert_fusion = (bf16[1024,1408]{1,0:T(8,128)(2,1)}, bf16[1024,1408]{1,0:T(8,128)(2,1)S(1)}, bf16[1024,1408]{1,0:T(8,128)(2,1)}) fusion(f32[1024,1408]{1,0:T(8,128)} %fusion.41, f32[1024,1408]{1,0:T(8,128)} %fusion.28, bf16[2048,1408]{1,0:T(8,128)(2,1)} %all-gather.4.cloned.1.call-done, bf16[256,2048]{1,0:T(8,128)(2,1)} %collective-permute-done.7, ...), kind=kOutput, calls=%fused_computation.9 | convolution fusion | flops 5931008000 | bytes 30146560 | tf_op jit(solution)/shard_map/dot_general | solution.py:19
  424.8 8.7 %convolution_convert_fusion = bf16[2048,1408]{1,0:T(8,128)(2,1)} fusion(bf16[1024,2048]{1,0:T(8,128)(2,1)S(1)} %copy-done.24, bf16[1024,1408]{1,0:T(8,128)(2,1)S(1)} %get-tuple-element.49), kind=kOutput, calls=%fused_computation.6 | convolution fusion | flops 5908463616 | bytes 12845056 | tf_op jit(solution)/shard_map/dot_general | solution.py:27
  433.6 11.2 %convolution_convert_fusion.2 = bf16[2048,1408]{1,0:T(8,128)(2,1)} fusion(bf16[1024,1408]{1,0:T(8,128)(2,1)} %get-tuple-element.50, bf16[256,2048]{1,0:T(8,128)(2,1)} %collective-permute-done.7, bf16[256,2048]{1,0:T(8,128)(2,1)} %copy-done.72, bf16[256,2048]{1,0:T(8,128)(2,1)} %copy-done.74, bf16[256,2048]{1,0:T(8,128)(2,1)} %copy-done.60), kind=kOutput, calls=%fused_computation.8 | convolution fusion | flops 5925240832 | bytes 12845056 | tf_op jit(solution)/shard_map/dot_general | solution.py:27
  444.9 11.8 %fusion.42 = f32[1024,2048]{1,0:T(8,128)} fusion(bf16[1024,1408]{1,0:T(8,128)(2,1)} %get-tuple-element.50, bf16[2048,1408]{1,0:T(8,128)(2,1)} %all-gather.4.cloned.1.call-done), kind=kOutput, calls=%fused_computation.135 | convolution fusion | flops 5905580032 | bytes 17039360 | tf_op jit(solution)/shard_map/dot_general | solution.py:23
  456.8 11.2 %add_convert_fusion.1 = bf16[1024,2048]{1,0:T(8,128)(2,1)S(1)} fusion(f32[1024,2048]{1,0:T(8,128)} %fusion.42, bf16[1024,1408]{1,0:T(8,128)(2,1)S(1)} %copy-done.76, bf16[2048,1408]{1,0:T(8,128)(2,1)} %all-gather.6.cloned.1.call-done), kind=kOutput, calls=%fused_computation.5 | convolution fusion | flops 5909774336 | bytes 21233664 | tf_op jit(solution)/shard_map/dot_general | solution.py:23
  471.4 6.9 convolution_convert_fusion.3
  483.9 10.4 %convolution_convert_fusion.1 = bf16[2048,1408]{1,0:T(8,128)(2,1)} fusion(bf16[1024,1408]{1,0:T(8,128)(2,1)S(1)} %copy-done.76, bf16[256,2048]{1,0:T(8,128)(2,1)} %collective-permute-done.7, bf16[256,2048]{1,0:T(8,128)(2,1)S(1)} %copy-done.73, bf16[256,2048]{1,0:T(8,128)(2,1)S(1)} %copy-done.75, bf16[256,2048]{1,0:T(8,128)(2,1)S(1)} %copy-done.61), kind=kOutput, calls=%fused_computation.7 | convolution fusion | flops 5925240832 | bytes 12845056 | tf_op jit(solution)/shard_map/dot_general | solution.py:27
  497.8 11.0 %collective-permute-done.11 = bf16[256,2048]{1,0:T(8,128)(2,1)} collective-permute-done((bf16[256,2048]{1,0:T(8,128)(2,1)}, bf16[256,2048]{1,0:T(8,128)(2,1)}, u32[]{:S(2)}, u32[]{:S(2)}) %collective-permute-start.11) | collective-permute-done | bytes 1048608 | tf_op jit(solution)/shard_map/ppermute | solution.py:54
  508.8 2.7 convert_add_fusion.1
  511.8 19.5 %collective-permute-done.9 = bf16[256,2048]{1,0:T(8,128)(2,1)S(1)} collective-permute-done((bf16[256,2048]{1,0:T(8,128)(2,1)S(1)}, bf16[256,2048]{1,0:T(8,128)(2,1)S(1)}, u32[]{:S(2)}, u32[]{:S(2)}) %collective-permute-start.9) | collective-permute-done | bytes 1048608 | tf_op jit(solution)/shard_map/ppermute | solution.py:54
  531.3 4.6 fusion.30
  537.1 23.1 %collective-permute-done.13 = bf16[256,2048]{1,0:T(8,128)(2,1)S(1)} collective-permute-done((bf16[256,2048]{1,0:T(8,128)(2,1)}, bf16[256,2048]{1,0:T(8,128)(2,1)S(1)}, u32[]{:S(2)}, u32[]{:S(2)}) %collective-permute-start.13) | collective-permute-done | bytes 1048608 | tf_op jit(solution)/shard_map/ppermute | solution.py:54
  566.2 3.9 multiply_reduce_fusion.1
  573.9 4.7 subtract_convert_fusion
  580.6 3.1 fusion.9
  599.3 4.8 fusion.2
  604.2 6.3 add_convert_fusion
  610.4 4.5 all-to-all-start.2
  623.6 5.2 convolution_convert_fusion.9.refs_0_
  628.8 3.8 convolution_convert_fusion.6.refs_3_
  632.7 12.6 %all-to-all-done.2 = bf16[4,128,1408]{2,1,0:T(8,128)(2,1)} async-done(((bf16[4,128,1408]{2,1,0:T(8,128)(2,1)}), bf16[4,128,1408]{2,1,0:T(8,128)(2,1)}, u32[]{:S(2)}, u32[]{:S(2)}) %all-to-all-start.2) | async-done | bytes 1441824 | tf_op jit(solution)/shard_map/all_to_all | solution.py:60
  645.2 8.2 all-to-all-start
  653.5 6.0 convolution_convert_fusion.5.refs_4_
  659.5 3.0 add_convert_fusion.2
  662.8 3.9 convolution_convert_fusion.7.refs_2_
  666.7 3.8 convolution_convert_fusion.8.refs_1_
  670.5 103.2 %shard_map.187 = (f32[128,1024]{1,0:T(8,128)S(1)}, f32[128,1024]{1,0:T(8,128)S(1)}, f32[128,1024]{1,0:T(8,128)S(1)}, f32[128,1024]{1,0:T(8,128)S(1)}, f32[128,1024]{1,0:T(8,128)S(1)}) custom-call(bf16[2048,512]{1,0:T(8,128)(2,1)S(1)} %convolution_convert_fusion.9.refs_0_, bf16[2048,512]{1,0:T(8,128)(2,1)} %convolution_convert_fusion.8.refs_1_, ...), custom_call_target="tpu_custom_call" | custom-call | bytes 314572800 | tf_op jit(solution)/shard_map/pallas_call | solution.py:413
  776.1 4.8 all-to-all-start.1
  783.6 3.9 subtract_add_fusion
  787.6 2.7 reshape.262
  792.1 3.0 reshape.263
  799.4 10.1 %all-to-all-done.1 = bf16[4,128,1408]{2,1,0:T(8,128)(2,1)} async-done(((bf16[4,128,1408]{2,1,0:T(8,128)(2,1)}), bf16[4,128,1408]{2,1,0:T(8,128)(2,1)}, u32[]{:S(2)}, u32[]{:S(2)}) %all-to-all-start.1) | async-done | bytes 1441824 | tf_op jit(solution)/shard_map/all_to_all | solution.py:60
  (305 shorter events, 128.8 us)
Async XLA Ops:
  7.2 317.8 %all-gather.6.cloned.1.call-start = ((), (), s32[]{:S(2)}) async-start(), calls=%async_computation.7 | async-start | bytes 7208960 | tf_op jit(solution)/shard_map/all_gather | solution.py:75
  12.1 10.3 %copy-start.68 = (f32[256]{0:T(256)}, f32[256]{0:T(256)S(1)}, u32[]{:S(2)}) copy-start(f32[256]{0:T(256)S(1)} %get-tuple-element.89) | copy-start | bytes 3076
  24.3 182.5 %copy-start.71 = (s32[1,4]{1,0:T(1,128)S(1)}, s32[1,4]{1,0:T(1,128)}, u32[]{:S(2)}) copy-start(s32[1,4]{1,0:T(1,128)} %param.12) | copy-start | bytes 52
  206.7 134.2 %all-gather.8.cloned.1.call-start = ((), (), s32[]{:S(2)}) async-start(), calls=%async_computation.8 | async-start | bytes 7208960 | tf_op jit(solution)/shard_map/all_gather | solution.py:75
  206.8 32.6 %collective-permute-start = (s32[1,4]{1,0:T(1,128)S(1)}, s32[1,4]{1,0:T(1,128)S(1)}, u32[]{:S(2)}, u32[]{:S(2)}) collective-permute-start(s32[1,4]{1,0:T(1,128)S(1)} %copy-done.71), channel_id=1, source_target_pairs={{0,8},{2,10},{4,12},{6,14},{8,0},{10,2},{12,4},{14,6},{16,24},{18,... | collective-permute-start | bytes 56 | tf_op jit(solution)/shard_map/ppermute | solution.py:54
  207.5 201.1 %all-gather.4.cloned.1.call-start = ((), (), s32[]{:S(2)}) async-start(), calls=%async_computation.6 | async-start | bytes 7208960 | tf_op jit(solution)/shard_map/all_gather | solution.py:75
  207.8 10.3 %copy-start.15 = (bf16[1024,2048]{1,0:T(8,128)(2,1)S(1)}, bf16[1024,2048]{1,0:T(8,128)(2,1)}, u32[]{:S(2)}) copy-start(bf16[1024,2048]{1,0:T(8,128)(2,1)} %copy-done.14) | copy-start | bytes 12582916
  207.8 10.3 %copy-start.19 = (bf16[2048,1024]{1,0:T(8,128)(2,1)S(1)}, bf16[2048,1024]{1,0:T(8,128)(2,1)}, u32[]{:S(2)}) copy-start(bf16[2048,1024]{1,0:T(8,128)(2,1)} %copy-done.18) | copy-start | bytes 12582916
  227.7 17.6 %copy-start.38 = (bf16[2,512,4,128]{3,1,2,0:T(8,128)(2,1)}, bf16[2,512,4,128]{3,1,2,0:T(8,128)(2,1)S(1)}, u32[]{:S(2)}) copy-start(bf16[2,512,4,128]{3,1,2,0:T(8,128)(2,1)S(1)} %copy.48) | copy-start | bytes 3145732
  248.1 1.2 collective-permute-start.1
  249.4 4.4 collective-permute-start.2
  262.0 4.8 collective-permute-start.3
  262.6 347.8 %reduce-scatter.8.cloned.1.call-start = ((), (), s32[]{:S(2)}) async-start(), calls=%async_computation.11 | async-start | bytes 7208960 | tf_op jit(solution)/shard_map/reduce_scatter | solution.py:78
  262.6 30.5 %copy-start.28 = (f32[256,2048]{1,0:T(8,128)S(1)}, f32[256,2048]{1,0:T(8,128)}, u32[]{:S(2)}) copy-start(f32[256,2048]{1,0:T(8,128)} %reshape.267) | copy-start | bytes 6291460
  268.6 24.5 %collective-permute-start.4 = (bf16[256,2048]{1,0:T(8,128)(2,1)S(1)}, bf16[256,2048]{1,0:T(8,128)(2,1)S(1)}, u32[]{:S(2)}, u32[]{:S(2)}) collective-permute-start(bf16[256,2048]{1,0:T(8,128)(2,1)S(1)} %add_convert_fusion.6), channel_id=1, source_target_pairs={{0,8},{2,10},{4,12},{6,14},{8,0},{10,2},{12,4},{14,6},{16,24},{18,... | collective-permute-start | bytes 3145736 | tf_op jit(solution)/shard_map/ppermute | solution.py:54
  296.9 23.7 %collective-permute-start.6 = (bf16[256,2048]{1,0:T(8,128)(2,1)S(1)}, bf16[256,2048]{1,0:T(8,128)(2,1)S(1)}, u32[]{:S(2)}, u32[]{:S(2)}) collective-permute-start(bf16[256,2048]{1,0:T(8,128)(2,1)S(1)} %multiply_convert_fusion.6), channel_id=1, source_target_pairs={{0,8},{2,10},{4,12},{6,14},{8,0},{10,2},{12,4},{14,6},{16,24},{18,... | collective-permute-start | bytes 3145736 | tf_op jit(solution)/shard_map/ppermute | solution.py:54
  297.9 24.7 %collective-permute-start.5 = (bf16[256,2048]{1,0:T(8,128)(2,1)S(1)}, bf16[256,2048]{1,0:T(8,128)(2,1)S(1)}, u32[]{:S(2)}, u32[]{:S(2)}) collective-permute-start(bf16[256,2048]{1,0:T(8,128)(2,1)S(1)} %multiply_convert_fusion.6), channel_id=1, source_target_pairs={{0,1},{1,0},{2,3},{3,2},{4,5},{5,4},{6,7},{7,6},{8,9},{9,8},{10,11... | collective-permute-start | bytes 3145736 | tf_op jit(solution)/shard_map/ppermute | solution.py:57
  320.7 4.3 collective-permute-start.7
  408.6 16.3 %copy-start.24 = (bf16[1024,2048]{1,0:T(8,128)(2,1)S(1)}, bf16[1024,2048]{1,0:T(8,128)(2,1)}, u32[]{:S(2)}) copy-start(bf16[1024,2048]{1,0:T(8,128)(2,1)} %copy-done.23) | copy-start | bytes 12582916
  433.5 199.1 %reduce-scatter.4.cloned.1.call-start = ((), (), s32[]{:S(2)}) async-start(), calls=%async_computation.9 | async-start | bytes 7208960 | tf_op jit(solution)/shard_map/reduce_scatter | solution.py:78
  444.8 331.3 %reduce-scatter.6.cloned.1.call-start = ((), (), s32[]{:S(2)}) async-start(), calls=%async_computation.10 | async-start | bytes 7208960 | tf_op jit(solution)/shard_map/reduce_scatter | solution.py:78
  444.9 11.9 %copy-start.76 = (bf16[1024,1408]{1,0:T(8,128)(2,1)S(1)}, bf16[1024,1408]{1,0:T(8,128)(2,1)}, u32[]{:S(2)}) copy-start(bf16[1024,1408]{1,0:T(8,128)(2,1)} %get-tuple-element.48) | copy-start | bytes 8650756
  444.9 24.3 %slice-start = ((s8[5767168]{0:T(1024)(128)(4,1)}), s8[4194304]{0:T(1024)(128)(4,1)S(1)}, s32[]{:S(2)}) async-start(s8[5767168]{0:T(1024)(128)(4,1)} %bitcast.147), calls=%async_computation.12 | async-start | bytes 8388608
  456.7 12.4 %slice-start.1 = ((s8[5767168]{0:T(1024)(128)(4,1)}), s8[1572864]{0:T(1024)(128)(4,1)S(1)}, s32[]{:S(2)}) async-start(s8[5767168]{0:T(1024)(128)(4,1)} %bitcast.147), calls=%async_computation.13 | async-start | bytes 3145728
  468.0 14.0 %copy-start.46 = (bf16[1024,2048]{1,0:T(8,128)(2,1)}, bf16[1024,2048]{1,0:T(8,128)(2,1)S(1)}, u32[]{:S(2)}) copy-start(bf16[1024,2048]{1,0:T(8,128)(2,1)S(1)} %add_convert_fusion.1) | copy-start | bytes 12582916
  468.5 13.5 %collective-permute-start.10 = (bf16[512,2048]{1,0:T(8,128)(2,1)S(1)}, bf16[512,2048]{1,0:T(8,128)(2,1)S(1)}, u32[]{:S(2)}, u32[]{:S(2)}) collective-permute-start(bf16[512,2048]{1,0:T(8,128)(2,1)S(1)} %pad_maximum_fusion.4), channel_id=1, source_target_pairs={{0,1},{1,0},{2,3},{3,2},{4,5},{5,4},{6,7},{7,6},{8,9},{9,8},{10,11... | collective-permute-start | bytes 6291464 | tf_op jit(solution)/shard_map/ppermute | solution.py:57
  481.4 13.0 %collective-permute-start.8 = (bf16[512,2048]{1,0:T(8,128)(2,1)}, bf16[512,2048]{1,0:T(8,128)(2,1)}, u32[]{:S(2)}, u32[]{:S(2)}) collective-permute-start(bf16[512,2048]{1,0:T(8,128)(2,1)} %pad_maximum_fusion.3), channel_id=1, source_target_pairs={{0,1},{1,0},{2,3},{3,2},{4,5},{5,4},{6,7},{7,6},{8,9},{9,8},{10,11... | collective-permute-start | bytes 6291464 | tf_op jit(solution)/shard_map/ppermute | solution.py:57
  483.7 25.1 %collective-permute-start.11 = (bf16[256,2048]{1,0:T(8,128)(2,1)}, bf16[256,2048]{1,0:T(8,128)(2,1)}, u32[]{:S(2)}, u32[]{:S(2)}) collective-permute-start(bf16[256,2048]{1,0:T(8,128)(2,1)} %add_convert_fusion.3), channel_id=1, source_target_pairs={{0,8},{2,10},{4,12},{6,14},{8,0},{10,2},{12,4},{14,6},{16,24},{18,... | collective-permute-start | bytes 3145736 | tf_op jit(solution)/shard_map/ppermute | solution.py:54
  494.4 14.4 %copy-start.53 = (bf16[512,2048]{1,0:T(8,128)(2,1)S(1)}, bf16[512,2048]{1,0:T(8,128)(2,1)}, u32[]{:S(2)}) copy-start(bf16[512,2048]{1,0:T(8,128)(2,1)} %copy-done.52) | copy-start | bytes 6291460
  496.6 14.9 %copy-start.32 = (f32[256,2048]{1,0:T(8,128)S(1)}, f32[256,2048]{1,0:T(8,128)}, u32[]{:S(2)}) copy-start(f32[256,2048]{1,0:T(8,128)} %copy-done.31) | copy-start | bytes 6291460
  496.6 34.7 %collective-permute-start.9 = (bf16[256,2048]{1,0:T(8,128)(2,1)S(1)}, bf16[256,2048]{1,0:T(8,128)(2,1)S(1)}, u32[]{:S(2)}, u32[]{:S(2)}) collective-permute-start(bf16[256,2048]{1,0:T(8,128)(2,1)S(1)} %add_convert_fusion.5), channel_id=1, source_target_pairs={{0,8},{2,10},{4,12},{6,14},{8,0},{10,2},{12,4},{14,6},{16,24},{18,... | collective-permute-start | bytes 3145736 | tf_op jit(solution)/shard_map/ppermute | solution.py:54
  535.9 24.3 %collective-permute-start.13 = (bf16[256,2048]{1,0:T(8,128)(2,1)}, bf16[256,2048]{1,0:T(8,128)(2,1)S(1)}, u32[]{:S(2)}, u32[]{:S(2)}) collective-permute-start(bf16[256,2048]{1,0:T(8,128)(2,1)} %get-tuple-element.42), channel_id=1, source_target_pairs={{0,8},{2,10},{4,12},{6,14},{8,0},{10,2},{12,4},{14,6},{16,24},{18,... | collective-permute-start | bytes 3145736 | tf_op jit(solution)/shard_map/ppermute | solution.py:54
  536.1 25.6 %collective-permute-start.12 = (bf16[256,2048]{1,0:T(8,128)(2,1)}, bf16[256,2048]{1,0:T(8,128)(2,1)}, u32[]{:S(2)}, u32[]{:S(2)}) collective-permute-start(bf16[256,2048]{1,0:T(8,128)(2,1)} %get-tuple-element.42), channel_id=1, source_target_pairs={{0,1},{1,0},{2,3},{3,2},{4,5},{5,4},{6,7},{7,6},{8,9},{9,8},{10,11... | collective-permute-start | bytes 3145736 | tf_op jit(solution)/shard_map/ppermute | solution.py:57
  560.2 3.9 collective-permute-start.14
  566.2 7.7 copy-start.66
  566.2 7.7 copy-start.67
  570.1 1.3 collective-permute-start.15
  571.3 2.5 collective-permute-start.16
  586.2 12.1 %copy-start.62 = (bf16[64,8,2,512]{3,1,2,0:T(8,128)(2,1)}, bf16[64,8,2,512]{3,1,2,0:T(8,128)(2,1)S(1)}, u32[]{:S(2)}) copy-start(bf16[64,8,2,512]{3,1,2,0:T(8,128)(2,1)S(1)} %copy.60) | copy-start | bytes 3145732
  598.3 5.9 copy-start.56
  598.3 5.9 copy-start.58
  610.4 34.8 %all-to-all-start.2 = ((bf16[4,128,1408]{2,1,0:T(8,128)(2,1)}), bf16[4,128,1408]{2,1,0:T(8,128)(2,1)}, u32[]{:S(2)}, u32[]{:S(2)}) async-start(bf16[4,128,1408]{2,1,0:T(8,128)(2,1)} %bitcast.137), calls=%async_computation.5 | async-start | bytes 2883584 | tf_op jit(solution)/shard_map/all_to_all | solution.py:60
  618.3 41.2 %collective-permute-start.17 = (bf16[512,2048]{1,0:T(8,128)(2,1)}, bf16[512,2048]{1,0:T(8,128)(2,1)}, u32[]{:S(2)}, u32[]{:S(2)}) collective-permute-start(bf16[512,2048]{1,0:T(8,128)(2,1)} %pad_maximum_fusion.5), channel_id=1, source_target_pairs={{0,1},{1,0},{2,3},{3,2},{4,5},{5,4},{6,7},{7,6},{8,9},{9,8},{10,11... | collective-permute-start | bytes 6291464 | tf_op jit(solution)/shard_map/ppermute | solution.py:57
  632.7 20.8 %copy-start.57 = (bf16[1024,512]{0,1:T(8,128)(2,1)S(1)}, bf16[1024,512]{0,1:T(8,128)(2,1)}, u32[]{:S(2)}) copy-start(bf16[1024,512]{0,1:T(8,128)(2,1)} %copy-done.56) | copy-start | bytes 3145732
  645.2 130.9 %all-to-all-start = ((bf16[4,128,1408]{2,1,0:T(8,128)(2,1)}), bf16[4,128,1408]{2,1,0:T(8,128)(2,1)}, u32[]{:S(2)}, u32[]{:S(2)}) async-start(bf16[4,128,1408]{2,1,0:T(8,128)(2,1)} %bitcast.136), calls=%async_computation.1 | async-start | bytes 2883584 | tf_op jit(solution)/shard_map/all_to_all | solution.py:60
  653.5 9.3 %copy-start.17 = (bf16[1024,2048]{1,0:T(8,128)(2,1)S(1)}, bf16[1024,2048]{1,0:T(8,128)(2,1)}, u32[]{:S(2)}) copy-start(bf16[1024,2048]{1,0:T(8,128)(2,1)} %copy-done.14) | copy-start | bytes 12582916
  662.5 118.5 %collective-permute-start.18 = (bf16[256,2048]{1,0:T(8,128)(2,1)}, bf16[256,2048]{1,0:T(8,128)(2,1)}, u32[]{:S(2)}, u32[]{:S(2)}) collective-permute-start(bf16[256,2048]{1,0:T(8,128)(2,1)} %add_convert_fusion.2), channel_id=1, source_target_pairs={{0,8},{2,10},{4,12},{6,14},{8,0},{10,2},{12,4},{14,6},{16,24},{18,... | collective-permute-start | bytes 3145736 | tf_op jit(solution)/shard_map/ppermute | solution.py:54
  776.1 33.4 %all-to-all-start.1 = ((bf16[4,128,1408]{2,1,0:T(8,128)(2,1)}), bf16[4,128,1408]{2,1,0:T(8,128)(2,1)}, u32[]{:S(2)}, u32[]{:S(2)}) async-start(bf16[4,128,1408]{2,1,0:T(8,128)(2,1)} %bitcast.138), calls=%async_computation.3 | async-start | bytes 2883584 | tf_op jit(solution)/shard_map/all_to_all | solution.py:60
  (61 other events, 180.9 us)
Sparse Core Ops, SparseCore 0:
  206.8 66.3 all-gather.5
  275.1 65.7 all-gather.7
  342.7 65.7 all-gather.3
  433.7 65.8 reduce-scatter.7
  502.3 65.8 reduce-scatter.3
  571.0 65.8 reduce-scatter.5

commit v3 on v2

--- a/solution.py
+++ b/solution.py
@@ -74,11 +74,13 @@
     def gather(self, lined):
         return lax.all_gather(lined, "wide", axis=0, axis_index_groups=self.planes, tiled=True)
 
-    def reduce(self, grad):
-        lined = lax.psum_scatter(
+    def plane_sum(self, grad):
+        return lax.psum_scatter(
             grad, "wide", scatter_dimension=0, axis_index_groups=self.planes, tiled=True
         )
-        got = self.line(lined.reshape(LINE, -1, grad.shape[1])).astype(F32)
+
+    def line_sum(self, lined):
+        got = self.line(lined.reshape(LINE, -1, lined.shape[1])).astype(F32)
         return jnp.concatenate([got[0] + got[2], got[1] + got[3]], axis=1)
 
     def group_gather(self, value):
@@ -126,72 +128,61 @@
     pl.semaphore_wait(barrier, len(devices))
 
 
-def gather_kernel(wide, chunks, n_in, n_out, *refs):
-    ins, outs = refs[: n_in + 2], refs[n_in + 2 : n_in + n_out + 4]
-    line_send, line_recv, own_sem, plane_send, plane_recv, token_sem, token_send, token_recv = refs[
-        n_in + n_out + 4 :
-    ]
+def forward_kernel(wide, small, large, *refs):
+    (
+        w_in, (normed_own, cot_own, x_own, ends_own),
+        w_out, (normed_out, cot_out, query_pre_out, key_pre_out, gate_out, query_out, key_out, value_out, mixed_out,
+                probs_out, middle_out, mid_out, left_out, right_out, product_out),
+        (normed, wide_w, query_pre, key_pre, gate, query, key, value, mixed, probs, blended, part, part_core, part_far,
+         square, square_core, square_far, ends_far, mid, middle, large_w, left, right, product),
+        (line_send, line_recv, own_sem, plane_send, plane_recv, load_sem, save_sem, token_sem, token_send, token_recv,
+         small_send, small_recv),
+    ) = split_refs(refs, (8, 4, 6, 15, 24, 12))
     me, core, z, on_line, flip = place_of(wide)
     extra = list(range(4, wide.bit_length() - 1))
     plane_at = (me // 16) * 4 + me % 4
     others = [on_line(k)[0] for k in (1, 2, 3)] + [flip(b) for b in [0, 1] + extra]
     meet([(other, core) for other in others] + [(me, 1 - core)])
-    rb = ins[0].shape[0]
-
-    def token_copies(i):
-        source, out = ins[n_in + i], outs[n_out + i]
-        size = source.shape[0]
-
-        def send(j, source, device):
-            return pltpu.make_async_remote_copy(
-                src_ref=source, dst_ref=out.at[pl.ds((j + 1) * size, size)],
-                send_sem=token_send.at[i, j], recv_sem=token_recv.at[i, j],
-                device_id=device, device_id_type=pl.DeviceIdType.MESH,
-            )
-
-        return (
-            pltpu.make_async_copy(source, out.at[pl.ds(0, size)], token_sem.at[i]),
-            send(0, source, (me, 1 - core)),
-            send(1, source, (flip(2), core)),
-            send(2, out.at[pl.ds(2 * size, size)], (me, 1 - core)),
-        )
-
-    def part(i, start, size):
-        source, out, col, _ = chunks[i]
-        width = ins[source].shape[1] // 2
-        return outs[out].at[pl.ds(pl.multiple_of(start, min(size, rb)), size), pl.ds(col, width)]
+    rb = w_in[0].shape[0]
+    q = LINE * rb
+    h = q // 2
+    quarter, features = x_own.shape
+    row_len = 2 * quarter
+    chunks = [(0, 0), (0, small), (1, 0), (1, small), (2, 0), (3, 0), (4, 0), (5, 0)]
+    near_device, far_device = (me, 1 - core), (flip(2), core)
+
+
+    def part_of(i, start, size):
+        out, col = chunks[i]
+        cols = w_in[i].shape[1] // 2
+        return w_out[out].at[pl.ds(pl.multiple_of(start, min(size, rb)), size), pl.ds(col, cols)]
 
     def block(m):
-        return (plane_at ^ m) * (LINE * rb)
+        return (plane_at ^ m) * q
+
+    def remote(source, target, send_sem, recv_sem, device):
+        return pltpu.make_async_remote_copy(
+            src_ref=source, dst_ref=target, send_sem=send_sem, recv_sem=recv_sem,
+            device_id=device, device_id_type=pl.DeviceIdType.MESH,
+        )
 
     def mine(i, there):
-        source = chunks[i][0]
-        width = ins[source].shape[1] // 2
-        return ins[source].at[:, pl.ds(pl.multiple_of((there % 2) * width, HEAD_DIM), width)]
-
-    def landing(i):
-        return part(i, (block(0) if chunks[i][3] else 0) + z * rb, rb)
+        cols = w_in[i].shape[1] // 2
+        return w_in[i].at[:, pl.ds(pl.multiple_of((there % 2) * cols, HEAD_DIM), cols)]
 
     def line_copy(i, k):
         device, there = on_line(k)
-        return pltpu.make_async_remote_copy(
-            src_ref=mine(i, there), dst_ref=landing(i),
-            send_sem=line_send.at[i, k - 1], recv_sem=line_recv.at[i, k - 1],
-            device_id=(device, core), device_id_type=pl.DeviceIdType.MESH,
+        return remote(
+            mine(i, there), part_of(i, block(0) + z * rb, rb),
+            line_send.at[i, k - 1], line_recv.at[i, k - 1], (device, core),
         )
 
     def own_copy(i):
-        return pltpu.make_async_copy(mine(i, z), landing(i), own_sem.at[i])
+        return pltpu.make_async_copy(mine(i, z), part_of(i, block(0) + z * rb, rb), own_sem.at[i])
 
     def plane(i, j, start, size, bit):
-        return pltpu.make_async_remote_copy(
-            src_ref=part(i, start, size), dst_ref=part(i, start, size),
-            send_sem=plane_send.at[i, j], recv_sem=plane_recv.at[i, j],
-            device_id=(flip(bit), core), device_id_type=pl.DeviceIdType.MESH,
-        )
-
-    q = LINE * rb
-    h = q // 2
+        place = part_of(i, start, size)
+        return remote(place, place, plane_send.at[i, j], plane_recv.at[i, j], (flip(bit), core))
 
     def first(i):
         return plane(i, 0, block(0), q, 0), plane(i, 1, block(0), q, 1)
@@ -204,75 +195,375 @@
         for k in (1, 2, 3):
             line_copy(i, k).start()
 
-    count = len(chunks)
-    spread = [c[3] for c in chunks]
-    tokens = [token_copies(0), token_copies(1)]
-    for copy in tokens[0][:3]:
+    def start_plane(i):
+        own_copy(i).wait()
+        for k in (1, 2, 3):
+            line_copy(i, k).wait_recv()
+        for copy in first(i):
+            copy.start()
+
+    def forward_plane(i):
+        for got, onward in zip(first(i), second(i)):
+            got.wait_recv()
+            onward.start()
+
+    def complete(i):
+        for copy in second(i):
+            copy.wait_recv()
+        for e, bit in enumerate(extra):
+            size = q << (2 + e)
+            copy = plane(i, 4 + e, (plane_at >> (2 + e)) * size, size, bit)
+            copy.start()
+            copy.wait()
+
+
+    def rows(b):
+        return pl.ds(b * quarter, quarter)
+
+    def token_copies(n, source, out):
+        send = lambda j, source, device: remote(
+            source, out.at[rows(j + 1)], token_send.at[n, j], token_recv.at[n, j], device
+        )
+        return send(0, source, near_device), send(1, source, far_device), send(2, out.at[rows(2)], near_device)
+
+    def start_tokens(copies):
+        copies[0].start()
+        copies[1].start()
+
+    def pass_tokens(copies):
+        copies[1].wait_recv()
+        copies[2].start()
+
+    def end_tokens(copies):
+        copies[0].wait_recv()
+        copies[2].wait_recv()
+
+    def sent_tokens(copies):
+        for copy in copies:
+            copy.wait_send()
+
+    saves = []
+
+    def save(source, target):
+        copy = pltpu.make_async_copy(source, target, save_sem.at[len(saves)])
         copy.start()
-    for i in range(2):
-        start_line(i)
-    for i in range(count + 1):
-        if i == 2:
-            for copy in tokens[1][:3]:
-                copy.start()
-            tokens[0][2].wait_recv()
-            tokens[0][3].start()
-        if i < count:
-            own_copy(i).wait()
-            for k in (1, 2, 3):
-                line_copy(i, k).wait_recv()
-            if spread[i]:
-                for copy in first(i):
-                    copy.start()
-            if i + 2 < count:
-                start_line(i + 2)
-        if i > 0 and spread[i - 1]:
-            for got, onward in zip(first(i - 1), second(i - 1)):
-                got.wait_recv()
-                onward.start()
-    tokens[1][2].wait_recv()
-    tokens[1][3].start()
-    for own, near, far, onward in tokens:
-        own.wait()
-        near.wait()
-        far.wait_send()
-        onward.wait()
-    for i in range(count):
+        saves.append(copy)
+
+    normed_copies = token_copies(0, normed_own, normed)
+    cot_copies = token_copies(1, cot_own, cot_out)
+    mid_copies = token_copies(2, mid.at[rows(0)], mid)
+    normed_local = pltpu.make_async_copy(normed_own, normed.at[rows(0)], token_sem.at[0])
+    cot_local = pltpu.make_async_copy(cot_own, cot_out.at[rows(0)], token_sem.at[1])
+    ends_copy = remote(ends_own, ends_far, small_send.at[0], small_recv.at[0], far_device)
+
+
+    def load(i, slot):
+        return pltpu.make_async_copy(
+            part_of(i, 0, features), wide_w.at[slot] if i < 5 else large_w, load_sem.at[i]
+        )
+
+    def project(i, slot, keep):
+        copy = load(i, slot)
+        copy.start()
+        copy.wait()
+
+        def body(n, carry):
+            at = pl.ds(pl.multiple_of(n * row_len, row_len), row_len)
+            keep(at, jnp.dot(normed[at], wide_w[slot], preferred_element_type=F32))
+            return carry
+
+        lax.fori_loop(0, 2, body, 0)
+
+    def keep_query(at, total):
+        query_pre[at] = total
+        query[at] = (total * sigmoid(total)).astype(BF16)
+
+    def keep_key(at, total):
+        key_pre[at] = total
+        key[at] = (total * sigmoid(total)).astype(BF16)
+
+    def keep_value(at, total):
+        value[at] = total.astype(BF16)
+
+    def keep_gate(at, total):
+        gate[at] = total
+
+    heads = small // HEAD_DIM
+    first_head = (core * 2 + z % 2) * heads
+
+    def attend(row, ends):
+        at = pl.ds(row * row_len, row_len)
+
+        def place(dim):
+            index = lax.broadcasted_iota(jnp.int32, (row_len, row_len), dim) + core * quarter
+            return jnp.where(index >= row_len, index - row_len, index).astype(F32)
+
+        def body(head, carry):
+            cols = pl.ds(pl.multiple_of(head * HEAD_DIM, HEAD_DIM), HEAD_DIM)
+            scores = lax.dot_general(
+                query[at, cols], key[at, cols], (((1,), (1,)), ((), ())), preferred_element_type=F32
+            )
+            to, source = place(0), place(1)
+            allowed = (to >= source) & (to < ends[0:1, :])
+            rate = (first_head + head).astype(F32) * (DECAY * HEAD_DIM / features)
+            decay = jnp.where(allowed, jnp.exp(-rate * jnp.maximum(to - source, 0.0)), 0.0)
+            weights = (scores * decay).astype(BF16)
+            probs[row, head] = weights
+            mixed[at, cols] = jnp.dot(weights, value[at, cols], preferred_element_type=F32)
+            return carry
+
+        lax.fori_loop(0, heads, body, 0)
+        for b in (2 * row, 2 * row + 1):
+            m = mixed[rows(b)]
+            total = jnp.sum(m * m, axis=1, keepdims=True)
+            square[rows(b)] = jnp.broadcast_to(total, (quarter, HEAD_DIM))
+            blended[rows(b)] = (gate[rows(b)] * m).astype(BF16)
+
+    def output_part(row, slot):
+        at = pl.ds(row * row_len, row_len)
+
+        def body(n, carry):
+            cols = pl.ds(pl.multiple_of(n * row_len, row_len), row_len)
+            part[at, cols] = lax.dot_general(
+                blended[at], wide_w[slot, cols], (((1,), (1,)), ((), ())), preferred_element_type=F32
+            ).astype(BF16)
+            return carry
+
+        lax.fori_loop(0, features // row_len, body, 0)
+
+    tile = 32
+
+    def tiles(body):
+        def step(n, carry):
+            body(pl.multiple_of(n * tile, tile))
+            return carry
+
+        lax.fori_loop(0, quarter // tile, step, 0)
+
+
+    normed_local.start()
+    start_tokens(normed_copies)
+    ends_copy.start()
+    start_line(0)
+    start_line(1)
+    start_plane(0)
+    start_line(2)
+    start_plane(1)
+    start_line(3)
+    pass_tokens(normed_copies)
+    forward_plane(0)
+    start_plane(2)
+    start_line(4)
+    forward_plane(1)
+    normed_local.wait()
+    end_tokens(normed_copies)
+    save(normed, normed_out)
+    complete(0)
+    project(0, 0, keep_query)
+    save(query_pre, query_pre_out)
+    save(query, query_out)
+    start_plane(3)
+    start_line(5)
+    forward_plane(2)
+    complete(1)
+    project(1, 1, keep_key)
+    save(key_pre, key_pre_out)
+    save(key, key_out)
+    start_plane(4)
+    start_line(6)
+    forward_plane(3)
+    complete(2)
+    project(2, 0, keep_value)
+    save(value, value_out)
+    forward_plane(4)
+    complete(3)
+    project(3, 1, keep_gate)
+    save(gate, gate_out)
+    ends_copy.wait()
+    attend(1, ends_far)
+    square_near = remote(
+        square.at[rows(1)], square_core.at[rows(0)], small_send.at[1], small_recv.at[1], near_device
+    )
+    square_diag = remote(
+        square.at[rows(3)], square_core.at[rows(1)], small_send.at[2], small_recv.at[2], near_device
+    )
+    square_pair = remote(square.at[rows(2)], square_far, small_send.at[3], small_recv.at[3], far_device)
+    square_diag.start()
+    start_plane(5)
+    attend(0, ends_own)
+    save(mixed, mixed_out)
+    save(probs, probs_out)
+    square_near.start()
+    square_diag.wait_recv()
+    square[rows(2)] += square_core[rows(1)]
+    square_pair.start()
+    complete(4)
+    copy = load(4, 0)
+    copy.start()
+    copy.wait()
+    output_part(1, 0)
+    part_near = remote(part.at[rows(1)], part_core.at[rows(0)], small_send.at[4], small_recv.at[4], near_device)
+    part_diag = remote(part.at[rows(3)], part_core.at[rows(1)], small_send.at[5], small_recv.at[5], near_device)
+    part_pair = remote(part.at[rows(2)], part_far, small_send.at[6], small_recv.at[6], far_device)
+    part_diag.start()
+    part_diag.wait_recv()
+
+    @tiles
+    def _(start):
+        here = pl.ds(start + 2 * quarter, tile)
+        part[here] = (part[here].astype(F32) + part_core[pl.ds(start + quarter, tile)].astype(F32)).astype(BF16)
+
+    part_pair.start()
+    output_part(0, 0)
+    part_near.start()
+    forward_plane(5)
+    start_plane(6)
+    square_near.wait_recv()
+    square_pair.wait_recv()
+    part_near.wait_recv()
+    part_pair.wait_recv()
+
+    @tiles
+    def _(start):
+        here = pl.ds(start, tile)
+        total = part[here].astype(F32) + part_core[here].astype(F32) + part_far[here].astype(F32)
+        squares = square[here, 0:1] + square_core[here, 0:1] + square_far[here, 0:1]
+        total = x_own[here].astype(F32) + total * lax.rsqrt(squares / features + EPS)
+        middle[here] = total
+        mid[here] = (total * lax.rsqrt(jnp.mean(total * total, axis=1, keepdims=True) + EPS)).astype(BF16)
+
+    start_tokens(mid_copies)
+    save(middle, middle_out)
+    complete(5)
+    copy = load(5, 0)
+    copy.start()
+    copy.wait()
+    mid_copies[0].wait_recv()
+
+    def left_rows(row):
+        at = pl.ds(row * row_len, row_len)
+        left[at] = jnp.dot(mid[at], large_w[...], preferred_element_type=F32).astype(BF16)
+
+    left_rows(0)
+    pass_tokens(mid_copies)
+    start_line(7)
+    cot_local.start()
+    start_tokens(cot_copies)
+    forward_plane(6)
+    mid_copies[2].wait_recv()
+    left_rows(1)
+    save(mid, mid_out)
+    save(left, left_out)
+    complete(6)
+    copy = load(6, 0)
+    copy.start()
+    copy.wait()
+
+    def right_rows(n, carry):
+        at = pl.ds(pl.multiple_of(n * row_len, row_len), row_len)
+        total = jnp.dot(mid[at], large_w[...], preferred_element_type=F32)
+        right[at] = total.astype(BF16)
+        product[at] = (left[at].astype(F32) * total).astype(BF16)
+        return carry
+
+    start_plane(7)
+    lax.fori_loop(0, 2, right_rows, 0)
+    save(right, right_out)
+    save(product, product_out)
+    pass_tokens(cot_copies)
+    forward_plane(7)
+    complete(7)
+    cot_local.wait()
+    end_tokens(cot_copies)
+    for copies in (normed_copies, cot_copies, mid_copies):
+        sent_tokens(copies)
+    for copy in (square_near, square_diag, square_pair, part_near, part_diag, part_pair):
+        copy.wait_send()
+    for i in range(8):
         for k in (1, 2, 3):
             line_copy(i, k).wait_send()
-        if spread[i]:
-            for copy in first(i):
-                copy.wait_send()
-            for copy in second(i):
-                copy.wait()
-    for e, bit in enumerate(extra):
-        size = q << (2 + e)
-        start = (plane_at >> (2 + e)) * size
-        copies = [plane(i, 4 + e, start, size, bit) for i in range(count) if spread[i]]
-        for copy in copies:
-            copy.start()
-        for copy in copies:
-            copy.wait()
-
-
-def gather_weights(wide, weights, chunks, outs, tokens):
-    count = len(chunks)
+        for copy in first(i) + second(i):
+            copy.wait_send()
+    for copy in saves:
+        copy.wait()
+
+
+def split_refs(refs, counts):
+    parts, at = [], 0
+    for count in counts:
+        parts.append(refs[at : at + count])
+        at += count
+    return parts
+
+
+def forward(wide, weights, normed, cot, x, ends):
+    small, large = weights[0].shape[1] // 2, weights[5].shape[1] // 2
+    quarter, features = x.shape
+    tokens, row_len, heads = 4 * quarter, 2 * quarter, small // HEAD_DIM
     steps = wide.bit_length() - 1
-    anywhere = pl.BlockSpec(memory_space=pl.ANY)
+    anywhere, vmem = pl.BlockSpec(memory_space=pl.ANY), pl.BlockSpec(memory_space=pltpu.VMEM)
     dma = pltpu.SemaphoreType.DMA
+    outs = [
+        ((features, 2 * small), BF16),
+        ((features, 2 * small), BF16),
+        ((features, small), BF16),
+        ((features, large), BF16),
+        ((features, large), BF16),
+        ((features, large), BF16),
+        ((tokens, features), BF16),
+        ((tokens, features), BF16),
+        ((tokens, small), F32),
+        ((tokens, small), F32),
+        ((tokens, small), F32),
+        ((tokens, small), BF16),
+        ((tokens, small), BF16),
+        ((tokens, small), BF16),
+        ((tokens, small), F32),
+        ((2, heads, row_len, row_len), BF16),
+        ((quarter, features), F32),
+        ((tokens, features), BF16),
+        ((tokens, large), BF16),
+        ((tokens, large), BF16),
+        ((tokens, large), BF16),
+    ]
+    held = [
+        ((tokens, features), BF16),
+        ((2, features, small), BF16),
+        ((tokens, small), F32),
+        ((tokens, small), F32),
+        ((tokens, small), F32),
+        ((tokens, small), BF16),
+        ((tokens, small), BF16),
+        ((tokens, small), BF16),
+        ((tokens, small), F32),
+        ((2, heads, row_len, row_len), BF16),
+        ((tokens, small), BF16),
+        ((tokens, features), BF16),
+        ((row_len, features), BF16),
+        ((quarter, features), BF16),
+        ((tokens, HEAD_DIM), F32),
+        ((row_len, HEAD_DIM), F32),
+        ((quarter, HEAD_DIM), F32),
+        (ends.shape, F32),
+        ((tokens, features), BF16),
+        ((quarter, features), F32),
+        ((features, large), BF16),
+        ((tokens, large), BF16),
+        ((tokens, large), BF16),
+        ((tokens, large), BF16),
+    ]
+    sems = [(8, 3), (8, 3), (8,), (8, steps), (8, steps), (8,), (14,), (2,), (3, 3), (3, 3), (7,), (7,)]
     return pl.pallas_call(
-        functools.partial(gather_kernel, wide, chunks, len(weights), len(outs)),
-        out_shape=[jax.ShapeDtypeStruct(o, BF16) for o in outs]
-        + [jax.ShapeDtypeStruct((4 * t.shape[0], t.shape[1]), BF16) for t in tokens],
-        in_specs=[anywhere] * (len(weights) + 2),
-        out_specs=[anywhere] * (len(outs) + 2),
-        scratch_shapes=[dma((count, 3)), dma((count, 3)), dma((count,)), dma((count, steps)), dma((count, steps))]
-        + [dma((2,)), dma((2, 3)), dma((2, 3))],
+        functools.partial(forward_kernel, wide, small, large),
+        out_shape=[jax.ShapeDtypeStruct(s, t) for s, t in outs],
+        in_specs=[anywhere] * 10 + [vmem] * 2,
+        out_specs=[anywhere] * len(outs),
+        scratch_shapes=[pltpu.VMEM(s, t) for s, t in held] + [dma(s) for s in sems],
         compiler_params=pltpu.CompilerParams(
-            has_side_effects=True, collective_id=1, vmem_limit_bytes=1 << 20
+            has_side_effects=True, collective_id=1, vmem_limit_bytes=60 << 20
         ),
         cost_estimate=pl.CostEstimate(flops=0, bytes_accessed=300 << 20, transcendentals=0),
-    )(*weights, *tokens)
+    )(*weights, normed, cot, x, ends)
 
 
 def reduce_kernel(wide, count, *refs):
@@ -450,6 +741,14 @@
     return jnp.where(allowed[:, None], weights[None], 0.0)
 
 
+def ends_of(lengths, places):
+    total, ends = 0, 0
+    for c in range(lengths.shape[1]):
+        ends = ends + jnp.where(places >= total, lengths[0, c], 0)
+        total = total + lengths[0, c]
+    return jnp.broadcast_to(ends.astype(F32)[None], (8, places.shape[0]))
+
+
 def sigmoid(z):
     return 1.0 / (1.0 + jnp.exp(-z))
 
@@ -462,65 +761,50 @@
     half = (net.me >> 2) & 1
     features = layer_input.shape[1]
 
-    inputs = net.permute(layer_input).astype(F32)
+    x = net.permute(layer_input)
+    inputs = x.astype(F32)
     norm_one = norm_scale_of(inputs)
     cot = net.permute(cotangent)
-    rows, small, large = features, w_query.shape[1] // 2, w_left.shape[1] // 2
-    qk_w, vg_w, output_w, left_lined, right_lined, down_lined, normed, cot_all = gather_weights(
-        wide,
-        [w_query, w_key, w_value, w_gate, w_output, w_left, w_right, w_down],
-        [(0, 0, 0, 1), (1, 0, small, 1), (2, 1, 0, 1), (3, 1, small, 1), (4, 2, 0, 1), (5, 3, 0, 0), (6, 4, 0, 0), (7, 5, 0, 0)],
-        [(rows, 2 * small), (rows, 2 * small), (rows, small), *[(LINE * w_left.shape[0], large)] * 3],
-        [(inputs * norm_one).astype(BF16), cot],
-    )
-    left_w = net.gather(left_lined)
-    right_w = net.gather(right_lined)
-    down_w = net.gather(down_lined)
-
     quarter = inputs.shape[0]
     tokens = 4 * quarter
     row_len = 2 * quarter
+    own = jnp.arange(quarter, dtype=jnp.int32)
+    places = jnp.concatenate([own + core * quarter, own + (1 - core) * quarter])
+    (
+        qk_w, vg_w, output_w, left_w, right_w, down_w, normed, cot_all, query_pre, key_pre, gate, queries, keys, values,
+        mixed, probs, middle, mid, left, right, product,
+    ) = forward(
+        wide,
+        [w_query, w_key, w_value, w_gate, w_output, w_left, w_right, w_down],
+        (inputs * norm_one).astype(BF16),
+        cot,
+        x,
+        ends_of(doc_lengths, places),
+    )
+
     width = output_w.shape[1]
     heads = width // HEAD_DIM
     all_heads = features // HEAD_DIM
     head_ids = (core * 2 + half) * heads + jnp.arange(heads, dtype=jnp.int32)
     rates = DECAY * head_ids.astype(F32) / all_heads
-    own = jnp.arange(quarter, dtype=jnp.int32)
-    places = jnp.concatenate([own + core * quarter, own + (1 - core) * quarter])
     lengths = jnp.concatenate([doc_lengths, net.flip(doc_lengths, 2)])
     decay = masks(lengths, places, rates)
-
-    qk_pre = mm(normed, qk_w)
-    query_pre, key_pre = qk_pre[:, :width], qk_pre[:, width:]
-    vg = mm(normed, vg_w)
-    values, gate = vg[:, :width].astype(BF16), vg[:, width:]
     query_sig, key_sig = sigmoid(query_pre), sigmoid(key_pre)
-    queries = (query_pre * query_sig).astype(BF16)
-    keys = (key_pre * key_sig).astype(BF16)
     shape = (2, row_len, heads, HEAD_DIM)
     q4, k4, v4 = (a.reshape(shape) for a in (queries, keys, values))
-    scores = jnp.einsum("rihd,rjhd->rhij", q4, k4, preferred_element_type=F32)
-    probs = (scores * decay).astype(BF16)
-    mixed = jnp.einsum("rhij,rjhd->rihd", probs, v4, preferred_element_type=F32)
-    mixed = mixed.reshape(tokens, width)
     squares = net.group_sum(jnp.sum(mixed * mixed, axis=1))
     attn_scale = lax.rsqrt(squares / features + EPS)[:, None]
     scaled = mixed * attn_scale
     blended = (gate * scaled).astype(BF16)
-    middle = inputs + net.group_scatter(mm_t(blended, output_w, BF16))
     norm_two = norm_scale_of(middle)
-    mid = net.group_gather((middle * norm_two).astype(BF16))
-    left = mm(mid, left_w)
-    right = mm(mid, right_w)
-    product = (left * right).astype(BF16)
     grad_down = t_mm(cot_all, product, BF16)
     output_part = mm_t(product, down_w, BF16)
     layer_output = middle + net.group_scatter(output_part)
     layer_output = net.restore(layer_output.astype(BF16))
 
     grad_product = mm(cot_all, down_w)
-    grad_left_pre = (grad_product * right).astype(BF16)
-    grad_right_pre = (grad_product * left).astype(BF16)
+    grad_left_pre = (grad_product * right.astype(F32)).astype(BF16)
+    grad_right_pre = (grad_product * left.astype(F32)).astype(BF16)
     grad_mid = net.group_scatter(
         (mm_t(grad_left_pre, left_w) + mm_t(grad_right_pre, right_w)).astype(BF16)
     )
@@ -530,7 +814,8 @@
     grad_middle = cot.astype(F32) + norm_back(middle, norm_two, grad_mid)
     branch = net.group_gather(grad_middle.astype(BF16))
     branch = after(branch, output_part, grad_down)
-    grad_left, grad_right, grad_down = (net.reduce(g) for g in (grad_left, grad_right, grad_down))
+    grad_down, grad_left, grad_right = (net.plane_sum(g) for g in (grad_down, grad_left, grad_right))
+    grad_down = net.line_sum(after(grad_down, branch))
     grad_blended = mm(branch, output_w)
     grad_output = t_mm(branch, blended, BF16)
     grad_gate_pre = (grad_blended * scaled).astype(BF16)
@@ -548,6 +833,8 @@
     grad_scores = (grad_probs * decay).astype(BF16)
     grad_queries = jnp.einsum("rhij,rjhd->rihd", grad_scores, k4, preferred_element_type=F32)
     grad_keys = jnp.einsum("rhij,rihd->rjhd", grad_scores, q4, preferred_element_type=F32)
+    grad_queries, grad_keys = (after(g, grad_down) for g in (grad_queries, grad_keys))
+    grad_left = net.line_sum(after(grad_left, grad_queries))
     grad_query_pre = (
         grad_queries.reshape(tokens, width) * (query_sig * (1.0 + query_pre * (1.0 - query_sig)))
     ).astype(BF16)
@@ -556,6 +843,8 @@
     ).astype(BF16)
     grad_query = t_mm(normed, grad_query_pre, BF16)
     grad_key = t_mm(normed, grad_key_pre, BF16)
+    grad_key = after(grad_key, grad_left)
+    grad_right = net.line_sum(after(grad_right, grad_left))
     grad_output, grad_gate, grad_value, grad_query, grad_key = reduce_weights(
         wide, [grad_output, grad_gate, grad_value, grad_query, grad_key]
     )

time: 838 us -> 750 us (0.89)
  waiting for transfers between devices: 193 us -> 87.5 us
  Pallas kernels: 276 us -> 381 us
  matrix products: 171 us -> 126 us
  local copies, waits for them, and re-layouts: 75.2 us -> 50.4 us
  other arithmetic: 61.8 us -> 48.8 us
    pallas_call x1, Pallas kernels: 173 us -> 278 us  [forward(): pl.pallas_call(functools.partial(forward_kernel, wide, small, large), out...]
    all_gather x3 -> x0, waiting for transfers between devices: 58.9 us -> none  [gather(): lax.all_gather(lined, 'wide', axis=0, axis_index_groups=self.planes, tile...]
    ppermute x9 -> x7, waiting for transfers between devices: 101 us -> 55.4 us  [flip(): lax.ppermute(value, 'wide', [(w, w ^ 1 << bit) for w in range(self.wide)])]
    dot_general x6 -> x2, matrix products: 59.5 us -> 14.9 us  [mm(): lax.dot_general(a, b, (((1,), (0,)), ((), ())), preferred_element_type=F32)]
    unnamed x176 -> x118, local copies, waits for them, and re-layouts: 32.4 us -> 21.3 us
    ppermute x10 -> x7, waiting for transfers between devices: 9.63 us -> 0.63 us  [core(): return lax.ppermute(value, 'narrow', [(0, 1), (1, 0)])]
    all_to_all x3, waiting for transfers between devices: 22.7 us -> 31.4 us  [line(): lax.all_to_all(value, 'wide', 0, 0, axis_index_groups=self.lines, tiled=T...]
    dot_general x6 -> x5, matrix products: 43.4 us -> 48.7 us  [mm_t(): lax.dot_general(a, b, (((1,), (1,)), ((), ())), preferred_element_type=F32)]
  transfers between devices with their start and end apart: 28 -> 20, of which waited for: 15 -> 8; matrix products, arithmetic and copies ran while one was open for 28% -> 24% of each run, Pallas kernels for 12% -> 14%
where the time goes in v3:
time: 750 us; the launch traced here: 739 us
  Pallas kernels  381 us (51%)
  matrix products  126 us (17%)
  waiting for transfers between devices  87.5 us (12%)
  local copies, waits for them, and re-layouts  50.4 us (7%)
  other arithmetic  48.8 us (7%)
  starting transfers between devices  28.6 us (4%)
  between operations  16.9 us (2%)
    pallas_call x1, Pallas kernels, forward(): pl.pallas_call(functools.partial(forward_kernel, wide, small, large), out...  278 us
    pallas_call x1, Pallas kernels, reduce_weights(): pl.pallas_call(functools.partial(reduce_kernel, wide, count), out_shape=[...  104 us
    ppermute x7, waiting for transfers between devices, flip(): lax.ppermute(value, 'wide', [(w, w ^ 1 << bit) for w in range(self.wide)])  55.4 us
    dot_general x8, matrix products, t_mm(): lax.dot_general(a, b, (((0,), (0,)), ((), ())), preferred_element_type=F32)  51 us
    dot_general x5, matrix products, mm_t(): lax.dot_general(a, b, (((1,), (1,)), ((), ())), preferred_element_type=F32)  48.7 us
    all_to_all x3, waiting for transfers between devices, line(): lax.all_to_all(value, 'wide', 0, 0, axis_index_groups=self.lines, tiled=T...  31.4 us
    unnamed x118, local copies, waits for them, and re-layouts  21.3 us
    all_to_all x3, starting transfers between devices, line(): lax.all_to_all(value, 'wide', 0, 0, axis_index_groups=self.lines, tiled=T...  18.2 us
  transfers between devices with their start and end apart: 20, of which 8 were waited for; matrix products, arithmetic and copies ran while one was open for 24% of the time, Pallas kernels for 14%

profile of v3, /device:TPU:25, one launch (start us, length us, event | category | flops | bytes accessed | tf_op | source)
XLA Modules:
  0.0 739.0 jit_solution(8710229685760781923)
XLA Ops:
  19.8 2.6 pad_add_fusion
  23.0 277.7 %shard_map.186 = (bf16[2048,1024]{1,0:T(8,128)(2,1)}, bf16[2048,1024]{1,0:T(8,128)(2,1)}, bf16[2048,512]{1,0:T(8,128)(2,1)}, bf16[2048,1408]{1,0:T(8,128)(2,1)},...) custom-call(bf16[128,1024]{1,0:T(8,128)(2,1)} %refs_0_.1, ...), custom_call_target="tpu_custom_call" | custom-call | bytes 314572800 | tf_op jit(solution)/shard_map/pallas_call | solution.py:556
  300.7 11.1 %convolution_convert_fusion = bf16[2048,1408]{1,0:T(8,128)(2,1)} fusion(bf16[1024,2048]{1,0:T(8,128)(2,1)} %get-tuple-element.47, bf16[1024,1408]{1,0:T(8,128)(2,1)} %get-tuple-element.45), kind=kOutput, calls=%fused_computation.3 | convolution fusion | flops 5908463616 | bytes 12845056 | tf_op jit(solution)/shard_map/dot_general | solution.py:27
  311.9 11.2 %fusion.45 = f32[1024,1408]{1,0:T(8,128)S(1)} fusion(bf16[1024,2048]{1,0:T(8,128)(2,1)} %get-tuple-element.47, bf16[2048,1408]{1,0:T(8,128)(2,1)} %get-tuple-element.46), kind=kOutput, calls=%fused_computation.125 | convolution fusion | flops 5905580032 | bytes 15728640 | tf_op jit(solution)/shard_map/dot_general | solution.py:19
  323.1 2.5 copy-done.49
  325.6 8.8 %convolution_convert_fusion.2 = bf16[2048,1408]{1,0:T(8,128)(2,1)} fusion(bf16[1024,2048]{1,0:T(8,128)(2,1)S(1)} %copy-done.43, f32[1024,1408]{1,0:T(8,128)S(1)} %fusion.45, bf16[1024,1408]{1,0:T(8,128)(2,1)S(1)} %copy-done.47), kind=kOutput, calls=%fused_computation.5 | convolution fusion | flops 5912788992 | bytes 18612224 | tf_op jit(solution)/shard_map/dot_general | solution.py:27
  334.5 13.6 %fusion.35 = f32[1024,2048]{1,0:T(8,128)} fusion(bf16[2048,1408]{1,0:T(8,128)(2,1)} %get-tuple-element.49, f32[1024,1408]{1,0:T(8,128)} %copy-done.49, bf16[1024,1408]{1,0:T(8,128)(2,1)} %get-tuple-element.48), kind=kOutput, calls=%fused_computation.115 | convolution fusion | flops 5909905408 | bytes 22806528 | tf_op jit(solution)/shard_map/dot_general | solution.py:23
  348.1 11.8 %add_convert_fusion.1 = bf16[1024,2048]{1,0:T(8,128)(2,1)S(1)} fusion(f32[1024,2048]{1,0:T(8,128)} %fusion.35, bf16[2048,1408]{1,0:T(8,128)(2,1)S(1)} %bitcast.115, f32[1024,1408]{1,0:T(8,128)} %copy-done.49, bf16[1024,1408]{1,0:T(8,128)(2,1)} %get-tuple-element.50), kind=kOutput, calls=%fused_computation.2 | convolution fusion | flops 5914099712 | bytes 27000832 | tf_op jit(solution)/shard_map/dot_general | solution.py:23
  360.9 2.3 copy-done.46
  363.2 9.4 %convolution_convert_fusion.3 = bf16[1024,2048]{1,0:T(8,128)(2,1)S(1)} fusion(bf16[1024,1408]{1,0:T(8,128)(2,1)S(1)} %copy-done.46, bf16[2048,1408]{1,0:T(8,128)(2,1)} %get-tuple-element.46), kind=kOutput, calls=%fused_computation.10 | convolution fusion | flops 5907677184 | bytes 12845056 | tf_op jit(solution)/shard_map/dot_general | solution.py:23
  379.2 9.0 %convolution_convert_fusion.1 = bf16[2048,1408]{1,0:T(8,128)(2,1)} fusion(bf16[1024,2048]{1,0:T(8,128)(2,1)S(1)} %copy-done.44, f32[1024,1408]{1,0:T(8,128)S(1)} %bitcast.117, bf16[1024,1408]{1,0:T(8,128)(2,1)S(1)} %copy-done.45), kind=kOutput, calls=%fused_computation.4 | convolution fusion | flops 5912788992 | bytes 18612224 | tf_op jit(solution)/shard_map/dot_general | solution.py:27
  388.2 2.1 add_convert_fusion.5
  390.7 12.3 %collective-permute-done.3 = bf16[256,2048]{1,0:T(8,128)(2,1)S(1)} collective-permute-done((bf16[256,2048]{1,0:T(8,128)(2,1)}, bf16[256,2048]{1,0:T(8,128)(2,1)S(1)}, u32[]{:S(2)}, u32[]{:S(2)}) %collective-permute-start.3) | collective-permute-done | bytes 1048608 | tf_op jit(solution)/shard_map/ppermute | solution.py:54
  405.2 20.2 %collective-permute-done.1 = bf16[256,2048]{1,0:T(8,128)(2,1)S(1)} collective-permute-done((bf16[256,2048]{1,0:T(8,128)(2,1)S(1)}, bf16[256,2048]{1,0:T(8,128)(2,1)S(1)}, u32[]{:S(2)}, u32[]{:S(2)}) %collective-permute-start.1) | collective-permute-done | bytes 1048608 | tf_op jit(solution)/shard_map/ppermute | solution.py:54
  425.4 4.2 fusion.36
  432.8 20.8 %collective-permute-done.7 = bf16[256,2048]{1,0:T(8,128)(2,1)} collective-permute-done((bf16[256,2048]{1,0:T(8,128)(2,1)S(1)}, bf16[256,2048]{1,0:T(8,128)(2,1)}, u32[]{:S(2)}, u32[]{:S(2)}) %collective-permute-start.7) | collective-permute-done | bytes 1048608 | tf_op jit(solution)/shard_map/ppermute | solution.py:54
  455.6 2.5 reshape.295
  458.1 2.2 reshape.298
  461.4 2.6 multiply_exponential_fusion
  464.4 2.2 pad_maximum_fusion
  467.5 2.2 copy-done.48
  469.7 3.7 multiply_reduce_fusion
  479.0 4.0 subtract_convert_fusion
  483.3 3.0 fusion.14
  488.4 4.9 all-to-all-start
  493.3 4.3 multiply_convert_fusion
  498.9 2.9 convolution_bitcast_fusion.1
  502.5 6.9 fusion.7
  509.4 14.6 %all-to-all-done = bf16[4,128,1408]{2,1,0:T(8,128)(2,1)S(1)} async-done(((bf16[4,128,1408]{2,1,0:T(8,128)(2,1)}), bf16[4,128,1408]{2,1,0:T(8,128)(2,1)S(1)}, u32[]{:S(2)}, u32[]{:S(2)}) %all-to-all-start) | async-done | bytes 1441824 | tf_op jit(solution)/shard_map/all_to_all | solution.py:60
  527.4 2.0 copy.46
  529.5 3.1 fusion.5
  533.6 2.0 copy-done.41
  535.5 7.0 add_convert_fusion
  546.2 2.3 collective-permute-start.12
  551.5 6.6 all-to-all-start.1
  558.1 6.1 convolution_convert_fusion.7.refs_1_
  564.2 3.8 convolution_convert_fusion.6.refs_2_
  567.9 2.5 convolution_convert_fusion.8.refs_0_
  570.4 2.9 add_convert_fusion.2
  573.6 16.8 %all-to-all-done.1 = bf16[4,128,1408]{2,1,0:T(8,128)(2,1)} async-done(((bf16[4,128,1408]{2,1,0:T(8,128)(2,1)}), bf16[4,128,1408]{2,1,0:T(8,128)(2,1)}, u32[]{:S(2)}, u32[]{:S(2)}) %all-to-all-start.1) | async-done | bytes 1441824 | tf_op jit(solution)/shard_map/all_to_all | solution.py:60
  593.3 6.7 all-to-all-start.2
  600.1 6.1 convolution_convert_fusion.5.refs_3_
  606.2 3.8 convolution_convert_fusion.4.refs_4_
  610.0 103.7 %shard_map.187 = (f32[128,1024]{1,0:T(8,128)S(1)}, f32[128,1024]{1,0:T(8,128)S(1)}, f32[128,1024]{1,0:T(8,128)S(1)}, f32[128,1024]{1,0:T(8,128)S(1)}, f32[128,1024]{1,0:T(8,128)S(1)}) custom-call(bf16[2048,512]{1,0:T(8,128)(2,1)S(1)} %convolution_convert_fusion.8.refs_0_, bf16[2048,512]{1,0:T(8,128)(2,1)} %convolution_convert_fusion.7.refs_1_, ...), custom_call_target="tpu_custom_call" | custom-call | bytes 314572800 | tf_op jit(solution)/shard_map/pallas_call | solution.py:704
  713.8 2.7 fusion.4
  716.6 2.3 fusion.3
  718.9 2.4 reshape.300
  721.3 2.1 copy.49
  (214 shorter events, 61.7 us)
Async XLA Ops:
  7.2 481.2 %reduce-scatter.4.cloned.1.call-start = ((), (), s32[]{:S(2)}) async-start(), calls=%async_computation.6 | async-start | bytes 7208960 | tf_op jit(solution)/shard_map/reduce_scatter | solution.py:78
  11.5 5.2 copy-start.6
  12.1 4.6 copy-start.36
  311.8 239.7 %reduce-scatter.6.cloned.1.call-start = ((), (), s32[]{:S(2)}) async-start(), calls=%async_computation.7 | async-start | bytes 7208960 | tf_op jit(solution)/shard_map/reduce_scatter | solution.py:78
  311.8 13.8 %copy-start.43 = (bf16[1024,2048]{1,0:T(8,128)(2,1)S(1)}, bf16[1024,2048]{1,0:T(8,128)(2,1)}, u32[]{:S(2)}) copy-start(bf16[1024,2048]{1,0:T(8,128)(2,1)} %get-tuple-element.52) | copy-start | bytes 12582916
  311.8 13.8 %copy-start.47 = (bf16[1024,1408]{1,0:T(8,128)(2,1)S(1)}, bf16[1024,1408]{1,0:T(8,128)(2,1)}, u32[]{:S(2)}) copy-start(bf16[1024,1408]{1,0:T(8,128)(2,1)} %get-tuple-element.48) | copy-start | bytes 8650756
  334.4 13.7 %slice-start = ((s8[5767168]{0:T(1024)(128)(4,1)}), s8[1572864]{0:T(1024)(128)(4,1)S(1)}, s32[]{:S(2)}) async-start(s8[5767168]{0:T(1024)(128)(4,1)} %bitcast.114), calls=%async_computation.9 | async-start | bytes 3145728
  334.4 258.9 %reduce-scatter.8.cloned.1.call-start = ((), (), s32[]{:S(2)}) async-start(), calls=%async_computation.8 | async-start | bytes 7208960 | tf_op jit(solution)/shard_map/reduce_scatter | solution.py:78
  334.5 13.6 %slice-start.1 = ((s8[5767168]{0:T(1024)(128)(4,1)}), s8[4194304]{0:T(1024)(128)(4,1)S(1)}, s32[]{:S(2)}) async-start(s8[5767168]{0:T(1024)(128)(4,1)} %bitcast.114), calls=%async_computation.10 | async-start | bytes 8388608
  359.9 16.8 %copy-start.13 = (bf16[1024,2048]{1,0:T(8,128)(2,1)}, bf16[1024,2048]{1,0:T(8,128)(2,1)S(1)}, u32[]{:S(2)}) copy-start(bf16[1024,2048]{1,0:T(8,128)(2,1)S(1)} %add_convert_fusion.1) | copy-start | bytes 12582916
  360.1 17.9 %slice-start.2 = ((s8[5767168]{0:T(1024)(128)(4,1)}), s8[4194304]{0:T(1024)(128)(4,1)S(1)}, s32[]{:S(2)}) async-start(s8[5767168]{0:T(1024)(128)(4,1)} %bitcast.116), calls=%async_computation.11 | async-start | bytes 8388608
  360.4 17.7 %slice-start.3 = ((s8[5767168]{0:T(1024)(128)(4,1)}), s8[1572864]{0:T(1024)(128)(4,1)S(1)}, s32[]{:S(2)}) async-start(s8[5767168]{0:T(1024)(128)(4,1)} %bitcast.116), calls=%async_computation.12 | async-start | bytes 3145728
  360.4 16.3 %collective-permute-start.2 = (bf16[512,2048]{1,0:T(8,128)(2,1)S(1)}, bf16[512,2048]{1,0:T(8,128)(2,1)S(1)}, u32[]{:S(2)}, u32[]{:S(2)}) collective-permute-start(bf16[512,2048]{1,0:T(8,128)(2,1)S(1)} %pad_maximum_fusion.2), channel_id=1, source_target_pairs={{0,1},{1,0},{2,3},{3,2},{4,5},{5,4},{6,7},{7,6},{8,9},{9,8},{10,11... | collective-permute-start | bytes 6291464 | tf_op jit(solution)/shard_map/ppermute | solution.py:57
  376.2 12.0 %collective-permute-start = (bf16[512,2048]{1,0:T(8,128)(2,1)}, bf16[512,2048]{1,0:T(8,128)(2,1)}, u32[]{:S(2)}, u32[]{:S(2)}) collective-permute-start(bf16[512,2048]{1,0:T(8,128)(2,1)} %pad_maximum_fusion.1), channel_id=1, source_target_pairs={{0,1},{1,0},{2,3},{3,2},{4,5},{5,4},{6,7},{7,6},{8,9},{9,8},{10,11... | collective-permute-start | bytes 6291464 | tf_op jit(solution)/shard_map/ppermute | solution.py:57
  378.0 25.0 %collective-permute-start.3 = (bf16[256,2048]{1,0:T(8,128)(2,1)}, bf16[256,2048]{1,0:T(8,128)(2,1)S(1)}, u32[]{:S(2)}, u32[]{:S(2)}) collective-permute-start(bf16[256,2048]{1,0:T(8,128)(2,1)} %add_convert_fusion.3), channel_id=1, source_target_pairs={{0,8},{2,10},{4,12},{6,14},{8,0},{10,2},{12,4},{14,6},{16,24},{18,... | collective-permute-start | bytes 3145736 | tf_op jit(solution)/shard_map/ppermute | solution.py:54
  390.3 14.5 %copy-start.10 = (f32[256,2048]{1,0:T(8,128)S(1)}, f32[256,2048]{1,0:T(8,128)}, u32[]{:S(2)}) copy-start(f32[256,2048]{1,0:T(8,128)} %get-tuple-element.44) | copy-start | bytes 6291460
  390.3 35.1 %collective-permute-start.1 = (bf16[256,2048]{1,0:T(8,128)(2,1)S(1)}, bf16[256,2048]{1,0:T(8,128)(2,1)S(1)}, u32[]{:S(2)}, u32[]{:S(2)}) collective-permute-start(bf16[256,2048]{1,0:T(8,128)(2,1)S(1)} %add_convert_fusion.5), channel_id=1, source_target_pairs={{0,8},{2,10},{4,12},{6,14},{8,0},{10,2},{12,4},{14,6},{16,24},{18,... | collective-permute-start | bytes 3145736 | tf_op jit(solution)/shard_map/ppermute | solution.py:54
  404.8 20.6 %copy-start.8 = (bf16[256,2048]{1,0:T(8,128)(2,1)S(1)}, bf16[256,2048]{1,0:T(8,128)(2,1)}, u32[]{:S(2)}) copy-start(bf16[256,2048]{1,0:T(8,128)(2,1)} %reshape.287.refs_9_) | copy-start | bytes 3145732
  429.6 23.9 %collective-permute-start.7 = (bf16[256,2048]{1,0:T(8,128)(2,1)S(1)}, bf16[256,2048]{1,0:T(8,128)(2,1)}, u32[]{:S(2)}, u32[]{:S(2)}) collective-permute-start(bf16[256,2048]{1,0:T(8,128)(2,1)S(1)} %get-tuple-element.86), channel_id=1, source_target_pairs={{0,8},{2,10},{4,12},{6,14},{8,0},{10,2},{12,4},{14,6},{16,24},{18,... | collective-permute-start | bytes 3145736 | tf_op jit(solution)/shard_map/ppermute | solution.py:54
  429.8 34.2 %collective-permute-start.11 = (s32[1,4]{1,0:T(1,128)S(1)}, s32[1,4]{1,0:T(1,128)S(1)}, u32[]{:S(2)}, u32[]{:S(2)}) collective-permute-start(s32[1,4]{1,0:T(1,128)S(1)} %copy-done.35), channel_id=1, source_target_pairs={{0,8},{2,10},{4,12},{6,14},{8,0},{10,2},{12,4},{14,6},{16,24},{18,... | collective-permute-start | bytes 56 | tf_op jit(solution)/shard_map/ppermute | solution.py:54
  431.3 33.0 %collective-permute-start.6 = (bf16[256,2048]{1,0:T(8,128)(2,1)S(1)}, bf16[256,2048]{1,0:T(8,128)(2,1)}, u32[]{:S(2)}, u32[]{:S(2)}) collective-permute-start(bf16[256,2048]{1,0:T(8,128)(2,1)S(1)} %get-tuple-element.86), channel_id=1, source_target_pairs={{0,1},{1,0},{2,3},{3,2},{4,5},{5,4},{6,7},{7,6},{8,9},{9,8},{10,11... | collective-permute-start | bytes 3145736 | tf_op jit(solution)/shard_map/ppermute | solution.py:57
  453.6 10.8 %collective-permute-start.8 = (bf16[256,2048]{1,0:T(8,128)(2,1)}, bf16[256,2048]{1,0:T(8,128)(2,1)}, u32[]{:S(2)}, u32[]{:S(2)}) collective-permute-start(bf16[256,2048]{1,0:T(8,128)(2,1)} %collective-permute-done.7), channel_id=1, source_target_pairs={{0,1},{1,0},{2,3},{3,2},{4,5},{5,4},{6,7},{7,6},{8,9},{9,8},{10,11... | collective-permute-start | bytes 3145736 | tf_op jit(solution)/shard_map/ppermute | solution.py:57
  455.6 4.7 copy-start.33
  464.3 5.4 copy-start.48
  466.6 6.8 copy-start.16
  473.4 1.8 collective-permute-start.9
  474.7 1.3 collective-permute-start.4
  475.2 2.9 collective-permute-start.10
  476.0 2.9 collective-permute-start.5
  488.4 35.6 %all-to-all-start = ((bf16[4,128,1408]{2,1,0:T(8,128)(2,1)}), bf16[4,128,1408]{2,1,0:T(8,128)(2,1)S(1)}, u32[]{:S(2)}, u32[]{:S(2)}) async-start(bf16[4,128,1408]{2,1,0:T(8,128)(2,1)} %bitcast.108), calls=%async_computation.1 | async-start | bytes 2883584 | tf_op jit(solution)/shard_map/all_to_all | solution.py:60
  493.3 4.4 copy-start.14
  533.4 9.2 %copy-start.31 = (bf16[1024,512]{1,0:T(8,128)(2,1)}, bf16[1024,512]{1,0:T(8,128)(2,1)S(1)}, u32[]{:S(2)}) copy-start(bf16[1024,512]{1,0:T(8,128)(2,1)S(1)} %fusion.6) | copy-start | bytes 3145732
  544.6 4.0 copy-start.21
  546.2 24.2 %collective-permute-start.12 = (bf16[512,2048]{1,0:T(8,128)(2,1)}, bf16[512,2048]{1,0:T(8,128)(2,1)}, u32[]{:S(2)}, u32[]{:S(2)}) collective-permute-start(bf16[512,2048]{1,0:T(8,128)(2,1)} %pad_maximum_fusion.3), channel_id=1, source_target_pairs={{0,1},{1,0},{2,3},{3,2},{4,5},{5,4},{6,7},{7,6},{8,9},{9,8},{10,11... | collective-permute-start | bytes 6291464 | tf_op jit(solution)/shard_map/ppermute | solution.py:57
  549.8 8.2 %copy-start.28 = (bf16[1024,512]{1,0:T(8,128)(2,1)S(1)}, bf16[1024,512]{1,0:T(8,128)(2,1)}, u32[]{:S(2)}) copy-start(bf16[1024,512]{1,0:T(8,128)(2,1)} %get-tuple-element.89) | copy-start | bytes 3145732
  551.5 38.9 %all-to-all-start.1 = ((bf16[4,128,1408]{2,1,0:T(8,128)(2,1)}), bf16[4,128,1408]{2,1,0:T(8,128)(2,1)}, u32[]{:S(2)}, u32[]{:S(2)}) async-start(bf16[4,128,1408]{2,1,0:T(8,128)(2,1)} %bitcast.106), calls=%async_computation.3 | async-start | bytes 2883584 | tf_op jit(solution)/shard_map/all_to_all | solution.py:60
  558.1 6.1 copy-start.19
  558.1 6.1 copy-start.39
  564.2 3.8 copy-start.17
  564.2 3.8 copy-start.23
  564.2 3.8 copy-start.25
  573.3 140.4 %collective-permute-start.13 = (bf16[256,2048]{1,0:T(8,128)(2,1)}, bf16[256,2048]{1,0:T(8,128)(2,1)}, u32[]{:S(2)}, u32[]{:S(2)}) collective-permute-start(bf16[256,2048]{1,0:T(8,128)(2,1)} %add_convert_fusion.2), channel_id=1, source_target_pairs={{0,8},{2,10},{4,12},{6,14},{8,0},{10,2},{12,4},{14,6},{16,24},{18,... | collective-permute-start | bytes 3145736 | tf_op jit(solution)/shard_map/ppermute | solution.py:54
  593.3 6.8 copy-start.32
  593.3 132.0 %all-to-all-start.2 = ((bf16[4,128,1408]{2,1,0:T(8,128)(2,1)}), bf16[4,128,1408]{2,1,0:T(8,128)(2,1)}, u32[]{:S(2)}, u32[]{:S(2)}) async-start(bf16[4,128,1408]{2,1,0:T(8,128)(2,1)} %bitcast.107), calls=%async_computation.5 | async-start | bytes 2883584 | tf_op jit(solution)/shard_map/all_to_all | solution.py:60
  600.1 6.1 copy-start.30
  600.1 6.1 copy-start.40
  610.0 103.8 %copy-start.7 = (bf16[256,2048]{1,0:T(8,128)(2,1)S(1)}, bf16[256,2048]{1,0:T(8,128)(2,1)}, u32[]{:S(2)}) copy-start(bf16[256,2048]{1,0:T(8,128)(2,1)} %copy-done.6) | copy-start | bytes 3145732
  610.0 103.8 %copy-start.12 = (bf16[1024,2048]{1,0:T(8,128)(2,1)S(1)}, bf16[1024,2048]{1,0:T(8,128)(2,1)}, u32[]{:S(2)}) copy-start(bf16[1024,2048]{1,0:T(8,128)(2,1)} %copy-done.11) | copy-start | bytes 12582916
  (26 other events, 66.0 us)
Sparse Core Ops, SparseCore 0:
  311.9 65.6 reduce-scatter.3
  380.5 65.8 reduce-scatter.5
  449.4 65.8 reduce-scatter.7

commit v4 on v3

--- a/solution.py
+++ b/solution.py
@@ -275,18 +275,18 @@
         lax.fori_loop(0, 2, body, 0)
 
     def keep_query(at, total):
-        query_pre[at] = total
+        query_pre[at] = total.astype(BF16)
         query[at] = (total * sigmoid(total)).astype(BF16)
 
     def keep_key(at, total):
-        key_pre[at] = total
+        key_pre[at] = total.astype(BF16)
         key[at] = (total * sigmoid(total)).astype(BF16)
 
     def keep_value(at, total):
         value[at] = total.astype(BF16)
 
     def keep_gate(at, total):
-        gate[at] = total
+        gate[at] = total.astype(BF16)
 
     heads = small // HEAD_DIM
     first_head = (core * 2 + z % 2) * heads
@@ -309,15 +309,15 @@
             decay = jnp.where(allowed, jnp.exp(-rate * jnp.maximum(to - source, 0.0)), 0.0)
             weights = (scores * decay).astype(BF16)
             probs[row, head] = weights
-            mixed[at, cols] = jnp.dot(weights, value[at, cols], preferred_element_type=F32)
+            mixed[at, cols] = jnp.dot(weights, value[at, cols], preferred_element_type=F32).astype(BF16)
             return carry
 
         lax.fori_loop(0, heads, body, 0)
         for b in (2 * row, 2 * row + 1):
-            m = mixed[rows(b)]
+            m = mixed[rows(b)].astype(F32)
             total = jnp.sum(m * m, axis=1, keepdims=True)
             square[rows(b)] = jnp.broadcast_to(total, (quarter, HEAD_DIM))
-            blended[rows(b)] = (gate[rows(b)] * m).astype(BF16)
+            blended[rows(b)] = (gate[rows(b)].astype(F32) * m).astype(BF16)
 
     def output_part(row, slot):
         at = pl.ds(row * row_len, row_len)
@@ -512,13 +512,13 @@
         ((features, large), BF16),
         ((tokens, features), BF16),
         ((tokens, features), BF16),
-        ((tokens, small), F32),
-        ((tokens, small), F32),
-        ((tokens, small), F32),
-        ((tokens, small), BF16),
-        ((tokens, small), BF16),
-        ((tokens, small), BF16),
-        ((tokens, small), F32),
+        ((tokens, small), BF16),
+        ((tokens, small), BF16),
+        ((tokens, small), BF16),
+        ((tokens, small), BF16),
+        ((tokens, small), BF16),
+        ((tokens, small), BF16),
+        ((tokens, small), BF16),
         ((2, heads, row_len, row_len), BF16),
         ((quarter, features), F32),
         ((tokens, features), BF16),
@@ -529,13 +529,13 @@
     held = [
         ((tokens, features), BF16),
         ((2, features, small), BF16),
-        ((tokens, small), F32),
-        ((tokens, small), F32),
-        ((tokens, small), F32),
-        ((tokens, small), BF16),
-        ((tokens, small), BF16),
-        ((tokens, small), BF16),
-        ((tokens, small), F32),
+        ((tokens, small), BF16),
+        ((tokens, small), BF16),
+        ((tokens, small), BF16),
+        ((tokens, small), BF16),
+        ((tokens, small), BF16),
+        ((tokens, small), BF16),
+        ((tokens, small), BF16),
         ((2, heads, row_len, row_len), BF16),
         ((tokens, small), BF16),
         ((tokens, features), BF16),
@@ -566,179 +566,503 @@
     )(*weights, normed, cot, x, ends)
 
 
-def reduce_kernel(wide, count, *refs):
-    grads, outs = refs[:count], refs[count : 2 * count]
-    held, near, far, line, more, load_sem, send, recv, line_send, line_recv, more_send, more_recv = refs[2 * count :]
+def backward_kernel(wide, small, large, *refs):
+    (
+        (branch_in, normed_in, gate_in, mixed_in, query_pre_in, key_pre_in, query_in, key_in, value_in, probs_in,
+         blended_in, output_w, vg_w, qk_w, right_in, left_in, down_in, scale, ends),
+        (output_out, gate_out, value_out, query_out, key_out, right_out, left_out, down_out, normed_grad_out,
+         big_near, big_far, big_line),
+        (branch, normed, weights, gate, mixed, query_pre, key_pre, query, key, value, grad_blended, grad_mixed, blended,
+         vg_grad, qk_grad, inner, inner_core, inner_sum, inner_far, inner_col, part_core, part_far, held, near, far,
+         line, stage, added, small_result, big_result),
+        (load_sem, send, recv, line_send, line_recv, big_send, big_recv, big_line_send, big_line_recv, small_send,
+         small_recv, stage_sem, result_sem, more_send, more_recv),
+    ) = split_refs(refs, (19, 12, 30, 15))
     me, core, z, on_line, flip = place_of(wide)
     extra = list(range(4, wide.bit_length() - 1))
     plane_at = (me // 16) * 4 + me % 4
     others = [on_line(k)[0] for k in (1, 2, 3)] + [flip(b) for b in [0, 1] + extra]
-    rows, cols = grads[0].shape
-    rb = rows // wide
+    tokens, features = branch.shape
+    quarter, row_len = tokens // 4, tokens // 2
+    rb = features // wide
     q = LINE * rb
     h = q // 2
-
-    def rows_at(i, start, size):
-        return held.at[i, pl.ds(pl.multiple_of(start, min(size, h)), size)]
-
-    def block(m):
-        return (plane_at ^ m) * q
+    heads = small // HEAD_DIM
+    near_device, far_device = (me, 1 - core), (flip(2), core)
+    lower = z % 2 == 0
 
     def remote(source, target, send_sem, recv_sem, device):
         return pltpu.make_async_remote_copy(
             src_ref=source, dst_ref=target, send_sem=send_sem, recv_sem=recv_sem,
-            device_id=(device, core), device_id_type=pl.DeviceIdType.MESH,
-        )
+            device_id=device, device_id_type=pl.DeviceIdType.MESH,
+        )
+
+    def block(m):
+        return pl.multiple_of((plane_at ^ m) * q, q)
+
+    def rows(b):
+        return pl.ds(b * quarter, quarter)
+
+    def loops(count, body):
+        def step(n, carry):
+            body(n)
+            return carry
+
+        lax.fori_loop(0, count, step, 0)
+
+    pending = {}
+
+    def load(name, source, target):
+        copy = pltpu.make_async_copy(source, target, load_sem.at[len(pending)])
+        copy.start()
+        pending[name] = copy
+
+    def ready(*names):
+        for name in names:
+            pending[name].wait()
+
+    results = []
+
+    def give(source, target):
+        copy = pltpu.make_async_copy(source, target, result_sem.at[len(results)])
+        copy.start()
+        results.append(copy)
+        return len(results) - 1
+
+    def given(n):
+        if results[n] is not None:
+            results[n].wait()
+            results[n] = None
+
+    load("branch", branch_in, branch)
+    for n in range(4):
+        load("output%d" % n, output_w.at[pl.ds(n * row_len, row_len)], weights.at[n, :, pl.ds(0, small)])
+    load("gate", gate_in, gate)
+    load("mixed", mixed_in, mixed)
+    load("blended", blended_in, blended)
+    load("normed", normed_in, normed)
+    load("value", value_in, value)
+    load("query", query_in, query)
+    load("key", key_in, key)
+    for r in range(2):
+        for n in range(heads):
+            load("probs%d%d" % (r, n), probs_in.at[r, n], held.at[3 + r, pl.ds(n * row_len, row_len)])
+    load("query_pre", query_pre_in, query_pre)
+    load("key_pre", key_pre_in, key_pre)
+    meet([(other, core) for other in others] + [(me, 1 - core)])
+
+
+    def rows_at(i, start, size):
+        return held.at[i, pl.ds(pl.multiple_of(start, min(size, h)), size)]
 
     def step(i, j, start, size, target, bit):
-        return remote(rows_at(i, start, size), target, send.at[i, j], recv.at[i, j], flip(bit))
-
-    def copies(i):
-        return (
-            step(i, 0, block(3), h, near.at[i, 0], 1),
-            step(i, 1, block(3) + h, h, near.at[i, 1], 0),
-            step(i, 2, block(1) + h, h, far.at[i, 0, pl.ds(h, h)], 0),
-            step(i, 3, block(2), h, far.at[i, 1, pl.ds(0, h)], 1),
-            step(i, 4, block(1), h, far.at[i, 0, pl.ds(0, h)], 0),
-            step(i, 5, block(2) + h, h, far.at[i, 1, pl.ds(h, h)], 1),
-        )
+        return remote(rows_at(i, start, size), target, send.at[i, j], recv.at[i, j], (flip(bit), core))
+
+    def copies(i, j):
+        if j == 0:
+            return step(i, 0, block(3), h, near.at[i, 0], 1)
+        if j == 1:
+            return step(i, 1, block(3) + h, h, near.at[i, 1], 0)
+        if j == 2:
+            return step(i, 2, block(1) + h, h, far.at[i, 0, pl.ds(h, h)], 0)
+        if j == 3:
+            return step(i, 3, block(2), h, far.at[i, 1, pl.ds(0, h)], 1)
+        if j == 4:
+            return step(i, 4, block(1), h, far.at[i, 0, pl.ds(0, h)], 0)
+        return step(i, 5, block(2) + h, h, far.at[i, 1, pl.ds(h, h)], 1)
 
     def line_copy(i, k):
         device, there = on_line(k)
         return remote(
             rows_at(i, block(0) + there * rb, rb), line.at[i, k - 1],
-            line_send.at[i, k - 1], line_recv.at[i, k - 1], device,
-        )
-
-    def load(i):
-        return pltpu.make_async_copy(grads[i], held.at[i], load_sem.at[i])
-
-    def add(i, start, size, *sources):
-        tile = min(64, size)
-
-        def body(n, carry):
+            line_send.at[i, k - 1], line_recv.at[i, k - 1], (device, core),
+        )
+
+    tile = min(64, h)
+
+    def add(target, start, size, *sources):
+        def body(n):
             at = pl.ds(pl.multiple_of(start + n * tile, tile), tile)
-            total = held[i, at].astype(F32)
+            total = target[at].astype(F32)
             for source in sources:
-                total = total + source[pl.ds(n * tile, tile)].astype(F32)
-            held[i, at] = total.astype(BF16)
-            return carry
-
-        lax.fori_loop(0, size // tile, body, 0)
-
-    for i in range(count):
-        load(i).start()
-    meet([(other, core) for other in others])
-
-    def begin(i):
-        load(i).wait()
-        for e in reversed(range(len(extra))):
-            size = q << (2 + e)
-            half = plane_at >> (2 + e)
-            copy = remote(
-                rows_at(i, (half ^ 1) * size, size), more.at[i, e, pl.ds(0, size)],
-                more_send.at[i, e], more_recv.at[i, e], flip(extra[e]),
-            )
-            copy.start()
-            copy.wait()
-            add(i, half * size, size, more.at[i, e])
-        for copy in copies(i)[:4]:
-            copy.start()
+                total = total + source[pl.ds(pl.multiple_of(n * tile, tile), tile)].astype(F32)
+            target[at] = total.astype(BF16)
+
+        loops(size // tile, body)
+
+    def begin(i, side, other):
+        def fill(m):
+            held[i, pl.ds(block(m), q)] = lax.dot_general(
+                side[:, pl.ds(block(m), q)], other(), (((0,), (0,)), ((), ())), preferred_element_type=F32
+            ).astype(BF16)
+
+        if extra:
+            loops(wide // LINE, fill)
+            for e in reversed(range(len(extra))):
+                size = q << (2 + e)
+                half = plane_at >> (2 + e)
+                copy = remote(
+                    rows_at(i, (half ^ 1) * size, size), branch_more(i, e, size),
+                    more_send.at[i, e], more_recv.at[i, e], (flip(extra[e]), core),
+                )
+                copy.start()
+                copy.wait()
+                add(held.at[i], half * size, size, branch_more(i, e, size))
+            for j in range(4):
+                copies(i, j).start()
+        else:
+            fill(3)
+            copies(i, 0).start()
+            copies(i, 1).start()
+            fill(1)
+            copies(i, 2).start()
+            fill(2)
+            copies(i, 3).start()
+            fill(0)
+
+    def branch_more(i, e, size):
+        return far.at[i, e, pl.ds(0, size)]
 
     def fold(i):
-        c = copies(i)
-        c[0].wait_recv()
-        add(i, block(1), h, near.at[i, 0])
-        c[4].start()
-        c[1].wait_recv()
-        add(i, block(2) + h, h, near.at[i, 1])
-        c[5].start()
+        copies(i, 0).wait_recv()
+        add(held.at[i], block(1), h, near.at[i, 0])
+        copies(i, 4).start()
+        copies(i, 1).wait_recv()
+        add(held.at[i], block(2) + h, h, near.at[i, 1])
+        copies(i, 5).start()
 
     def to_line(i):
-        for copy in copies(i)[2:]:
-            copy.wait_recv()
-        add(i, block(0), q, far.at[i, 0], far.at[i, 1])
+        for j in range(2, 6):
+            copies(i, j).wait_recv()
+        add(held.at[i], block(0), q, far.at[i, 0], far.at[i, 1])
         for k in (1, 2, 3):
             line_copy(i, k).start()
 
-    def finish(i):
+    def finish(i, out):
         for k in (1, 2, 3):
             line_copy(i, k).wait_recv()
-        own = held[i, pl.ds(pl.multiple_of(block(0) + z * rb, rb), rb)].astype(F32) + line[i, 1].astype(F32)
+        own = held[i, pl.ds(block(0) + pl.multiple_of(z * rb, rb), rb)].astype(F32) + line[i, 1].astype(F32)
         other = line[i, 0].astype(F32) + line[i, 2].astype(F32)
-        lower = z % 2 == 0
-
+        put(small_result.at[i % 2], own, other, small)
+        return give(small_result.at[i % 2], out)
+
+    def put(target, own, other, cols):
         @pl.when(lower)
         def _():
-            outs[i][:, pl.ds(0, cols)] = own
-            outs[i][:, pl.ds(cols, cols)] = other
+            target[:, pl.ds(0, cols)] = own
+            target[:, pl.ds(cols, cols)] = other
 
         @pl.when(jnp.logical_not(lower))
         def _():
-            outs[i][:, pl.ds(0, cols)] = other
-            outs[i][:, pl.ds(cols, cols)] = own
-
-    for n in range(count + 3):
-        if n < count:
-            begin(n)
-        if 0 <= n - 1 < count:
-            fold(n - 1)
-        if 0 <= n - 2 < count:
-            to_line(n - 2)
-        if 0 <= n - 3 < count:
-            finish(n - 3)
-    for i in range(count):
-        for copy in copies(i):
-            copy.wait_send()
+            target[:, pl.ds(0, cols)] = other
+            target[:, pl.ds(cols, cols)] = own
+
+
+    stage_count = [0]
+
+    def stage_in(source, target):
+        copy = pltpu.make_async_copy(source, target, stage_sem.at[stage_count[0]])
+        stage_count[0] += 1
+        copy.start()
+        return copy
+
+    def big_rows(start, size):
+        return right_in.at[pl.ds(pl.multiple_of(start, min(size, h)), size)]
+
+    def big_copy(j):
+        sources = (
+            lambda: big_rows(block(3), h), lambda: big_rows(block(3) + h, h), lambda: big_rows(block(1) + h, h),
+            lambda: big_rows(block(2), h), lambda: stage.at[pl.ds(0, h)], lambda: stage.at[pl.ds(h, h)],
+        )
+        targets = (
+            lambda: big_near.at[0], lambda: big_near.at[1], lambda: big_far.at[0, pl.ds(h, h)],
+            lambda: big_far.at[1, pl.ds(0, h)], lambda: big_far.at[0, pl.ds(0, h)], lambda: big_far.at[1, pl.ds(h, h)],
+        )
+        bit = (1, 0, 0, 1, 0, 1)[j]
+        return remote(sources[j](), targets[j](), big_send.at[j], big_recv.at[j], (flip(bit), core))
+
+    def big_begin():
+        for j in range(4):
+            big_copy(j).start()
+
+    def big_fold():
+        for n, (m, start) in enumerate(((1, 0), (2, h))):
+            here = pl.ds(n * h, h)
+            first = stage_in(big_rows(block(m) + start, h), stage.at[here])
+            big_copy(n).wait_recv()
+            second = stage_in(big_near.at[n], added.at[here])
+            first.wait()
+            second.wait()
+            add(stage, n * h, h, added.at[here])
+            big_copy(4 + n).start()
+
+    def big_to_line():
+        for j in range(2, 6):
+            big_copy(j).wait_recv()
+        for j in (4, 5):
+            big_copy(j).wait_send()
+        stage_in(big_rows(block(0), q), stage).wait()
+        for n in range(2):
+            a = stage_in(big_far.at[0, pl.ds(n * h, h)], added.at[pl.ds(0, h)])
+            b = stage_in(big_far.at[1, pl.ds(n * h, h)], added.at[pl.ds(h, h)])
+            a.wait()
+            b.wait()
+            add(stage, n * h, h, added.at[pl.ds(0, h)], added.at[pl.ds(h, h)])
+        for k in (1, 2, 3):
+            big_line_copy(0, k).start()
+
+    def big_line_copy(n, k):
+        device, there = on_line(k)
+        source = (stage, left_in, down_in)[n]
+        return remote(
+            source.at[pl.ds(pl.multiple_of(there * rb, rb), rb)], big_line.at[n, k - 1],
+            big_line_send.at[n, k - 1], big_line_recv.at[n, k - 1], (device, core),
+        )
+
+    def big_finish(n, out):
+        for k in (1, 2, 3):
+            big_line_copy(n, k).wait_recv()
+        source = (stage, left_in, down_in)[n]
+        moves = [stage_in(big_line.at[n, k], added.at[pl.ds(k * rb, rb)]) for k in range(3)]
+        moves.append(stage_in(source.at[pl.ds(pl.multiple_of(z * rb, rb), rb)], added.at[pl.ds(3 * rb, rb)]))
+        for move in moves:
+            move.wait()
+        for n_big in results_of_big:
+            given(n_big)
+        got = [added[pl.ds(k * rb, rb)].astype(F32) for k in range(4)]
+        put(big_result, got[3] + got[1], got[0] + got[2], large)
+        results_of_big.append(give(big_result, out))
+
+    results_of_big = []
+
+
+    def grad_rows(row):
+        at = pl.ds(row * row_len, row_len)
+        total = jnp.zeros((row_len, small), F32)
+        for n in range(4):
+            total = total + jnp.dot(
+                branch[at, pl.ds(n * row_len, row_len)], weights[n, :, pl.ds(0, small)], preferred_element_type=F32
+            )
+        grad_blended[at] = total
+        m = mixed[at].astype(F32)
+        vg_grad[at, pl.ds(small, small)] = (total * (m * scale[at, 0:1])).astype(BF16)
+        inner[:, at] = lax.dot_general(
+            jnp.ones((8, small), F32), total * gate[at].astype(F32) * m, (((1,), (1,)), ((), ())),
+            preferred_element_type=F32, precision=lax.Precision.HIGHEST,
+        )
+
+    def mix_rows(n):
+        at = pl.ds(pl.multiple_of(n * 128, 128), 128)
+        s = scale[at, 0:1]
+        value_of = s * (grad_blended[at] * gate[at].astype(F32))
+        value_of = value_of - mixed[at].astype(F32) * (s * s * s * (inner_col[at, 0:1] / features))
+        grad_mixed[at] = value_of.astype(BF16)
+
+    first_head = (core * 2 + z % 2) * heads
+
+    def attend_back(row):
+        at = pl.ds(row * row_len, row_len)
+
+        def place(dim):
+            index = lax.broadcasted_iota(jnp.int32, (row_len, row_len), dim) + core * quarter
+            return jnp.where(index >= row_len, index - row_len, index).astype(F32)
+
+        def slope(pre):
+            s = sigmoid(pre)
+            return s * (1.0 + pre * (1.0 - s))
+
+        def body(head):
+            cols = pl.ds(pl.multiple_of(head * HEAD_DIM, HEAD_DIM), HEAD_DIM)
+            more = pl.ds(pl.multiple_of(small + head * HEAD_DIM, HEAD_DIM), HEAD_DIM)
+            got = grad_mixed[at, cols]
+            grad_probs = lax.dot_general(
+                got, value[at, cols], (((1,), (1,)), ((), ())), preferred_element_type=F32
+            )
+            to, source = place(0), place(1)
+            allowed = (to >= source) & (to < ends[pl.ds(8 * row, 1), :])
+            rate = (first_head + head).astype(F32) * (DECAY * HEAD_DIM / features)
+            decay = jnp.where(allowed, jnp.exp(-rate * jnp.maximum(to - source, 0.0)), 0.0)
+            grad_scores = (grad_probs * decay).astype(BF16)
+            probs = held[3 + row, pl.ds(pl.multiple_of(head * row_len, row_len), row_len)]
+            vg_grad[at, cols] = lax.dot_general(
+                probs, got, (((0,), (0,)), ((), ())), preferred_element_type=F32
+            ).astype(BF16)
+            grad_query = jnp.dot(grad_scores, key[at, cols], preferred_element_type=F32)
+            qk_grad[at, cols] = (grad_query * slope(query_pre[at, cols].astype(F32))).astype(BF16)
+            grad_key = lax.dot_general(
+                grad_scores, query[at, cols], (((0,), (0,)), ((), ())), preferred_element_type=F32
+            )
+            qk_grad[at, more] = (grad_key * slope(key_pre[at, cols].astype(F32))).astype(BF16)
+
+        loops(heads, body)
+
+    def load_weights(pair):
+        for n in range(2):
+            here = pl.ds((2 * pair + n) * row_len, row_len)
+            load("vg%d%d" % (pair, n), vg_w.at[here], weights.at[n])
+            load("qk%d%d" % (pair, n), qk_w.at[here], weights.at[2 + n])
+
+    def normed_part(pair, row):
+        at = pl.ds(row * row_len, row_len)
+        for n in range(2):
+            total = lax.dot_general(vg_grad[at], weights[n], (((1,), (1,)), ((), ())), preferred_element_type=F32)
+            total = total + lax.dot_general(
+                qk_grad[at], weights[2 + n], (((1,), (1,)), ((), ())), preferred_element_type=F32
+            )
+            branch[at, pl.ds((2 * pair + n) * row_len, row_len)] = total.astype(BF16)
+
+
+    big_begin()
+    ready("branch", "output0", "output1", "output2", "output3", "gate", "mixed")
+    grad_rows(1)
+    grad_rows(0)
+    core_copy = remote(inner, inner_core, small_send.at[0], small_recv.at[0], near_device)
+    core_copy.start()
+    ready("blended")
+    core_copy.wait_recv()
+    for b in range(4):
+        inner_sum[:, rows(b)] = inner[:, rows(b)] + inner_core[:, rows(b ^ 1)]
+    far_copy = remote(inner_sum, inner_far, small_send.at[1], small_recv.at[1], far_device)
+    far_copy.start()
+    begin(0, branch, lambda: blended[...])
+    far_copy.wait_recv()
+    for b in range(4):
+        total = inner_sum[:, rows(b)] + inner_far[:, rows(b ^ 2)]
+        inner_col[rows(b)] = jnp.broadcast_to(total.T[:, 0:1], (quarter, HEAD_DIM))
+    for n in (2, 1):
+        for k in (1, 2, 3):
+            big_line_copy(n, k).start()
+    loops(tokens // 128, mix_rows)
+    load_weights(0)
+    ready("normed")
+    begin(1, normed, lambda: vg_grad[:, pl.ds(small, small)])
+    ready("value", "query", "key", "query_pre", "key_pre")
+    for r in range(2):
+        ready(*("probs%d%d" % (r, n) for n in range(heads)))
+    attend_back(1)
+    big_fold()
+    fold(0)
+    attend_back(0)
+    begin(2, normed, lambda: vg_grad[:, pl.ds(0, small)])
+    fold(1)
+    begin(3, normed, lambda: qk_grad[:, pl.ds(0, small)])
+    begin(4, normed, lambda: qk_grad[:, pl.ds(small, small)])
+    big_to_line()
+    to_line(0)
+    fold(2)
+    ready("vg00", "vg01", "qk00", "qk01")
+    normed_part(0, 1)
+    normed_part(0, 0)
+    load_weights(1)
+    to_line(1)
+    ready("vg10", "vg11", "qk10", "qk11")
+    normed_part(1, 1)
+    part_near = remote(branch.at[rows(1)], part_core.at[rows(0)], small_send.at[2], small_recv.at[2], near_device)
+    part_diag = remote(branch.at[rows(3)], part_core.at[rows(1)], small_send.at[3], small_recv.at[3], near_device)
+    part_pair = remote(branch.at[rows(2)], part_far, small_send.at[4], small_recv.at[4], far_device)
+    part_diag.start()
+    normed_part(1, 0)
+    part_near.start()
+    part_diag.wait_recv()
+    add(branch, 2 * quarter, quarter, part_core.at[rows(1)])
+    part_pair.start()
+    fold(3)
+    fold(4)
+    to_line(2)
+    big_finish(2, down_out)
+    big_finish(1, left_out)
+    first = finish(0, output_out)
+    second = finish(1, gate_out)
+    to_line(3)
+    big_finish(0, right_out)
+    given(first)
+    first = finish(2, value_out)
+    to_line(4)
+    part_near.wait_recv()
+    part_pair.wait_recv()
+    add(part_far, 0, quarter, branch.at[rows(0)], part_core.at[rows(0)])
+    give(part_far, normed_grad_out)
+    given(second)
+    finish(3, query_out)
+    given(first)
+    finish(4, key_out)
+    for copy in (core_copy, far_copy, part_near, part_diag, part_pair):
+        copy.wait_send()
+    for i in range(5):
+        for j in range(6):
+            copies(i, j).wait_send()
         for k in (1, 2, 3):
             line_copy(i, k).wait_send()
-
-
-def reduce_weights(wide, grads):
-    count = len(grads)
-    rows, cols = grads[0].shape
-    rb = rows // wide
+    for j in range(4):
+        big_copy(j).wait_send()
+    for n in range(3):
+        for k in (1, 2, 3):
+            big_line_copy(n, k).wait_send()
+    for n in range(len(results)):
+        given(n)
+
+
+def backward(wide, arrays, small, large):
+    tokens, features = arrays[0].shape
+    quarter, row_len = tokens // 4, tokens // 2
+    rb = features // wide
     q = LINE * rb
     extra = max(1, wide.bit_length() - 5)
+    anywhere, vmem = pl.BlockSpec(memory_space=pl.ANY), pl.BlockSpec(memory_space=pltpu.VMEM)
     dma = pltpu.SemaphoreType.DMA
+    far_rows = q if wide == 16 else features // 2
+    outs = [((rb, 2 * small), F32)] * 5 + [((rb, 2 * large), F32)] * 3 + [
+        ((quarter, features), BF16),
+        ((2, q // 2, large), BF16),
+        ((2, q, large), BF16),
+        ((3, 3, rb, large), BF16),
+    ]
+    held = [
+        ((tokens, features), BF16),
+        ((tokens, features), BF16),
+        ((4, row_len, 2 * small), BF16),
+        ((tokens, small), BF16),
+        ((tokens, small), BF16),
+        ((tokens, small), BF16),
+        ((tokens, small), BF16),
+        ((tokens, small), BF16),
+        ((tokens, small), BF16),
+        ((tokens, small), BF16),
+        ((tokens, small), F32),
+        ((tokens, small), BF16),
+        ((tokens, small), BF16),
+        ((tokens, 2 * small), BF16),
+        ((tokens, 2 * small), BF16),
+        ((8, tokens), F32),
+        ((8, tokens), F32),
+        ((8, tokens), F32),
+        ((8, tokens), F32),
+        ((tokens, HEAD_DIM), F32),
+        ((row_len, features), BF16),
+        ((quarter, features), BF16),
+        ((5, features, small), BF16),
+        ((5, 2, q // 2, small), BF16),
+        ((5, 2, far_rows, small), BF16),
+        ((5, 3, rb, small), BF16),
+        ((q, large), BF16),
+        ((q, large), BF16),
+        ((2, rb, 2 * small), F32),
+        ((rb, 2 * large), F32),
+    ]
+    sems = [
+        (40,), (5, 6), (5, 6), (5, 3), (5, 3), (6,), (6,), (3, 3), (3, 3), (5,), (5,), (24,), (9,), (5, extra), (5, extra),
+    ]
     return pl.pallas_call(
-        functools.partial(reduce_kernel, wide, count),
-        out_shape=[jax.ShapeDtypeStruct((rb, 2 * cols), F32)] * count,
-        in_specs=[pl.BlockSpec(memory_space=pl.ANY)] * count,
-        out_specs=[pl.BlockSpec(memory_space=pltpu.VMEM)] * count,
-        scratch_shapes=[
-            pltpu.VMEM((count, rows, cols), BF16),
-            pltpu.VMEM((count, 2, q // 2, cols), BF16),
-            pltpu.VMEM((count, 2, q, cols), BF16),
-            pltpu.VMEM((count, 3, rb, cols), BF16),
-            pltpu.VMEM((count, extra, rows // 2 if wide > 16 else 16, cols), BF16),
-            dma((count,)),
-            dma((count, 6)),
-            dma((count, 6)),
-            dma((count, 3)),
-            dma((count, 3)),
-            dma((count, extra)),
-            dma((count, extra)),
-        ],
+        functools.partial(backward_kernel, wide, small, large),
+        out_shape=[jax.ShapeDtypeStruct(s, t) for s, t in outs],
+        in_specs=[anywhere] * 17 + [vmem] * 2,
+        out_specs=[anywhere] * len(outs),
+        scratch_shapes=[pltpu.VMEM(s, t) for s, t in held] + [dma(s) for s in sems],
         compiler_params=pltpu.CompilerParams(
-            has_side_effects=True, collective_id=2, vmem_limit_bytes=48 << 20
+            has_side_effects=True, collective_id=2, vmem_limit_bytes=60 << 20
         ),
         cost_estimate=pl.CostEstimate(flops=0, bytes_accessed=300 << 20, transcendentals=0),
-    )(*grads)
-
-
-def masks(lengths, places, rates):
-    starts, total = [], 0
-    for c in range(lengths.shape[1] - 1):
-        total = total + lengths[:, c]
-        starts.append(total)
-    starts = jnp.stack(starts, axis=1)
-    docs = jnp.sum((places[None, :, None] >= starts[:, None, :]).astype(jnp.int32), axis=2)
-    gap = places[:, None] - places[None, :]
-    allowed = (gap >= 0)[None] & (docs[:, :, None] == docs[:, None, :])
-    spread = jnp.maximum(gap, 0).astype(F32)
-    weights = jnp.exp(-rates[:, None, None] * spread[None])
-    return jnp.where(allowed[:, None], weights[None], 0.0)
+    )(*arrays)
 
 
 def ends_of(lengths, places):
@@ -782,20 +1106,11 @@
         ends_of(doc_lengths, places),
     )
 
-    width = output_w.shape[1]
-    heads = width // HEAD_DIM
-    all_heads = features // HEAD_DIM
-    head_ids = (core * 2 + half) * heads + jnp.arange(heads, dtype=jnp.int32)
-    rates = DECAY * head_ids.astype(F32) / all_heads
-    lengths = jnp.concatenate([doc_lengths, net.flip(doc_lengths, 2)])
-    decay = masks(lengths, places, rates)
-    query_sig, key_sig = sigmoid(query_pre), sigmoid(key_pre)
-    shape = (2, row_len, heads, HEAD_DIM)
-    q4, k4, v4 = (a.reshape(shape) for a in (queries, keys, values))
-    squares = net.group_sum(jnp.sum(mixed * mixed, axis=1))
+    mixed_32 = mixed.astype(F32)
+    squares = net.group_sum(jnp.sum(mixed_32 * mixed_32, axis=1))
     attn_scale = lax.rsqrt(squares / features + EPS)[:, None]
-    scaled = mixed * attn_scale
-    blended = (gate * scaled).astype(BF16)
+    blended = (gate.astype(F32) * (mixed_32 * attn_scale)).astype(BF16)
+    both_ends = jnp.concatenate([ends_of(doc_lengths, places), ends_of(net.flip(doc_lengths, 2), places)])
     norm_two = norm_scale_of(middle)
     grad_down = t_mm(cot_all, product, BF16)
     output_part = mm_t(product, down_w, BF16)
@@ -814,43 +1129,19 @@
     grad_middle = cot.astype(F32) + norm_back(middle, norm_two, grad_mid)
     branch = net.group_gather(grad_middle.astype(BF16))
     branch = after(branch, output_part, grad_down)
-    grad_down, grad_left, grad_right = (net.plane_sum(g) for g in (grad_down, grad_left, grad_right))
-    grad_down = net.line_sum(after(grad_down, branch))
-    grad_blended = mm(branch, output_w)
-    grad_output = t_mm(branch, blended, BF16)
-    grad_gate_pre = (grad_blended * scaled).astype(BF16)
-    grad_gate = t_mm(normed, grad_gate_pre, BF16)
-    grad_scaled = grad_blended * gate
-    inner = net.group_sum(jnp.sum(grad_scaled * mixed, axis=1)) / features
-    grad_mixed = (
-        attn_scale * grad_scaled - mixed * (attn_scale * attn_scale * attn_scale) * inner[:, None]
-    ).astype(BF16)
-    g4 = grad_mixed.reshape(shape)
-    grad_probs = jnp.einsum("rihd,rjhd->rhij", g4, v4, preferred_element_type=F32)
-    grad_values = jnp.einsum("rhij,rihd->rjhd", probs, g4, preferred_element_type=F32)
-    grad_value_pre = grad_values.astype(BF16).reshape(tokens, width)
-    grad_value = t_mm(normed, grad_value_pre, BF16)
-    grad_scores = (grad_probs * decay).astype(BF16)
-    grad_queries = jnp.einsum("rhij,rjhd->rihd", grad_scores, k4, preferred_element_type=F32)
-    grad_keys = jnp.einsum("rhij,rihd->rjhd", grad_scores, q4, preferred_element_type=F32)
-    grad_queries, grad_keys = (after(g, grad_down) for g in (grad_queries, grad_keys))
-    grad_left = net.line_sum(after(grad_left, grad_queries))
-    grad_query_pre = (
-        grad_queries.reshape(tokens, width) * (query_sig * (1.0 + query_pre * (1.0 - query_sig)))
-    ).astype(BF16)
-    grad_key_pre = (
-        grad_keys.reshape(tokens, width) * (key_sig * (1.0 + key_pre * (1.0 - key_sig)))
-    ).astype(BF16)
-    grad_query = t_mm(normed, grad_query_pre, BF16)
-    grad_key = t_mm(normed, grad_key_pre, BF16)
-    grad_key = after(grad_key, grad_left)
-    grad_right = net.line_sum(after(grad_right, grad_left))
-    grad_output, grad_gate, grad_value, grad_query, grad_key = reduce_weights(
-        wide, [grad_output, grad_gate, grad_value, grad_query, grad_key]
+    grad_down, grad_left = net.plane_sum(grad_down), net.plane_sum(grad_left)
+    (
+        grad_output, grad_gate, grad_value, grad_query, grad_key, grad_right, grad_left, grad_down, grad_normed, *_
+    ) = backward(
+        wide,
+        [
+            branch, normed, gate, mixed, query_pre, key_pre, queries, keys, values, probs, blended, output_w, vg_w, qk_w,
+            grad_right, grad_left, grad_down, jnp.broadcast_to(attn_scale, (tokens, HEAD_DIM)), both_ends,
+        ],
+        queries.shape[1],
+        left.shape[1],
     )
-    total = mm_t(jnp.concatenate([grad_value_pre, grad_gate_pre], axis=1), vg_w)
-    total = total + mm_t(jnp.concatenate([grad_query_pre, grad_key_pre], axis=1), qk_w)
-    grad_normed = net.group_scatter(total.astype(BF16))
+    grad_normed = grad_normed.astype(F32)
     input_grad = net.restore(grad_middle + norm_back(inputs, norm_one, grad_normed))
     return (
         layer_output,

time: 750 us -> 668 us (0.89)
  Pallas kernels: 381 us -> 445 us
  matrix products: 126 us -> 75.2 us
  waiting for transfers between devices: 87.5 us -> 54.6 us
  other arithmetic: 48.8 us -> 21.9 us
  starting transfers between devices: 28.6 us -> 5.06 us
  local copies, waits for them, and re-layouts: 50.4 us -> 37.9 us
    pallas_call x1, Pallas kernels: 104 us -> 172 us  [backward(): pl.pallas_call(functools.partial(backward_kernel, wide, small, large), ou...]
    all_to_all x3 -> x0, waiting for transfers between devices: 31.4 us -> none  [line(): lax.all_to_all(value, 'wide', 0, 0, axis_index_groups=self.lines, tiled=T...]
    dot_general x8 -> x3, matrix products: 51 us -> 31.7 us  [t_mm(): lax.dot_general(a, b, (((0,), (0,)), ((), ())), preferred_element_type=F32)]
    all_to_all x3 -> x0, starting transfers between devices: 18.2 us -> none  [line(): lax.all_to_all(value, 'wide', 0, 0, axis_index_groups=self.lines, tiled=T...]
    dot_general x5 -> x3, matrix products: 48.7 us -> 32.9 us  [mm_t(): lax.dot_general(a, b, (((1,), (1,)), ((), ())), preferred_element_type=F32)]
    dot_general x4 -> x0, matrix products: 11 us -> none  [the longest x1 4.34 us: on_device(): jnp.einsum('rihd,rjhd->rhij', g4, v4, preferred_element_type=F32)]
    unnamed x118 -> x58, local copies, waits for them, and re-layouts: 21.3 us -> 17.9 us
    ppermute x7 -> x5, waiting for transfers between devices: 55.4 us -> 53.7 us  [flip(): lax.ppermute(value, 'wide', [(w, w ^ 1 << bit) for w in range(self.wide)])]
  transfers between devices with their start and end apart: 20 -> 12, of which waited for: 8 -> 5; matrix products, arithmetic and copies ran while one was open for 24% -> 12% of each run, Pallas kernels for 14% -> 0%
where the time goes in v4:
time: 668 us; the launch traced here: 659 us
  Pallas kernels  445 us (67%)
  matrix products  75.2 us (11%)
  waiting for transfers between devices  54.6 us (8%)
  local copies, waits for them, and re-layouts  37.9 us (6%)
  other arithmetic  21.9 us (3%)
  between operations  18.9 us (3%)
    pallas_call x1, Pallas kernels, forward(): pl.pallas_call(functools.partial(forward_kernel, wide, small, large), out...  274 us
    pallas_call x1, Pallas kernels, backward(): pl.pallas_call(functools.partial(backward_kernel, wide, small, large), ou...  172 us
    ppermute x5, waiting for transfers between devices, flip(): lax.ppermute(value, 'wide', [(w, w ^ 1 << bit) for w in range(self.wide)])  53.7 us
    dot_general x3, matrix products, mm_t(): lax.dot_general(a, b, (((1,), (1,)), ((), ())), preferred_element_type=F32)  32.9 us
    dot_general x3, matrix products, t_mm(): lax.dot_general(a, b, (((0,), (0,)), ((), ())), preferred_element_type=F32)  31.7 us
    unnamed x58, local copies, waits for them, and re-layouts  17.9 us
  transfers between devices with their start and end apart: 12, of which 5 were waited for; matrix products, arithmetic and copies ran while one was open for 12% of the time, Pallas kernels for 0%

profile of v4, /device:TPU:25, one launch (start us, length us, event | category | flops | bytes accessed | tf_op | source)
XLA Modules:
  0.0 658.7 jit_solution(18230452589209642664)
XLA Ops:
  7.5 1.8 reshape.192
  9.8 1.1 multiply_reduce_fusion.2
  10.9 0.7 fusion.17
  11.6 0.8 reshape.193.refs_10_
  12.4 2.2 reshape.194
  15.1 1.6 reshape.195.refs_9_
  16.7 1.2 fusion.5.refs_8_
  22.4 5.2 add_convert_fusion.4
  28.2 273.7 %shard_map.186 = (bf16[2048,1024]{1,0:T(8,128)(2,1)}, bf16[2048,1024]{1,0:T(8,128)(2,1)}, bf16[2048,512]{1,0:T(8,128)(2,1)}, bf16[2048,1408]{1,0:T(8,128)(2,1)},...) custom-call(bf16[128,1024]{1,0:T(8,128)(2,1)} %refs_0_.1, ...), custom_call_target="tpu_custom_call" | custom-call | bytes 314572800 | tf_op jit(solution)/shard_map/pallas_call | solution.py:556
  301.9 10.6 %fusion.18 = f32[1024,1408]{1,0:T(8,128)S(1)} fusion(bf16[1024,2048]{1,0:T(8,128)(2,1)} %get-tuple-element.45, bf16[2048,1408]{1,0:T(8,128)(2,1)} %get-tuple-element.44), kind=kOutput, calls=%fused_computation.60 | convolution fusion | flops 5905580032 | bytes 15728640 | tf_op jit(solution)/shard_map/dot_general | solution.py:19
  312.5 2.4 copy-done.21
  315.0 8.8 %convolution_convert_fusion.2 = bf16[2048,1408]{1,0:T(8,128)(2,1)} fusion(bf16[1024,2048]{1,0:T(8,128)(2,1)S(1)} %copy-done.15, f32[1024,1408]{1,0:T(8,128)S(1)} %fusion.18, bf16[1024,1408]{1,0:T(8,128)(2,1)S(1)} %copy-done.20), kind=kOutput, calls=%fused_computation.3 | convolution fusion | flops 5912788992 | bytes 18612224 | tf_op jit(solution)/shard_map/dot_general | solution.py:27
  323.8 1.7 copy-done.18
  325.6 11.1 %convolution_convert_fusion = bf16[2048,1408]{1,0:T(8,128)(2,1)} fusion(bf16[1024,2048]{1,0:T(8,128)(2,1)} %get-tuple-element.45, bf16[1024,1408]{1,0:T(8,128)(2,1)S(1)} %copy-done.18), kind=kOutput, calls=%fused_computation.1 | convolution fusion | flops 5908463616 | bytes 12845056 | tf_op jit(solution)/shard_map/dot_general | solution.py:27
  336.7 13.2 %fusion.10 = f32[1024,2048]{1,0:T(8,128)} fusion(bf16[2048,1408]{1,0:T(8,128)(2,1)} %get-tuple-element.47, f32[1024,1408]{1,0:T(8,128)} %copy-done.21, bf16[1024,1408]{1,0:T(8,128)(2,1)} %get-tuple-element.46), kind=kOutput, calls=%fused_computation.52 | convolution fusion | flops 5909905408 | bytes 22806528 | tf_op jit(solution)/shard_map/dot_general | solution.py:23
  349.9 12.8 %add_convert_fusion = bf16[1024,2048]{1,0:T(8,128)(2,1)S(1)} fusion(f32[1024,2048]{1,0:T(8,128)} %fusion.10, bf16[2048,1408]{1,0:T(8,128)(2,1)} %get-tuple-element.49, f32[1024,1408]{1,0:T(8,128)} %copy-done.21, bf16[1024,1408]{1,0:T(8,128)(2,1)} %get-tuple-element.48), kind=kOutput, calls=%fused_computation | convolution fusion | flops 5914099712 | bytes 27000832 | tf_op jit(solution)/shard_map/dot_general | solution.py:23
  363.3 1.5 copy-done.19
  364.8 6.9 %convolution_convert_fusion.3 = bf16[1024,2048]{1,0:T(8,128)(2,1)S(1)} fusion(bf16[1024,1408]{1,0:T(8,128)(2,1)S(1)} %copy-done.19, bf16[2048,1408]{1,0:T(8,128)(2,1)S(1)} %bitcast.49), kind=kOutput, calls=%fused_computation.7 | convolution fusion | flops 5907677184 | bytes 12845056 | tf_op jit(solution)/shard_map/dot_general | solution.py:23
  372.6 1.5 copy-done.16
  374.1 0.9 copy-done.17
  375.0 11.9 %convolution_convert_fusion.1.refs_14_ = bf16[2048,1408]{1,0:T(8,128)(2,1)} fusion(bf16[1024,2048]{1,0:T(8,128)(2,1)S(1)} %copy-done.16, f32[1024,1408]{1,0:T(8,128)} %copy-done.21, bf16[1024,1408]{1,0:T(8,128)(2,1)S(1)} %copy-done.17), kind=kOutput, calls=%fused_computation.2 | convolution fusion | flops 5912788992 | bytes 18612224 | tf_op jit(solution)/shard_map/dot_general | solution.py:27
  387.3 9.5 %collective-permute-done.3 = bf16[256,2048]{1,0:T(8,128)(2,1)S(1)} collective-permute-done((bf16[256,2048]{1,0:T(8,128)(2,1)S(1)}, bf16[256,2048]{1,0:T(8,128)(2,1)S(1)}, u32[]{:S(2)}, u32[]{:S(2)}) %collective-permute-start.3) | collective-permute-done | bytes 1048608 | tf_op jit(solution)/shard_map/ppermute | solution.py:54
  397.8 21.6 %collective-permute-done.1 = bf16[256,2048]{1,0:T(8,128)(2,1)S(1)} collective-permute-done((bf16[256,2048]{1,0:T(8,128)(2,1)S(1)}, bf16[256,2048]{1,0:T(8,128)(2,1)S(1)}, u32[]{:S(2)}, u32[]{:S(2)}) %collective-permute-start.1) | collective-permute-done | bytes 1048608 | tf_op jit(solution)/shard_map/ppermute | solution.py:54
  419.4 2.6 fusion.11
  422.7 1.3 collective-permute-start.7
  423.9 0.8 collective-permute-done.7
  425.1 20.7 %collective-permute-done.5 = bf16[256,2048]{1,0:T(8,128)(2,1)} collective-permute-done((bf16[256,2048]{1,0:T(8,128)(2,1)}, bf16[256,2048]{1,0:T(8,128)(2,1)}, u32[]{:S(2)}, u32[]{:S(2)}) %collective-permute-start.5) | collective-permute-done | bytes 1048608 | tf_op jit(solution)/shard_map/ppermute | solution.py:54
  445.8 2.2 collective-permute-start.6
  449.0 1.9 collective-permute-done.8
  450.9 1.3 fusion.2.refs_10_
  452.3 0.7 reshape.196
  453.6 1.6 reshape.197
  455.2 3.9 pad_maximum_fusion.refs_0_
  459.2 1.0 broadcast_in_dim.73.refs_17_
  460.2 171.5 %shard_map.187 = (f32[128,1024]{1,0:T(8,128)}, f32[128,1024]{1,0:T(8,128)}, f32[128,1024]{1,0:T(8,128)}, f32[128,1024]{1,0:T(8,128)}, f32[128,1024]{1,0:T(8,128)...) custom-call(bf16[1024,2048]{1,0:T(8,128)(2,1)} %pad_maximum_fusion.r, ...), custom_call_target="tpu_custom_call" | custom-call | bytes 314572800 | tf_op jit(solution)/shard_map/pallas_call | solution.py:1055
  631.7 1.7 fusion.7
  633.6 1.8 fusion.4
  635.4 2.4 reshape.199
  637.8 2.1 copy.24
  640.0 1.8 reshape.200
  641.8 2.0 copy.41
  643.9 1.9 copy.42
  645.7 0.8 copy.43
  646.5 0.8 copy.44
  647.3 0.8 copy.45
  648.1 1.1 copy.46
  649.2 1.1 copy.47
  650.3 1.1 copy.48
  (92 shorter events, 8.3 us)
Async XLA Ops:
  7.2 3.7 copy-start.14
  7.2 451.9 %reduce-scatter.3.cloned.1.call-start = ((), (), s32[]{:S(2)}) async-start(), calls=%async_computation.2 | async-start | bytes 7208960 | tf_op jit(solution)/shard_map/reduce_scatter | solution.py:78
  7.2 12.6 %collective-permute-start.9 = (s32[1,4]{1,0:T(1,128)}, s32[1,4]{1,0:T(1,128)S(1)}, u32[]{:S(2)}, u32[]{:S(2)}) collective-permute-start(s32[1,4]{1,0:T(1,128)} %param.12), channel_id=1, source_target_pairs={{0,8},{2,10},{4,12},{6,14},{8,0},{10,2},{12,4},{14,6},{16,24},{18,... | collective-permute-start | bytes 56 | tf_op jit(solution)/shard_map/ppermute | solution.py:54
  12.4 4.3 copy-start
  301.9 13.1 %copy-start.15 = (bf16[1024,2048]{1,0:T(8,128)(2,1)S(1)}, bf16[1024,2048]{1,0:T(8,128)(2,1)}, u32[]{:S(2)}) copy-start(bf16[1024,2048]{1,0:T(8,128)(2,1)} %get-tuple-element.50) | copy-start | bytes 12582916
  301.9 13.1 %copy-start.20 = (bf16[1024,1408]{1,0:T(8,128)(2,1)S(1)}, bf16[1024,1408]{1,0:T(8,128)(2,1)}, u32[]{:S(2)}) copy-start(bf16[1024,1408]{1,0:T(8,128)(2,1)} %get-tuple-element.46) | copy-start | bytes 8650756
  312.5 2.5 copy-start.21
  323.8 1.8 copy-start.18
  323.8 135.4 %reduce-scatter.5.cloned.1.call-start = ((), (), s32[]{:S(2)}) async-start(), calls=%async_computation.3 | async-start | bytes 7208960 | tf_op jit(solution)/shard_map/reduce_scatter | solution.py:78
  349.9 13.4 %slice-start = ((s8[5767168]{0:T(1024)(128)(4,1)}), s8[1572864]{0:T(1024)(128)(4,1)S(1)}, s32[]{:S(2)}) async-start(s8[5767168]{0:T(1024)(128)(4,1)} %bitcast.48), calls=%async_computation.4 | async-start | bytes 3145728
  349.9 13.4 %slice-start.1 = ((s8[5767168]{0:T(1024)(128)(4,1)}), s8[4194304]{0:T(1024)(128)(4,1)S(1)}, s32[]{:S(2)}) async-start(s8[5767168]{0:T(1024)(128)(4,1)} %bitcast.48), calls=%async_computation.5 | async-start | bytes 8388608
  362.9 1.9 copy-start.19
  363.2 8.9 %collective-permute-start.2 = (bf16[512,2048]{1,0:T(8,128)(2,1)S(1)}, bf16[512,2048]{1,0:T(8,128)(2,1)S(1)}, u32[]{:S(2)}, u32[]{:S(2)}) collective-permute-start(bf16[512,2048]{1,0:T(8,128)(2,1)S(1)} %pad_maximum_fusion.2), channel_id=1, source_target_pairs={{0,1},{1,0},{2,3},{3,2},{4,5},{5,4},{6,7},{7,6},{8,9},{9,8},{10,11... | collective-permute-start | bytes 6291464 | tf_op jit(solution)/shard_map/ppermute | solution.py:57
  371.9 2.2 copy-start.16
  371.9 3.1 copy-start.17
  372.0 14.8 %collective-permute-start = (bf16[512,2048]{1,0:T(8,128)(2,1)S(1)}, bf16[512,2048]{1,0:T(8,128)(2,1)S(1)}, u32[]{:S(2)}, u32[]{:S(2)}) collective-permute-start(bf16[512,2048]{1,0:T(8,128)(2,1)S(1)} %pad_maximum_fusion.1), channel_id=1, source_target_pairs={{0,1},{1,0},{2,3},{3,2},{4,5},{5,4},{6,7},{7,6},{8,9},{9,8},{10,11... | collective-permute-start | bytes 6291464 | tf_op jit(solution)/shard_map/ppermute | solution.py:57
  372.5 24.3 %collective-permute-start.3 = (bf16[256,2048]{1,0:T(8,128)(2,1)S(1)}, bf16[256,2048]{1,0:T(8,128)(2,1)S(1)}, u32[]{:S(2)}, u32[]{:S(2)}) collective-permute-start(bf16[256,2048]{1,0:T(8,128)(2,1)S(1)} %add_convert_fusion.1), channel_id=1, source_target_pairs={{0,8},{2,10},{4,12},{6,14},{8,0},{10,2},{12,4},{14,6},{16,24},{18,... | collective-permute-start | bytes 3145736 | tf_op jit(solution)/shard_map/ppermute | solution.py:54
  387.2 10.1 %copy-start.5 = (f32[256,2048]{1,0:T(8,128)S(1)}, f32[256,2048]{1,0:T(8,128)}, u32[]{:S(2)}) copy-start(f32[256,2048]{1,0:T(8,128)} %get-tuple-element.42) | copy-start | bytes 6291460
  387.2 32.2 %collective-permute-start.1 = (bf16[256,2048]{1,0:T(8,128)(2,1)S(1)}, bf16[256,2048]{1,0:T(8,128)(2,1)S(1)}, u32[]{:S(2)}, u32[]{:S(2)}) collective-permute-start(bf16[256,2048]{1,0:T(8,128)(2,1)S(1)} %add_convert_fusion.3), channel_id=1, source_target_pairs={{0,8},{2,10},{4,12},{6,14},{8,0},{10,2},{12,4},{14,6},{16,24},{18,... | collective-permute-start | bytes 3145736 | tf_op jit(solution)/shard_map/ppermute | solution.py:54
  397.3 22.1 %copy-start.3 = (bf16[256,2048]{1,0:T(8,128)(2,1)S(1)}, bf16[256,2048]{1,0:T(8,128)(2,1)}, u32[]{:S(2)}) copy-start(bf16[256,2048]{1,0:T(8,128)(2,1)} %reshape.195.refs_9_) | copy-start | bytes 3145732
  419.4 3.0 copy-start.2
  419.4 29.0 %copy-start.13 = (f32[8,512]{1,0:T(8,128)S(1)}, f32[8,512]{1,0:T(8,128)}, u32[]{:S(2)}) copy-start(f32[8,512]{1,0:T(8,128)} %broadcast_in_dim.72.refs_11_) | copy-start | bytes 49156
  419.4 31.5 %copy-start.6 = (bf16[1024,512]{1,0:T(8,128)(2,1)S(1)}, bf16[1024,512]{1,0:T(8,128)(2,1)}, u32[]{:S(2)}) copy-start(bf16[1024,512]{1,0:T(8,128)(2,1)} %get-tuple-element.54.refs_2_) | copy-start | bytes 3145732
  422.1 23.7 %collective-permute-start.5 = (bf16[256,2048]{1,0:T(8,128)(2,1)}, bf16[256,2048]{1,0:T(8,128)(2,1)}, u32[]{:S(2)}, u32[]{:S(2)}) collective-permute-start(bf16[256,2048]{1,0:T(8,128)(2,1)} %get-tuple-element.76), channel_id=1, source_target_pairs={{0,8},{2,10},{4,12},{6,14},{8,0},{10,2},{12,4},{14,6},{16,24},{18,... | collective-permute-start | bytes 3145736 | tf_op jit(solution)/shard_map/ppermute | solution.py:54
  422.7 2.1 collective-permute-start.7
  424.8 30.4 %collective-permute-start.4 = (bf16[256,2048]{1,0:T(8,128)(2,1)}, bf16[256,2048]{1,0:T(8,128)(2,1)}, u32[]{:S(2)}, u32[]{:S(2)}) collective-permute-start(bf16[256,2048]{1,0:T(8,128)(2,1)} %get-tuple-element.76), channel_id=1, source_target_pairs={{0,1},{1,0},{2,3},{3,2},{4,5},{5,4},{6,7},{7,6},{8,9},{9,8},{10,11... | collective-permute-start | bytes 3145736 | tf_op jit(solution)/shard_map/ppermute | solution.py:57
  445.8 9.4 %collective-permute-start.6 = (bf16[256,2048]{1,0:T(8,128)(2,1)}, bf16[256,2048]{1,0:T(8,128)(2,1)}, u32[]{:S(2)}, u32[]{:S(2)}) collective-permute-start(bf16[256,2048]{1,0:T(8,128)(2,1)} %collective-permute-done.5), channel_id=1, source_target_pairs={{0,1},{1,0},{2,3},{3,2},{4,5},{5,4},{6,7},{7,6},{8,9},{9,8},{10,11... | collective-permute-start | bytes 3145736 | tf_op jit(solution)/shard_map/ppermute | solution.py:57
  448.0 2.9 collective-permute-start.8
  460.2 171.6 %copy-start.1 = (bf16[256,2048]{1,0:T(8,128)(2,1)S(1)}, bf16[256,2048]{1,0:T(8,128)(2,1)}, u32[]{:S(2)}) copy-start(bf16[256,2048]{1,0:T(8,128)(2,1)} %copy-done) | copy-start | bytes 3145732
  631.7 1.9 copy-start.4
  640.0 5.8 copy-start.12
  640.0 6.6 copy-start.11
  641.8 5.5 copy-start.10
  641.8 6.3 copy-start.9
  645.7 3.5 copy-start.8
  648.1 2.2 copy-start.7
Sparse Core Ops, SparseCore 0:
  323.9 65.2 reduce-scatter.2
  392.2 65.8 reduce-scatter.4

commit v5 on v4

--- a/solution.py
+++ b/solution.py
@@ -132,12 +132,12 @@
     (
         w_in, (normed_own, cot_own, x_own, ends_own),
         w_out, (normed_out, cot_out, query_pre_out, key_pre_out, gate_out, query_out, key_out, value_out, mixed_out,
-                probs_out, middle_out, mid_out, left_out, right_out, product_out),
+                probs_out, middle_out, mid_out, left_out, right_out, product_out, square_out, ends_out),
         (normed, wide_w, query_pre, key_pre, gate, query, key, value, mixed, probs, blended, part, part_core, part_far,
-         square, square_core, square_far, ends_far, mid, middle, large_w, left, right, product),
+         square, square_core, square_far, square_all, ends_far, mid, middle, large_w, left, right, product),
         (line_send, line_recv, own_sem, plane_send, plane_recv, load_sem, save_sem, token_sem, token_send, token_recv,
          small_send, small_recv),
-    ) = split_refs(refs, (8, 4, 6, 15, 24, 12))
+    ) = split_refs(refs, (8, 4, 6, 17, 25, 12))
     me, core, z, on_line, flip = place_of(wide)
     extra = list(range(4, wide.bit_length() - 1))
     plane_at = (me // 16) * 4 + me % 4
@@ -252,6 +252,7 @@
     normed_copies = token_copies(0, normed_own, normed)
     cot_copies = token_copies(1, cot_own, cot_out)
     mid_copies = token_copies(2, mid.at[rows(0)], mid)
+    square_copies = token_copies(3, square_all.at[rows(0)], square_all)
     normed_local = pltpu.make_async_copy(normed_own, normed.at[rows(0)], token_sem.at[0])
     cot_local = pltpu.make_async_copy(cot_own, cot_out.at[rows(0)], token_sem.at[1])
     ends_copy = remote(ends_own, ends_far, small_send.at[0], small_recv.at[0], far_device)
@@ -428,12 +429,16 @@
         here = pl.ds(start, tile)
         total = part[here].astype(F32) + part_core[here].astype(F32) + part_far[here].astype(F32)
         squares = square[here, 0:1] + square_core[here, 0:1] + square_far[here, 0:1]
+        square_all[here] = jnp.broadcast_to(squares, (tile, HEAD_DIM))
         total = x_own[here].astype(F32) + total * lax.rsqrt(squares / features + EPS)
         middle[here] = total
         mid[here] = (total * lax.rsqrt(jnp.mean(total * total, axis=1, keepdims=True) + EPS)).astype(BF16)
 
     start_tokens(mid_copies)
+    start_tokens(square_copies)
     save(middle, middle_out)
+    save(ends_own, ends_out.at[pl.ds(0, 8)])
+    save(ends_far, ends_out.at[pl.ds(8, 8)])
     complete(5)
     copy = load(5, 0)
     copy.start()
@@ -450,8 +455,11 @@
     cot_local.start()
     start_tokens(cot_copies)
     forward_plane(6)
+    pass_tokens(square_copies)
     mid_copies[2].wait_recv()
     left_rows(1)
+    end_tokens(square_copies)
+    save(square_all, square_out)
     save(mid, mid_out)
     save(left, left_out)
     complete(6)
@@ -475,7 +483,7 @@
     complete(7)
     cot_local.wait()
     end_tokens(cot_copies)
-    for copies in (normed_copies, cot_copies, mid_copies):
+    for copies in (normed_copies, cot_copies, mid_copies, square_copies):
         sent_tokens(copies)
     for copy in (square_near, square_diag, square_pair, part_near, part_diag, part_pair):
         copy.wait_send()
@@ -525,6 +533,8 @@
         ((tokens, large), BF16),
         ((tokens, large), BF16),
         ((tokens, large), BF16),
+        ((tokens, HEAD_DIM), F32),
+        ((16, row_len), F32),
     ]
     held = [
         ((tokens, features), BF16),
@@ -544,6 +554,7 @@
         ((tokens, HEAD_DIM), F32),
         ((row_len, HEAD_DIM), F32),
         ((quarter, HEAD_DIM), F32),
+        ((tokens, HEAD_DIM), F32),
         (ends.shape, F32),
         ((tokens, features), BF16),
         ((quarter, features), F32),
@@ -552,7 +563,7 @@
         ((tokens, large), BF16),
         ((tokens, large), BF16),
     ]
-    sems = [(8, 3), (8, 3), (8,), (8, steps), (8, steps), (8,), (14,), (2,), (3, 3), (3, 3), (7,), (7,)]
+    sems = [(8, 3), (8, 3), (8,), (8, steps), (8, steps), (8,), (17,), (2,), (4, 3), (4, 3), (7,), (7,)]
     return pl.pallas_call(
         functools.partial(forward_kernel, wide, small, large),
         out_shape=[jax.ShapeDtypeStruct(s, t) for s, t in outs],
@@ -568,21 +579,24 @@
 
 def backward_kernel(wide, small, large, *refs):
     (
-        (branch_in, normed_in, gate_in, mixed_in, query_pre_in, key_pre_in, query_in, key_in, value_in, probs_in,
-         blended_in, output_w, vg_w, qk_w, right_in, left_in, down_in, scale, ends),
-        (output_out, gate_out, value_out, query_out, key_out, right_out, left_out, down_out, normed_grad_out,
-         big_near, big_far, big_line),
-        (branch, normed, weights, gate, mixed, query_pre, key_pre, query, key, value, grad_blended, grad_mixed, blended,
-         vg_grad, qk_grad, inner, inner_core, inner_sum, inner_far, inner_col, part_core, part_far, held, near, far,
-         line, stage, added, small_result, big_result),
+        (cot_in, product_in, left_in, right_in, mid_in, middle_in, normed_in, gate_in, mixed_in, query_pre_in,
+         key_pre_in, query_in, key_in, value_in, probs_in, square_in, ends_in, output_w, vg_w, qk_w, left_w, right_w,
+         down_w),
+        (output_out, gate_out, value_out, query_out, key_out, left_out, right_out, down_out, grad_middle_out,
+         out_own, out_near, out_far, out_source, grad_own, grad_near, grad_far, branch_out, big_grad, big_near, big_far,
+         big_line, big_more),
+        (held_tokens, normed, weights, gate, mixed, query, key, value, grad_blended, grad_mixed, vg_grad, qk_grad,
+         inner, inner_core, inner_sum, inner_far, inner_col, scale, ends, part_core, part_far, out_core, grad_core, own,
+         middle, held, near, far, line, stage, added, filled, small_result, big_result),
         (load_sem, send, recv, line_send, line_recv, big_send, big_recv, big_line_send, big_line_recv, small_send,
-         small_recv, stage_sem, result_sem, more_send, more_recv),
-    ) = split_refs(refs, (19, 12, 30, 15))
+         small_recv, stage_sem, result_sem, more_send, more_recv, chunk_sem, big_more_send, big_more_recv),
+    ) = split_refs(refs, (23, 22, 34, 18))
+    branch = held_tokens
     me, core, z, on_line, flip = place_of(wide)
     extra = list(range(4, wide.bit_length() - 1))
     plane_at = (me // 16) * 4 + me % 4
     others = [on_line(k)[0] for k in (1, 2, 3)] + [flip(b) for b in [0, 1] + extra]
-    tokens, features = branch.shape
+    tokens, features = held_tokens.shape
     quarter, row_len = tokens // 4, tokens // 2
     rb = features // wide
     q = LINE * rb
@@ -590,6 +604,10 @@
     heads = small // HEAD_DIM
     near_device, far_device = (me, 1 - core), (flip(2), core)
     lower = z % 2 == 0
+    widths = [min(small, large - at) for at in range(0, large, small)]
+    products = [query, key, value]
+    lefts = [gate, mixed, grad_blended]
+    rights = [grad_mixed, vg_grad.at[:, pl.ds(0, small)], vg_grad.at[:, pl.ds(small, small)]]
 
     def remote(source, target, send_sem, recv_sem, device):
         return pltpu.make_async_remote_copy(
@@ -617,9 +635,16 @@
         copy.start()
         pending[name] = copy
 
+    def load_cut(name, source, targets):
+        for n, target in enumerate(targets):
+            load(name + str(n), source.at[:, pl.ds(n * small, widths[n])], target.at[:, pl.ds(0, widths[n])])
+
     def ready(*names):
         for name in names:
             pending[name].wait()
+
+    def ready_cut(name):
+        ready(*(name + str(n) for n in range(len(widths))))
 
     results = []
 
@@ -634,21 +659,19 @@
             results[n].wait()
             results[n] = None
 
-    load("branch", branch_in, branch)
-    for n in range(4):
-        load("output%d" % n, output_w.at[pl.ds(n * row_len, row_len)], weights.at[n, :, pl.ds(0, small)])
-    load("gate", gate_in, gate)
-    load("mixed", mixed_in, mixed)
-    load("blended", blended_in, blended)
-    load("normed", normed_in, normed)
-    load("value", value_in, value)
-    load("query", query_in, query)
-    load("key", key_in, key)
+    load("cot", cot_in, held_tokens)
+    load_cut("product", product_in, products)
+    load_cut("down", down_w, [held.at[n] for n in range(3)])
+    load_cut("right", right_in, rights)
+    load_cut("left", left_in, lefts)
+    load("mid", mid_in, normed)
+    load("middle", middle_in, middle)
+    load("own", cot_in.at[rows(0)], own)
+    load("square", square_in, scale)
+    load("ends", ends_in, ends)
     for r in range(2):
         for n in range(heads):
             load("probs%d%d" % (r, n), probs_in.at[r, n], held.at[3 + r, pl.ds(n * row_len, row_len)])
-    load("query_pre", query_pre_in, query_pre)
-    load("key_pre", key_pre_in, key_pre)
     meet([(other, core) for other in others] + [(me, 1 - core)])
 
 
@@ -743,8 +766,12 @@
             line_copy(i, k).wait_recv()
         own = held[i, pl.ds(block(0) + pl.multiple_of(z * rb, rb), rb)].astype(F32) + line[i, 1].astype(F32)
         other = line[i, 0].astype(F32) + line[i, 2].astype(F32)
-        put(small_result.at[i % 2], own, other, small)
-        return give(small_result.at[i % 2], out)
+        if small_done:
+            given(small_done[-1])
+        put(small_result, own, other, small)
+        small_done.append(give(small_result, out))
+
+    small_done = []
 
     def put(target, own, other, cols):
         @pl.when(lower)
@@ -758,82 +785,191 @@
             target[:, pl.ds(cols, cols)] = own
 
 
-    stage_count = [0]
-
-    def stage_in(source, target):
-        copy = pltpu.make_async_copy(source, target, stage_sem.at[stage_count[0]])
-        stage_count[0] += 1
+    def big_rows(n, start, size):
+        return big_grad.at[n, pl.ds(pl.multiple_of(start, min(size, rb)), size)]
+
+    def big_copy(n, j):
+        if j == 0:
+            source, target = big_rows(n, block(3), h), big_near.at[n, 0]
+        elif j == 1:
+            source, target = big_rows(n, block(3) + h, h), big_near.at[n, 1]
+        elif j == 2:
+            source, target = big_rows(n, block(1) + h, h), big_far.at[n, 0, pl.ds(h, h)]
+        elif j == 3:
+            source, target = big_rows(n, block(2), h), big_far.at[n, 1, pl.ds(0, h)]
+        elif j == 4:
+            source, target = big_rows(n, block(1), h), big_far.at[n, 0, pl.ds(0, h)]
+        else:
+            source, target = big_rows(n, block(2) + h, h), big_far.at[n, 1, pl.ds(h, h)]
+        bit = (1, 0, 0, 1, 0, 1)[j]
+        return remote(source, target, big_send.at[n, j], big_recv.at[n, j], (flip(bit), core))
+
+    def big_line_copy(n, k):
+        device, there = on_line(k)
+        return remote(
+            big_rows(n, block(0) + there * rb, rb), big_line.at[n, k - 1],
+            big_line_send.at[n, k - 1], big_line_recv.at[n, k - 1], (device, core),
+        )
+
+    def move(j, source, target):
+        copy = pltpu.make_async_copy(source, target, stage_sem.at[j])
         copy.start()
         return copy
 
-    def big_rows(start, size):
-        return right_in.at[pl.ds(pl.multiple_of(start, min(size, h)), size)]
-
-    def big_copy(j):
-        sources = (
-            lambda: big_rows(block(3), h), lambda: big_rows(block(3) + h, h), lambda: big_rows(block(1) + h, h),
-            lambda: big_rows(block(2), h), lambda: stage.at[pl.ds(0, h)], lambda: stage.at[pl.ds(h, h)],
-        )
-        targets = (
-            lambda: big_near.at[0], lambda: big_near.at[1], lambda: big_far.at[0, pl.ds(h, h)],
-            lambda: big_far.at[1, pl.ds(0, h)], lambda: big_far.at[0, pl.ds(0, h)], lambda: big_far.at[1, pl.ds(h, h)],
-        )
-        bit = (1, 0, 0, 1, 0, 1)[j]
-        return remote(sources[j](), targets[j](), big_send.at[j], big_recv.at[j], (flip(bit), core))
-
-    def big_begin():
-        for j in range(4):
-            big_copy(j).start()
-
-    def big_fold():
-        for n, (m, start) in enumerate(((1, 0), (2, h))):
-            here = pl.ds(n * h, h)
-            first = stage_in(big_rows(block(m) + start, h), stage.at[here])
-            big_copy(n).wait_recv()
-            second = stage_in(big_near.at[n], added.at[here])
-            first.wait()
-            second.wait()
-            add(stage, n * h, h, added.at[here])
-            big_copy(4 + n).start()
-
-    def big_to_line():
+    def big_add(n, start, *sources):
+        moves = [move(0, big_rows(n, start, h), stage.at[pl.ds(0, h)])]
+        for j, source in enumerate(sources):
+            moves.append(move(1 + j, source, added.at[pl.ds(j * h, h)]))
+        for copy in moves:
+            copy.wait()
+        add(stage, 0, h, *(added.at[pl.ds(j * h, h)] for j in range(len(sources))))
+        move(0, stage.at[pl.ds(0, h)], big_rows(n, start, h)).wait()
+
+    def big_begin(n, side, parts):
+        def fill(m):
+            for c, width in enumerate(widths):
+                filled[:, pl.ds(c * small, width)] = lax.dot_general(
+                    side[:, pl.ds(block(m), q)], parts[c][:, pl.ds(0, width)], (((0,), (0,)), ((), ())),
+                    preferred_element_type=F32,
+                ).astype(BF16)
+            move(3, filled, big_rows(n, block(m), q)).wait()
+
+        if extra:
+            loops(wide // LINE, fill)
+            for e in reversed(range(len(extra))):
+                size = q << (2 + e)
+                half = plane_at >> (2 + e)
+                copy = remote(
+                    big_rows(n, (half ^ 1) * size, size), big_more.at[n, e, pl.ds(0, size)],
+                    big_more_send.at[n, e], big_more_recv.at[n, e], (flip(extra[e]), core),
+                )
+                copy.start()
+                copy.wait()
+                loops(
+                    size // h,
+                    lambda i: big_add(
+                        n, half * size + i * h, big_more.at[n, e, pl.ds(pl.multiple_of(i * h, h), h)]
+                    ),
+                )
+            for j in range(4):
+                big_copy(n, j).start()
+        else:
+            fill(3)
+            big_copy(n, 0).start()
+            big_copy(n, 1).start()
+            fill(1)
+            big_copy(n, 2).start()
+            fill(2)
+            big_copy(n, 3).start()
+            fill(0)
+
+    def big_fold(n):
+        big_copy(n, 0).wait_recv()
+        big_add(n, block(1), big_near.at[n, 0])
+        big_copy(n, 4).start()
+        big_copy(n, 1).wait_recv()
+        big_add(n, block(2) + h, big_near.at[n, 1])
+        big_copy(n, 5).start()
+
+    def big_to_line(n):
         for j in range(2, 6):
-            big_copy(j).wait_recv()
-        for j in (4, 5):
-            big_copy(j).wait_send()
-        stage_in(big_rows(block(0), q), stage).wait()
-        for n in range(2):
-            a = stage_in(big_far.at[0, pl.ds(n * h, h)], added.at[pl.ds(0, h)])
-            b = stage_in(big_far.at[1, pl.ds(n * h, h)], added.at[pl.ds(h, h)])
-            a.wait()
-            b.wait()
-            add(stage, n * h, h, added.at[pl.ds(0, h)], added.at[pl.ds(h, h)])
+            big_copy(n, j).wait_recv()
+        for j in range(2):
+            here = pl.ds(j * h, h)
+            big_add(n, block(0) + j * h, big_far.at[n, 0, here], big_far.at[n, 1, here])
         for k in (1, 2, 3):
-            big_line_copy(0, k).start()
-
-    def big_line_copy(n, k):
-        device, there = on_line(k)
-        source = (stage, left_in, down_in)[n]
-        return remote(
-            source.at[pl.ds(pl.multiple_of(there * rb, rb), rb)], big_line.at[n, k - 1],
-            big_line_send.at[n, k - 1], big_line_recv.at[n, k - 1], (device, core),
-        )
+            big_line_copy(n, k).start()
 
     def big_finish(n, out):
         for k in (1, 2, 3):
             big_line_copy(n, k).wait_recv()
-        source = (stage, left_in, down_in)[n]
-        moves = [stage_in(big_line.at[n, k], added.at[pl.ds(k * rb, rb)]) for k in range(3)]
-        moves.append(stage_in(source.at[pl.ds(pl.multiple_of(z * rb, rb), rb)], added.at[pl.ds(3 * rb, rb)]))
-        for move in moves:
-            move.wait()
-        for n_big in results_of_big:
-            given(n_big)
+        moves = [move(k, big_line.at[n, k], added.at[pl.ds(k * rb, rb)]) for k in range(3)]
+        moves.append(move(3, big_rows(n, block(0) + z * rb, rb), added.at[pl.ds(3 * rb, rb)]))
+        for copy in moves:
+            copy.wait()
+        if results_of_big:
+            given(results_of_big[-1])
         got = [added[pl.ds(k * rb, rb)].astype(F32) for k in range(4)]
         put(big_result, got[3] + got[1], got[0] + got[2], large)
         results_of_big.append(give(big_result, out))
 
     results_of_big = []
+
+
+    def gate_product(r):
+        at = pl.ds(r * row_len, row_len)
+        for c, width in enumerate(widths):
+            here = pl.ds(0, width)
+            total = jnp.dot(held_tokens[at], held[c, :, here], preferred_element_type=F32)
+            grad_left = (total * rights[c][at, here].astype(F32)).astype(BF16)
+            lefts[c][at, here] = (total * lefts[c][at, here].astype(F32)).astype(BF16)
+            rights[c][at, here] = grad_left
+
+    chunk = row_len // 2
+    chunks = features // chunk
+    wide_cols = 2 * small
+
+    def chunk_copies(n, slot):
+        source = pl.ds(pl.multiple_of(n * chunk, chunk), chunk)
+        target = pl.ds(pl.multiple_of(slot * chunk, chunk), chunk)
+        return [
+            pltpu.make_async_copy(
+                w.at[source, pl.ds(at, cols)], weights.at[2 * i + j, target, pl.ds(0, cols)], chunk_sem.at[slot, 2 * i + j]
+            )
+            for i, w in enumerate((left_w, right_w))
+            for j, (at, cols) in enumerate(((0, wide_cols), (wide_cols, large - wide_cols)))
+        ]
+
+    def mid_part(r):
+        at = pl.ds(r * row_len, row_len)
+        for copy in chunk_copies(0, 0):
+            copy.start()
+
+        def body(n):
+            slot = n % 2
+
+            @pl.when(n + 1 < chunks)
+            def _():
+                for copy in chunk_copies(n + 1, 1 - slot):
+                    copy.start()
+
+            for copy in chunk_copies(n, slot):
+                copy.wait()
+            here = pl.ds(pl.multiple_of(slot * chunk, chunk), chunk)
+            total = jnp.zeros((row_len, chunk), F32)
+            for i, parts in enumerate((rights, lefts)):
+                for c, width in enumerate(widths):
+                    w = weights[2 * i + c // 2, here, pl.ds((c % 2) * small, width)]
+                    total = total + lax.dot_general(
+                        parts[c][at, pl.ds(0, width)], w, (((1,), (1,)), ((), ())), preferred_element_type=F32
+                    )
+            held_tokens[at, pl.ds(pl.multiple_of(n * chunk, chunk), chunk)] = total.astype(BF16)
+
+        loops(chunks, body)
+
+    def output_part(r):
+        at = pl.ds(r * row_len, row_len)
+
+        def body(n):
+            here = pl.ds(pl.multiple_of(n * row_len, row_len), row_len)
+            total = jnp.zeros((row_len, row_len), F32)
+            for c, width in enumerate(widths):
+                total = total + lax.dot_general(
+                    products[c][at, pl.ds(0, width)], held[c, here, pl.ds(0, width)], (((1,), (1,)), ((), ())),
+                    preferred_element_type=F32,
+                )
+            held_tokens[at, here] = total.astype(BF16)
+
+        loops(features // row_len, body)
+
+    def middle_rows(n):
+        at = pl.ds(pl.multiple_of(n * 32, 32), 32)
+        grad = held_tokens[at].astype(F32) + part_core[at].astype(F32) + part_far[at].astype(F32)
+        values = middle[at]
+        s = lax.rsqrt(jnp.mean(values * values, axis=1, keepdims=True) + EPS)
+        grad = own[at].astype(F32) + norm_back(values, s, grad)
+        middle[at] = grad
+        own[at] = grad.astype(BF16)
 
 
     def grad_rows(row):
@@ -843,18 +979,25 @@
             total = total + jnp.dot(
                 branch[at, pl.ds(n * row_len, row_len)], weights[n, :, pl.ds(0, small)], preferred_element_type=F32
             )
-        grad_blended[at] = total
+        grad_blended[at] = total.astype(BF16)
         m = mixed[at].astype(F32)
-        vg_grad[at, pl.ds(small, small)] = (total * (m * scale[at, 0:1])).astype(BF16)
+        g = gate[at].astype(F32)
+        scaled = m * scale[at, 0:1]
+        vg_grad[at, pl.ds(small, small)] = (total * scaled).astype(BF16)
+        grad_mixed[at] = (g * scaled).astype(BF16)
         inner[:, at] = lax.dot_general(
-            jnp.ones((8, small), F32), total * gate[at].astype(F32) * m, (((1,), (1,)), ((), ())),
+            jnp.ones((8, small), F32), total * g * m, (((1,), (1,)), ((), ())),
             preferred_element_type=F32, precision=lax.Precision.HIGHEST,
         )
+
+    def scale_rows(n):
+        at = pl.ds(pl.multiple_of(n * 128, 128), 128)
+        scale[at] = lax.rsqrt(scale[at] / features + EPS)
 
     def mix_rows(n):
         at = pl.ds(pl.multiple_of(n * 128, 128), 128)
         s = scale[at, 0:1]
-        value_of = s * (grad_blended[at] * gate[at].astype(F32))
+        value_of = s * (grad_blended[at].astype(F32) * gate[at].astype(F32))
         value_of = value_of - mixed[at].astype(F32) * (s * s * s * (inner_col[at, 0:1] / features))
         grad_mixed[at] = value_of.astype(BF16)
 
@@ -888,11 +1031,11 @@
                 probs, got, (((0,), (0,)), ((), ())), preferred_element_type=F32
             ).astype(BF16)
             grad_query = jnp.dot(grad_scores, key[at, cols], preferred_element_type=F32)
-            qk_grad[at, cols] = (grad_query * slope(query_pre[at, cols].astype(F32))).astype(BF16)
+            qk_grad[at, cols] = (grad_query * slope(gate[at, cols].astype(F32))).astype(BF16)
             grad_key = lax.dot_general(
                 grad_scores, query[at, cols], (((0,), (0,)), ((), ())), preferred_element_type=F32
             )
-            qk_grad[at, more] = (grad_key * slope(key_pre[at, cols].astype(F32))).astype(BF16)
+            qk_grad[at, more] = (grad_key * slope(mixed[at, cols].astype(F32))).astype(BF16)
 
         loops(heads, body)
 
@@ -911,91 +1054,158 @@
             )
             branch[at, pl.ds((2 * pair + n) * row_len, row_len)] = total.astype(BF16)
 
-
-    big_begin()
-    ready("branch", "output0", "output1", "output2", "output3", "gate", "mixed")
+    def small_copy(n, source, target, device):
+        return remote(source, target, small_send.at[n], small_recv.at[n], device)
+
+
+    ready("cot")
+    ready_cut("product")
+    big_begin(0, held_tokens, products)
+    ready_cut("down")
+    ready_cut("left")
+    ready_cut("right")
+    gate_product(1)
+    gate_product(0)
+    mid_part(1)
+    part_diag = small_copy(0, held_tokens.at[rows(3)], part_core.at[rows(1)], near_device)
+    part_near = small_copy(1, held_tokens.at[rows(1)], part_core.at[rows(0)], near_device)
+    part_pair = small_copy(2, held_tokens.at[rows(2)], part_far, far_device)
+    part_diag.start()
+    part_diag.wait_recv()
+    add(held_tokens, 2 * quarter, quarter, part_core.at[rows(1)])
+    part_pair.start()
+    big_fold(0)
+    mid_part(0)
+    part_near.start()
+    ready("mid")
+    big_begin(1, normed, rights)
+    ready("middle", "own")
+    part_near.wait_recv()
+    part_pair.wait_recv()
+    loops(quarter // 32, middle_rows)
+    branch_own = move(4, own, branch_out.at[rows(0)])
+    branch_near = small_copy(3, own, branch_out.at[rows(1)], near_device)
+    branch_far = small_copy(4, own, branch_out.at[rows(2)], far_device)
+    branch_pass = small_copy(5, branch_out.at[rows(2)], branch_out.at[rows(3)], near_device)
+    branch_far.start()
+    branch_near.start()
+    give(middle, grad_middle_out)
+    for n in range(4):
+        load("output%d" % n, output_w.at[pl.ds(n * row_len, row_len)], weights.at[n, :, pl.ds(0, small)])
+    big_to_line(0)
+    big_begin(2, normed, lefts)
+    load("gate", gate_in, gate)
+    load("mixed", mixed_in, mixed)
+    load("normed", normed_in, normed)
+    big_fold(1)
+    for copy in (part_diag, part_near, part_pair):
+        copy.wait_send()
+    output_part(1)
+    out_diag = small_copy(6, held_tokens.at[rows(3)], out_core, near_device)
+    out_diag.start()
+    output_part(0)
+    out_next = small_copy(7, held_tokens.at[rows(1)], out_near, near_device)
+    out_next.start()
+    out_mine = move(5, held_tokens.at[rows(0)], out_own)
+    out_diag.wait_recv()
+    add(held_tokens, 2 * quarter, quarter, out_core)
+    out_pair = small_copy(8, out_source, out_far, far_device)
+    move(0, held_tokens.at[rows(2)], out_source).wait()
+    out_pair.start()
+    load("value", value_in, value)
+    load("query", query_in, query)
+    load("key", key_in, key)
+    out_mine.wait()
+    out_next.wait_send()
+    out_diag.wait_send()
+    branch_own.wait()
+    branch_near.wait_recv()
+    load("branch0", branch_out.at[pl.ds(0, row_len)], branch.at[pl.ds(0, row_len)])
+    ready("square")
+    loops(tokens // 128, scale_rows)
+    branch_far.wait_recv()
+    branch_pass.start()
+    ready("branch0", "output0", "output1", "output2", "output3", "gate", "mixed")
+    grad_rows(0)
+    branch_pass.wait_recv()
+    load("branch1", branch_out.at[pl.ds(row_len, row_len)], branch.at[pl.ds(row_len, row_len)])
+    ready("branch1")
     grad_rows(1)
-    grad_rows(0)
-    core_copy = remote(inner, inner_core, small_send.at[0], small_recv.at[0], near_device)
+    core_copy = small_copy(9, inner, inner_core, near_device)
     core_copy.start()
-    ready("blended")
     core_copy.wait_recv()
     for b in range(4):
         inner_sum[:, rows(b)] = inner[:, rows(b)] + inner_core[:, rows(b ^ 1)]
-    far_copy = remote(inner_sum, inner_far, small_send.at[1], small_recv.at[1], far_device)
+    far_copy = small_copy(10, inner_sum, inner_far, far_device)
     far_copy.start()
-    begin(0, branch, lambda: blended[...])
+    begin(0, branch, lambda: grad_mixed[...])
     far_copy.wait_recv()
     for b in range(4):
         total = inner_sum[:, rows(b)] + inner_far[:, rows(b ^ 2)]
         inner_col[rows(b)] = jnp.broadcast_to(total.T[:, 0:1], (quarter, HEAD_DIM))
-    for n in (2, 1):
-        for k in (1, 2, 3):
-            big_line_copy(n, k).start()
     loops(tokens // 128, mix_rows)
+    load("query_pre", query_pre_in, gate)
+    load("key_pre", key_pre_in, mixed)
     load_weights(0)
     ready("normed")
     begin(1, normed, lambda: vg_grad[:, pl.ds(small, small)])
-    ready("value", "query", "key", "query_pre", "key_pre")
+    big_to_line(1)
+    big_fold(2)
+    ready("value", "query", "key", "query_pre", "key_pre", "ends")
     for r in range(2):
         ready(*("probs%d%d" % (r, n) for n in range(heads)))
     attend_back(1)
-    big_fold()
     fold(0)
     attend_back(0)
     begin(2, normed, lambda: vg_grad[:, pl.ds(0, small)])
     fold(1)
     begin(3, normed, lambda: qk_grad[:, pl.ds(0, small)])
     begin(4, normed, lambda: qk_grad[:, pl.ds(small, small)])
-    big_to_line()
+    big_to_line(2)
     to_line(0)
     fold(2)
     ready("vg00", "vg01", "qk00", "qk01")
     normed_part(0, 1)
     normed_part(0, 0)
     load_weights(1)
+    big_finish(0, down_out)
     to_line(1)
     ready("vg10", "vg11", "qk10", "qk11")
     normed_part(1, 1)
-    part_near = remote(branch.at[rows(1)], part_core.at[rows(0)], small_send.at[2], small_recv.at[2], near_device)
-    part_diag = remote(branch.at[rows(3)], part_core.at[rows(1)], small_send.at[3], small_recv.at[3], near_device)
-    part_pair = remote(branch.at[rows(2)], part_far, small_send.at[4], small_recv.at[4], far_device)
-    part_diag.start()
+    grad_diag = small_copy(11, branch.at[rows(3)], grad_core, near_device)
+    grad_next = small_copy(12, branch.at[rows(1)], grad_near, near_device)
+    grad_pair = small_copy(13, branch.at[rows(2)], grad_far, far_device)
+    grad_diag.start()
     normed_part(1, 0)
-    part_near.start()
-    part_diag.wait_recv()
-    add(branch, 2 * quarter, quarter, part_core.at[rows(1)])
-    part_pair.start()
+    grad_next.start()
+    give(branch.at[rows(0)], grad_own)
+    grad_diag.wait_recv()
+    add(branch, 2 * quarter, quarter, grad_core)
+    grad_pair.start()
     fold(3)
     fold(4)
+    big_finish(1, left_out)
     to_line(2)
-    big_finish(2, down_out)
-    big_finish(1, left_out)
-    first = finish(0, output_out)
-    second = finish(1, gate_out)
+    finish(0, output_out)
+    finish(1, gate_out)
     to_line(3)
-    big_finish(0, right_out)
-    given(first)
-    first = finish(2, value_out)
+    big_finish(2, right_out)
+    finish(2, value_out)
     to_line(4)
-    part_near.wait_recv()
-    part_pair.wait_recv()
-    add(part_far, 0, quarter, branch.at[rows(0)], part_core.at[rows(0)])
-    give(part_far, normed_grad_out)
-    given(second)
+    for copy in (out_next, out_pair, grad_next, grad_pair):
+        copy.wait_recv()
     finish(3, query_out)
-    given(first)
     finish(4, key_out)
-    for copy in (core_copy, far_copy, part_near, part_diag, part_pair):
+    for copy in (branch_near, branch_far, branch_pass, out_pair, core_copy, far_copy, grad_diag, grad_next, grad_pair):
         copy.wait_send()
     for i in range(5):
         for j in range(6):
             copies(i, j).wait_send()
         for k in (1, 2, 3):
             line_copy(i, k).wait_send()
-    for j in range(4):
-        big_copy(j).wait_send()
     for n in range(3):
+        for j in range(6):
+            big_copy(n, j).wait_send()
         for k in (1, 2, 3):
             big_line_copy(n, k).wait_send()
     for n in range(len(results)):
@@ -1008,54 +1218,51 @@
     rb = features // wide
     q = LINE * rb
     extra = max(1, wide.bit_length() - 5)
-    anywhere, vmem = pl.BlockSpec(memory_space=pl.ANY), pl.BlockSpec(memory_space=pltpu.VMEM)
+    anywhere = pl.BlockSpec(memory_space=pl.ANY)
     dma = pltpu.SemaphoreType.DMA
-    far_rows = q if wide == 16 else features // 2
-    outs = [((rb, 2 * small), F32)] * 5 + [((rb, 2 * large), F32)] * 3 + [
-        ((quarter, features), BF16),
-        ((2, q // 2, large), BF16),
-        ((2, q, large), BF16),
+    many = features // 2 if wide > 16 else 16
+    far_rows = max(q, many)
+    part = (quarter, features)
+    outs = [((rb, 2 * small), F32)] * 5 + [((rb, 2 * large), F32)] * 3 + [(part, F32)] + [(part, BF16)] * 7 + [
+        ((tokens, features), BF16),
+        ((3, features, large), BF16),
+        ((3, 2, q // 2, large), BF16),
+        ((3, 2, q, large), BF16),
         ((3, 3, rb, large), BF16),
+        ((3, extra, many, large), BF16),
     ]
     held = [
         ((tokens, features), BF16),
         ((tokens, features), BF16),
         ((4, row_len, 2 * small), BF16),
-        ((tokens, small), BF16),
-        ((tokens, small), BF16),
-        ((tokens, small), BF16),
-        ((tokens, small), BF16),
-        ((tokens, small), BF16),
-        ((tokens, small), BF16),
-        ((tokens, small), BF16),
-        ((tokens, small), F32),
-        ((tokens, small), BF16),
-        ((tokens, small), BF16),
+        *[((tokens, small), BF16)] * 7,
         ((tokens, 2 * small), BF16),
         ((tokens, 2 * small), BF16),
-        ((8, tokens), F32),
-        ((8, tokens), F32),
-        ((8, tokens), F32),
-        ((8, tokens), F32),
+        *[((8, tokens), F32)] * 4,
         ((tokens, HEAD_DIM), F32),
+        ((tokens, HEAD_DIM), F32),
+        ((16, row_len), F32),
         ((row_len, features), BF16),
-        ((quarter, features), BF16),
+        *[(part, BF16)] * 4,
+        (part, F32),
         ((5, features, small), BF16),
         ((5, 2, q // 2, small), BF16),
         ((5, 2, far_rows, small), BF16),
         ((5, 3, rb, small), BF16),
+        ((q // 2, large), BF16),
         ((q, large), BF16),
         ((q, large), BF16),
-        ((2, rb, 2 * small), F32),
+        ((rb, 2 * small), F32),
         ((rb, 2 * large), F32),
     ]
     sems = [
-        (40,), (5, 6), (5, 6), (5, 3), (5, 3), (6,), (6,), (3, 3), (3, 3), (5,), (5,), (24,), (9,), (5, extra), (5, extra),
+        (52,), (5, 6), (5, 6), (5, 3), (5, 3), (3, 6), (3, 6), (3, 3), (3, 3), (14,), (14,), (6,), (10,), (5, extra),
+        (5, extra), (2, 4), (3, extra), (3, extra),
     ]
     return pl.pallas_call(
         functools.partial(backward_kernel, wide, small, large),
         out_shape=[jax.ShapeDtypeStruct(s, t) for s, t in outs],
-        in_specs=[anywhere] * 17 + [vmem] * 2,
+        in_specs=[anywhere] * len(arrays),
         out_specs=[anywhere] * len(outs),
         scratch_shapes=[pltpu.VMEM(s, t) for s, t in held] + [dma(s) for s in sems],
         compiler_params=pltpu.CompilerParams(
@@ -1096,7 +1303,7 @@
     places = jnp.concatenate([own + core * quarter, own + (1 - core) * quarter])
     (
         qk_w, vg_w, output_w, left_w, right_w, down_w, normed, cot_all, query_pre, key_pre, gate, queries, keys, values,
-        mixed, probs, middle, mid, left, right, product,
+        mixed, probs, middle, mid, left, right, product, squares, ends,
     ) = forward(
         wide,
         [w_query, w_key, w_value, w_gate, w_output, w_left, w_right, w_down],
@@ -1106,42 +1313,21 @@
         ends_of(doc_lengths, places),
     )
 
-    mixed_32 = mixed.astype(F32)
-    squares = net.group_sum(jnp.sum(mixed_32 * mixed_32, axis=1))
-    attn_scale = lax.rsqrt(squares / features + EPS)[:, None]
-    blended = (gate.astype(F32) * (mixed_32 * attn_scale)).astype(BF16)
-    both_ends = jnp.concatenate([ends_of(doc_lengths, places), ends_of(net.flip(doc_lengths, 2), places)])
-    norm_two = norm_scale_of(middle)
-    grad_down = t_mm(cot_all, product, BF16)
-    output_part = mm_t(product, down_w, BF16)
-    layer_output = middle + net.group_scatter(output_part)
-    layer_output = net.restore(layer_output.astype(BF16))
-
-    grad_product = mm(cot_all, down_w)
-    grad_left_pre = (grad_product * right.astype(F32)).astype(BF16)
-    grad_right_pre = (grad_product * left.astype(F32)).astype(BF16)
-    grad_mid = net.group_scatter(
-        (mm_t(grad_left_pre, left_w) + mm_t(grad_right_pre, right_w)).astype(BF16)
-    )
-    grad_left = t_mm(mid, grad_left_pre, BF16)
-    grad_right = t_mm(mid, grad_right_pre, BF16)
-    grad_mid = after(grad_mid, grad_left, grad_right)
-    grad_middle = cot.astype(F32) + norm_back(middle, norm_two, grad_mid)
-    branch = net.group_gather(grad_middle.astype(BF16))
-    branch = after(branch, output_part, grad_down)
-    grad_down, grad_left = net.plane_sum(grad_down), net.plane_sum(grad_left)
     (
-        grad_output, grad_gate, grad_value, grad_query, grad_key, grad_right, grad_left, grad_down, grad_normed, *_
+        grad_output, grad_gate, grad_value, grad_query, grad_key, grad_left, grad_right, grad_down, grad_middle,
+        out_own, out_near, out_far, _, grad_own, grad_near, grad_far, *_
     ) = backward(
         wide,
         [
-            branch, normed, gate, mixed, query_pre, key_pre, queries, keys, values, probs, blended, output_w, vg_w, qk_w,
-            grad_right, grad_left, grad_down, jnp.broadcast_to(attn_scale, (tokens, HEAD_DIM)), both_ends,
+            cot_all, product, left, right, mid, middle, normed, gate, mixed, query_pre, key_pre, queries, keys, values,
+            probs, squares, ends, output_w, vg_w, qk_w, left_w, right_w, down_w,
         ],
         queries.shape[1],
         left.shape[1],
     )
-    grad_normed = grad_normed.astype(F32)
+    layer_output = middle + out_own.astype(F32) + out_near.astype(F32) + out_far.astype(F32)
+    layer_output = net.restore(layer_output.astype(BF16))
+    grad_normed = grad_own.astype(F32) + grad_near.astype(F32) + grad_far.astype(F32)
     input_grad = net.restore(grad_middle + norm_back(inputs, norm_one, grad_normed))
     return (
         layer_output,

time: 668 us -> 606 us (0.907)
  Pallas kernels: 445 us -> 549 us
  matrix products: 75.2 us -> 0 us
  waiting for transfers between devices: 54.6 us -> 0 us
  between operations: 18.9 us -> 2.99 us
  other arithmetic: 21.9 us -> 11.8 us
  local copies, waits for them, and re-layouts: 37.9 us -> 30.5 us
    pallas_call x1, Pallas kernels: 172 us -> 278 us  [backward(): pl.pallas_call(functools.partial(backward_kernel, wide, small, large), ou...]
    dot_general x7 -> x0, matrix products: 75.2 us -> none  [the longest x3 32.9 us: mm_t(): lax.dot_general(a, b, (((1,), (1,)), ((), ())), preferred_element_type=F32)]
    ppermute x10 -> x0, waiting for transfers between devices: 54.5 us -> none  [the longest x5 53.7 us: flip(): lax.ppermute(value, 'wide', [(w, w ^ 1 << bit) for w in range(self.wide)])]
    unnamed x58 -> x42, local copies, waits for them, and re-layouts: 17.9 us -> 8.99 us
  transfers between devices with their start and end apart: 12 -> 0, of which waited for: 5 -> 0; matrix products, arithmetic and copies ran while one was open for 12% -> 0% of each run, Pallas kernels for 0% -> 0%
where the time goes in v5:
time: 606 us; the launch traced here: 594 us
  Pallas kernels  549 us (91%)
  local copies, waits for them, and re-layouts  30.5 us (5%)
  other arithmetic  11.8 us (2%)
    pallas_call x1, Pallas kernels, backward(): pl.pallas_call(functools.partial(backward_kernel, wide, small, large), ou...  278 us
    pallas_call x1, Pallas kernels, forward(): pl.pallas_call(functools.partial(forward_kernel, wide, small, large), out...  272 us

profile of v5, /device:TPU:25, one launch (start us, length us, event | category | flops | bytes accessed | tf_op | source)
XLA Modules:
  0.0 594.3 jit_solution(16400848018490331665)
XLA Ops:
  0.7 1.4 fusion.5
  4.0 2.6 add_convert_fusion.1
  6.6 0.6 broadcast_in_dim.30.refs_11_
  7.2 1.8 reshape.110
  9.0 1.1 multiply_reduce_fusion
  10.1 0.5 copy.30
  10.6 0.8 reshape.111.refs_10_
  11.5 0.0 copy-start
  11.5 0.0 copy-start.11
  11.5 1.2 fusion.refs_8_
  12.7 0.7 copy-done.11
  13.5 0.7 reshape.112
  14.2 0.0 copy-done
  14.2 0.5 copy.29
  14.8 1.6 reshape.113.refs_9_
  16.4 271.5 %shard_map.186 = (bf16[2048,1024]{1,0:T(8,128)(2,1)}, bf16[2048,1024]{1,0:T(8,128)(2,1)}, bf16[2048,512]{1,0:T(8,128)(2,1)}, bf16[2048,1408]{1,0:T(8,128)(2,1)},...) custom-call(bf16[128,1024]{1,0:T(8,128)(2,1)} %refs_0_.1, ...), custom_call_target="tpu_custom_call" | custom-call | bytes 314572800 | tf_op jit(solution)/shard_map/pallas_call | solution.py:567
  287.9 0.0 copy-start.2
  287.9 277.6 %shard_map.187 = (f32[128,1024]{1,0:T(8,128)}, f32[128,1024]{1,0:T(8,128)}, f32[128,1024]{1,0:T(8,128)}, f32[128,1024]{1,0:T(8,128)}, f32[128,1024]{1,0:T(8,128)...) custom-call(bf16[1024,2048]{1,0:T(8,128)(2,1)} %get-tuple-element.49, ...), custom_call_target="tpu_custom_call" | custom-call | bytes 314572800 | tf_op jit(solution)/shard_map/pallas_call | solution.py:1262
  565.5 0.0 copy-done.2
  565.5 2.5 add_convert_fusion
  568.0 1.5 reshape.114
  569.6 2.9 copy.23
  572.5 2.6 reshape.115
  575.1 0.0 copy-done.1
  575.1 0.0 copy-done.3
  575.1 0.0 copy-done.5
  575.1 0.0 copy-start.4
  575.1 0.0 copy-start.6
  575.1 0.0 copy-start.7
  575.1 2.0 fusion.4
  577.1 0.0 copy-done.4
  577.1 0.0 copy-done.6
  577.2 0.1 copy-done.7
  577.3 2.4 fusion.3
  579.6 2.4 reshape.116
  582.1 2.1 copy.24
  584.2 1.8 reshape.117
  586.1 0.8 copy.39
  586.9 0.8 copy.40
  587.7 0.0 copy-done.14
  587.7 0.8 copy.41
  588.5 0.8 copy.42
  589.3 0.8 copy.43
  590.1 1.1 copy.44
  591.2 0.0 copy-done.9
  591.2 1.1 copy.45
  592.3 0.8 copy-done.8
  593.0 1.1 copy.46
  (19 shorter events, 0.0 us)
Async XLA Ops:
  11.5 2.8 copy-start
  11.5 2.0 copy-start.11
  287.9 277.6 %copy-start.2 = (f32[256,2048]{1,0:T(8,128)S(1)}, f32[256,2048]{1,0:T(8,128)}, u32[]{:S(2)}) copy-start(f32[256,2048]{1,0:T(8,128)} %get-tuple-element.48.refs_5_) | copy-start | bytes 6291460
  569.6 5.5 copy-start.1
  569.6 5.5 copy-start.3
  569.6 5.5 copy-start.5
  575.1 2.0 copy-start.4
  575.1 2.0 copy-start.6
  575.1 2.2 copy-start.7
  584.2 1.9 copy-start.16
  584.2 2.7 copy-start.15
  586.1 1.6 copy-start.14
  586.1 2.4 copy-start.13
  586.1 3.2 copy-start.12
  586.9 3.2 copy-start.10
  589.3 1.9 copy-start.9
  591.2 1.9 copy-start.8

commit v6 on v5

--- a/solution.py
+++ b/solution.py
@@ -15,94 +15,21 @@
 BF16 = jnp.bfloat16
 
 
-def mm(a, b, out=F32):
-    return lax.dot_general(a, b, (((1,), (0,)), ((), ())), preferred_element_type=F32).astype(out)
-
-
-def mm_t(a, b, out=F32):
-    return lax.dot_general(a, b, (((1,), (1,)), ((), ())), preferred_element_type=F32).astype(out)
-
-
-def t_mm(a, b, out=F32):
-    return lax.dot_general(a, b, (((0,), (0,)), ((), ())), preferred_element_type=F32).astype(out)
-
-
-def norm_scale_of(values):
-    return lax.rsqrt(jnp.mean(values * values, axis=-1, keepdims=True) + EPS)
-
-
 def norm_back(values, scale, gradient):
     inner = jnp.mean(gradient * values, axis=-1, keepdims=True)
     return scale * gradient - values * (scale * scale * scale) * inner
 
 
-def after(value, *deps):
-    return lax.optimization_barrier((value,) + deps)[0]
-
-
-class Net:
-    def __init__(self, wide):
-        self.wide = wide
-        self.me = lax.axis_index("wide")
-        self.n_plane = wide // LINE
-        self.lines = [
-            [base + 4 * k for k in range(LINE)] for base in range(wide) if not base & 12
-        ]
-        self.planes = [[w for w in range(wide) if (w >> 2) % LINE == z] for z in range(LINE)]
-
-    def flip(self, value, bit):
-        return lax.ppermute(value, "wide", [(w, w ^ (1 << bit)) for w in range(self.wide)])
-
-    def core(self, value):
-        return lax.ppermute(value, "narrow", [(0, 1), (1, 0)])
-
-    def line(self, value):
-        return lax.all_to_all(
-            value, "wide", 0, 0, axis_index_groups=self.lines, tiled=True
-        )
-
-    def permute(self, value):
-        tokens, cols = value.shape
-        value = value.reshape(tokens, self.n_plane // 4, LINE, 4, cols // self.wide)
-        return value.transpose(0, 1, 3, 2, 4).reshape(tokens, cols)
-
-    def restore(self, value):
-        tokens, cols = value.shape
-        value = value.reshape(tokens, self.n_plane // 4, 4, LINE, cols // self.wide)
-        return value.transpose(0, 1, 3, 2, 4).reshape(tokens, cols)
-
-    def gather(self, lined):
-        return lax.all_gather(lined, "wide", axis=0, axis_index_groups=self.planes, tiled=True)
-
-    def plane_sum(self, grad):
-        return lax.psum_scatter(
-            grad, "wide", scatter_dimension=0, axis_index_groups=self.planes, tiled=True
-        )
-
-    def line_sum(self, lined):
-        got = self.line(lined.reshape(LINE, -1, lined.shape[1])).astype(F32)
-        return jnp.concatenate([got[0] + got[2], got[1] + got[3]], axis=1)
-
-    def group_gather(self, value):
-        near = self.core(value)
-        far = self.flip(value, 2)
-        return jnp.concatenate([value, near, far, self.core(far)], axis=0)
-
-    def group_sum(self, value):
-        quarter = value.shape[0] // 4
-        b = value.reshape(4, quarter)
-        got = self.core(b)
-        b = b + jnp.concatenate([got[1:2], got[0:1], got[3:4], got[2:3]])
-        got = self.flip(b, 2)
-        return (b + jnp.concatenate([got[2:], got[:2]])).reshape(-1)
-
-    def group_scatter(self, value):
-        quarter = value.shape[0] // 4
-        b = [value[i * quarter : (i + 1) * quarter] for i in range(4)]
-        got = self.core(jnp.concatenate([b[1], b[3]]))
-        far = (b[2].astype(F32) + got[quarter:].astype(F32)).astype(BF16)
-        own = b[0].astype(F32) + got[:quarter].astype(F32)
-        return own + self.flip(far, 2).astype(F32)
+def to_kept(value, wide):
+    tokens, cols = value.shape
+    value = value.reshape(tokens, wide // 16, LINE, 4, cols // wide)
+    return value.transpose(0, 1, 3, 2, 4).reshape(tokens, cols)
+
+
+def from_kept(value, wide):
+    tokens, cols = value.shape
+    value = value.reshape(tokens, wide // 16, 4, LINE, cols // wide)
+    return value.transpose(0, 1, 3, 2, 4).reshape(tokens, cols)
 
 
 def place_of(wide):
@@ -130,23 +57,37 @@
 
 def forward_kernel(wide, small, large, *refs):
     (
-        w_in, (normed_own, cot_own, x_own, ends_own),
+        w_in, (cot_in, x_in, lengths),
         w_out, (normed_out, cot_out, query_pre_out, key_pre_out, gate_out, query_out, key_out, value_out, mixed_out,
-                probs_out, middle_out, mid_out, left_out, right_out, product_out, square_out, ends_out),
+                probs_out, middle_out, mid_out, left_out, right_out, product_out, square_out, ends_out, big_grad),
         (normed, wide_w, query_pre, key_pre, gate, query, key, value, mixed, probs, blended, part, part_core, part_far,
-         square, square_core, square_far, square_all, ends_far, mid, middle, large_w, left, right, product),
+         square, square_core, square_far, square_all, ends_far, mid, middle, large_w, left, right, product, x_own, ends_own,
+         filled),
         (line_send, line_recv, own_sem, plane_send, plane_recv, load_sem, save_sem, token_sem, token_send, token_recv,
-         small_send, small_recv),
-    ) = split_refs(refs, (8, 4, 6, 17, 25, 12))
+         small_send, small_recv, piece_sem),
+    ) = split_refs(refs, (8, 3, 6, 18, 28, 13))
     me, core, z, on_line, flip = place_of(wide)
     extra = list(range(4, wide.bit_length() - 1))
     plane_at = (me // 16) * 4 + me % 4
     others = [on_line(k)[0] for k in (1, 2, 3)] + [flip(b) for b in [0, 1] + extra]
+    quarter, features = x_own.shape
+    pieces = pieces_of(wide, features)
+    x_loads = [
+        pltpu.make_async_copy(x_in.at[:, pl.ds(a, size)], x_own.at[:, pl.ds(b, size)], piece_sem.at[0, n])
+        for n, (a, b, size) in enumerate(pieces)
+    ]
+    cot_loads = [
+        pltpu.make_async_copy(
+            cot_in.at[:, pl.ds(a, size)], cot_out.at[pl.ds(0, quarter), pl.ds(b, size)], piece_sem.at[1, n]
+        )
+        for n, (a, b, size) in enumerate(pieces)
+    ]
+    for copy in x_loads + cot_loads:
+        copy.start()
     meet([(other, core) for other in others] + [(me, 1 - core)])
     rb = w_in[0].shape[0]
     q = LINE * rb
     h = q // 2
-    quarter, features = x_own.shape
     row_len = 2 * quarter
     chunks = [(0, 0), (0, small), (1, 0), (1, small), (2, 0), (3, 0), (4, 0), (5, 0)]
     near_device, far_device = (me, 1 - core), (flip(2), core)
@@ -184,27 +125,37 @@
         place = part_of(i, start, size)
         return remote(place, place, plane_send.at[i, j], plane_recv.at[i, j], (flip(bit), core))
 
-    def first(i):
-        return plane(i, 0, block(0), q, 0), plane(i, 1, block(0), q, 1)
+    def first(i, k):
+        target = part_of(i, block(0) + ((z - k) % LINE) * rb, rb)
+        source = target if k else mine(i, z)
+        return [
+            remote(source, target, plane_send.at[i, 4 * b + k], plane_recv.at[i, 4 * b + k], (flip(b), core))
+            for b in (0, 1)
+        ]
 
     def second(i):
-        return plane(i, 2, block(1), h, 1), plane(i, 3, block(2) + h, h, 0)
+        return plane(i, 8, block(1), h, 1), plane(i, 9, block(2) + h, h, 0)
 
     def start_line(i):
         own_copy(i).start()
         for k in (1, 2, 3):
             line_copy(i, k).start()
 
+    def start_own(i):
+        for copy in first(i, 0):
+            copy.start()
+
     def start_plane(i):
         own_copy(i).wait()
-        for k in (1, 2, 3):
+        for k in (1, 3, 2):
             line_copy(i, k).wait_recv()
-        for copy in first(i):
-            copy.start()
+            for copy in first(i, k):
+                copy.start()
 
     def forward_plane(i):
-        for got, onward in zip(first(i), second(i)):
-            got.wait_recv()
+        for b, onward in enumerate(second(i)):
+            for k in range(LINE):
+                first(i, k)[b].wait_recv()
             onward.start()
 
     def complete(i):
@@ -212,7 +163,7 @@
             copy.wait_recv()
         for e, bit in enumerate(extra):
             size = q << (2 + e)
-            copy = plane(i, 4 + e, (plane_at >> (2 + e)) * size, size, bit)
+            copy = plane(i, 10 + e, (plane_at >> (2 + e)) * size, size, bit)
             copy.start()
             copy.wait()
 
@@ -249,12 +200,10 @@
         copy.start()
         saves.append(copy)
 
-    normed_copies = token_copies(0, normed_own, normed)
-    cot_copies = token_copies(1, cot_own, cot_out)
+    normed_copies = token_copies(0, normed.at[rows(0)], normed)
+    cot_copies = token_copies(1, cot_out.at[rows(0)], cot_out)
     mid_copies = token_copies(2, mid.at[rows(0)], mid)
     square_copies = token_copies(3, square_all.at[rows(0)], square_all)
-    normed_local = pltpu.make_async_copy(normed_own, normed.at[rows(0)], token_sem.at[0])
-    cot_local = pltpu.make_async_copy(cot_own, cot_out.at[rows(0)], token_sem.at[1])
     ends_copy = remote(ends_own, ends_far, small_send.at[0], small_recv.at[0], far_device)
 
 
@@ -342,11 +291,28 @@
         lax.fori_loop(0, quarter // tile, step, 0)
 
 
-    normed_local.start()
+    start_line(0)
+    for i in range(6):
+        start_own(i)
+    for copy in x_loads:
+        copy.wait()
+
+    @tiles
+    def _(start):
+        here = pl.ds(start, tile)
+        values = x_own[here].astype(F32)
+        normed[here] = (values * lax.rsqrt(jnp.mean(values * values, axis=1, keepdims=True) + EPS)).astype(BF16)
+
     start_tokens(normed_copies)
+    start_line(1)
+    total, ends = 0, jnp.zeros(ends_own.shape, jnp.int32)
+    places = lax.broadcasted_iota(jnp.int32, ends_own.shape, 1) + core * quarter
+    places = jnp.where(places >= row_len, places - row_len, places)
+    for c in range(lengths.shape[1]):
+        ends = ends + jnp.where(places >= total, lengths[0, c], 0)
+        total = total + lengths[0, c]
+    ends_own[...] = ends.astype(F32)
     ends_copy.start()
-    start_line(0)
-    start_line(1)
     start_plane(0)
     start_line(2)
     start_plane(1)
@@ -356,7 +322,6 @@
     start_plane(2)
     start_line(4)
     forward_plane(1)
-    normed_local.wait()
     end_tokens(normed_copies)
     save(normed, normed_out)
     complete(0)
@@ -452,7 +417,10 @@
     left_rows(0)
     pass_tokens(mid_copies)
     start_line(7)
-    cot_local.start()
+    start_own(6)
+    start_own(7)
+    for copy in cot_loads:
+        copy.wait()
     start_tokens(cot_copies)
     forward_plane(6)
     pass_tokens(square_copies)
@@ -480,20 +448,47 @@
     save(product, product_out)
     pass_tokens(cot_copies)
     forward_plane(7)
+    end_tokens(cot_copies)
+    saves[0].wait()
+    sent_tokens(normed_copies)
+    copy = pltpu.make_async_copy(cot_out, normed, token_sem.at[0])
+    copy.start()
+    copy.wait()
+
+    def down_rows(n, carry):
+        at = pl.ds(pl.multiple_of(n * row_len, row_len), row_len)
+        filled[...] = lax.dot_general(
+            normed[:, at], product[...], (((0,), (0,)), ((), ())), preferred_element_type=F32
+        ).astype(BF16)
+        copy = pltpu.make_async_copy(filled, big_grad.at[0, at], token_sem.at[1])
+        copy.start()
+        copy.wait()
+        return carry
+
+    lax.fori_loop(0, features // row_len, down_rows, 0)
     complete(7)
-    cot_local.wait()
-    end_tokens(cot_copies)
-    for copies in (normed_copies, cot_copies, mid_copies, square_copies):
+    for copies in (cot_copies, mid_copies, square_copies):
         sent_tokens(copies)
     for copy in (square_near, square_diag, square_pair, part_near, part_diag, part_pair):
         copy.wait_send()
     for i in range(8):
         for k in (1, 2, 3):
             line_copy(i, k).wait_send()
-        for copy in first(i) + second(i):
+        for k in range(LINE):
+            for copy in first(i, k):
+                copy.wait_send()
+        for copy in second(i):
             copy.wait_send()
-    for copy in saves:
+    for copy in saves[1:]:
         copy.wait()
+
+
+def pieces_of(wide, features):
+    size = features // wide
+    if size % HEAD_DIM:
+        return [(0, 0, features)]
+    places = [(w, (w // 16 * 4 + w % 4) * LINE + w // 4 % LINE) for w in range(wide)]
+    return [(whole * size, kept * size, size) for whole, kept in places]
 
 
 def split_refs(refs, counts):
@@ -504,12 +499,12 @@
     return parts
 
 
-def forward(wide, weights, normed, cot, x, ends):
+def forward(wide, weights, cot, x, lengths):
     small, large = weights[0].shape[1] // 2, weights[5].shape[1] // 2
     quarter, features = x.shape
     tokens, row_len, heads = 4 * quarter, 2 * quarter, small // HEAD_DIM
     steps = wide.bit_length() - 1
-    anywhere, vmem = pl.BlockSpec(memory_space=pl.ANY), pl.BlockSpec(memory_space=pltpu.VMEM)
+    anywhere = pl.BlockSpec(memory_space=pl.ANY)
     dma = pltpu.SemaphoreType.DMA
     outs = [
         ((features, 2 * small), BF16),
@@ -535,6 +530,7 @@
         ((tokens, large), BF16),
         ((tokens, HEAD_DIM), F32),
         ((16, row_len), F32),
+        ((3, features, large), BF16),
     ]
     held = [
         ((tokens, features), BF16),
@@ -555,42 +551,49 @@
         ((row_len, HEAD_DIM), F32),
         ((quarter, HEAD_DIM), F32),
         ((tokens, HEAD_DIM), F32),
-        (ends.shape, F32),
+        ((8, row_len), F32),
         ((tokens, features), BF16),
         ((quarter, features), F32),
         ((features, large), BF16),
         ((tokens, large), BF16),
         ((tokens, large), BF16),
         ((tokens, large), BF16),
+        ((quarter, features), BF16),
+        ((8, row_len), F32),
+        ((row_len, large), BF16),
     ]
-    sems = [(8, 3), (8, 3), (8,), (8, steps), (8, steps), (8,), (17,), (2,), (4, 3), (4, 3), (7,), (7,)]
+    sems = [
+        (8, 3), (8, 3), (8,), (8, 6 + steps), (8, 6 + steps), (8,), (17,), (2,), (4, 3), (4, 3), (7,), (7,),
+        (2, len(pieces_of(wide, features))),
+    ]
     return pl.pallas_call(
         functools.partial(forward_kernel, wide, small, large),
         out_shape=[jax.ShapeDtypeStruct(s, t) for s, t in outs],
-        in_specs=[anywhere] * 10 + [vmem] * 2,
+        in_specs=[anywhere] * 10 + [pl.BlockSpec(memory_space=pltpu.SMEM)],
         out_specs=[anywhere] * len(outs),
         scratch_shapes=[pltpu.VMEM(s, t) for s, t in held] + [dma(s) for s in sems],
         compiler_params=pltpu.CompilerParams(
             has_side_effects=True, collective_id=1, vmem_limit_bytes=60 << 20
         ),
         cost_estimate=pl.CostEstimate(flops=0, bytes_accessed=300 << 20, transcendentals=0),
-    )(*weights, normed, cot, x, ends)
+    )(*weights, cot, x, lengths)
 
 
 def backward_kernel(wide, small, large, *refs):
     (
         (cot_in, product_in, left_in, right_in, mid_in, middle_in, normed_in, gate_in, mixed_in, query_pre_in,
          key_pre_in, query_in, key_in, value_in, probs_in, square_in, ends_in, output_w, vg_w, qk_w, left_w, right_w,
-         down_w),
-        (output_out, gate_out, value_out, query_out, key_out, left_out, right_out, down_out, grad_middle_out,
+         down_w, x_in, _),
+        (output_out, gate_out, value_out, query_out, key_out, left_out, right_out, down_out, layer_out, input_grad_out,
+         grad_middle_out,
          out_own, out_near, out_far, out_source, grad_own, grad_near, grad_far, branch_out, big_grad, big_near, big_far,
          big_line, big_more),
         (held_tokens, normed, weights, gate, mixed, query, key, value, grad_blended, grad_mixed, vg_grad, qk_grad,
          inner, inner_core, inner_sum, inner_far, inner_col, scale, ends, part_core, part_far, out_core, grad_core, own,
          middle, held, near, far, line, stage, added, filled, small_result, big_result),
         (load_sem, send, recv, line_send, line_recv, big_send, big_recv, big_line_send, big_line_recv, small_send,
-         small_recv, stage_sem, result_sem, more_send, more_recv, chunk_sem, big_more_send, big_more_recv),
-    ) = split_refs(refs, (23, 22, 34, 18))
+         small_recv, stage_sem, result_sem, more_send, more_recv, chunk_sem, big_more_send, big_more_recv, piece_sem),
+    ) = split_refs(refs, (25, 24, 34, 19))
     branch = held_tokens
     me, core, z, on_line, flip = place_of(wide)
     extra = list(range(4, wide.bit_length() - 1))
@@ -825,8 +828,10 @@
         add(stage, 0, h, *(added.at[pl.ds(j * h, h)] for j in range(len(sources))))
         move(0, stage.at[pl.ds(0, h)], big_rows(n, start, h)).wait()
 
-    def big_begin(n, side, parts):
+    def big_begin(n, side=None, parts=None):
         def fill(m):
+            if side is None:
+                return
             for c, width in enumerate(widths):
                 filled[:, pl.ds(c * small, width)] = lax.dot_general(
                     side[:, pl.ds(block(m), q)], parts[c][:, pl.ds(0, width)], (((0,), (0,)), ((), ())),
@@ -1057,10 +1062,33 @@
     def small_copy(n, source, target, device):
         return remote(source, target, small_send.at[n], small_recv.at[n], device)
 
-
+    pieces = pieces_of(wide, features)
+
+    def layer_rows(n):
+        at = pl.ds(pl.multiple_of(n * 32, 32), 32)
+        total = middle[at] + own[at].astype(F32) + part_core[at].astype(F32) + part_far[at].astype(F32)
+        own[at] = total.astype(BF16)
+
+    def input_rows(n):
+        at = pl.ds(pl.multiple_of(n * 32, 32), 32)
+        grad = own[at].astype(F32) + part_core[at].astype(F32) + part_far[at].astype(F32)
+        values = part_core[pl.ds(pl.multiple_of(quarter + n * 32, 32), 32)].astype(F32)
+        s = lax.rsqrt(jnp.mean(values * values, axis=1, keepdims=True) + EPS)
+        middle[at] = middle[at] + norm_back(values, s, grad)
+
+    def put_pieces(row, source, target):
+        copies = [
+            pltpu.make_async_copy(source.at[:, pl.ds(b, size)], target.at[:, pl.ds(a, size)], piece_sem.at[row, n])
+            for n, (a, b, size) in enumerate(pieces)
+        ]
+        for copy in copies:
+            copy.start()
+        return copies
+
+
+    big_begin(0)
     ready("cot")
     ready_cut("product")
-    big_begin(0, held_tokens, products)
     ready_cut("down")
     ready_cut("left")
     ready_cut("right")
@@ -1089,7 +1117,7 @@
     branch_pass = small_copy(5, branch_out.at[rows(2)], branch_out.at[rows(3)], near_device)
     branch_far.start()
     branch_near.start()
-    give(middle, grad_middle_out)
+    middle_given = give(middle, grad_middle_out)
     for n in range(4):
         load("output%d" % n, output_w.at[pl.ds(n * row_len, row_len)], weights.at[n, :, pl.ds(0, small)])
     big_to_line(0)
@@ -1178,25 +1206,57 @@
     grad_diag.start()
     normed_part(1, 0)
     grad_next.start()
-    give(branch.at[rows(0)], grad_own)
+    grad_given = give(branch.at[rows(0)], grad_own)
     grad_diag.wait_recv()
     add(branch, 2 * quarter, quarter, grad_core)
     grad_pair.start()
     fold(3)
     fold(4)
     big_finish(1, left_out)
+    given(middle_given)
+    branch_near.wait_send()
+    branch_far.wait_send()
+    out_next.wait_recv()
+    out_pair.wait_recv()
+    load("middle2", middle_in, middle)
+    load("out_own", out_own, own)
+    load("out_near", out_near, part_core.at[rows(0)])
+    load("out_far", out_far, part_far)
     to_line(2)
+    ready("middle2", "out_own", "out_near", "out_far")
+    loops(quarter // 32, layer_rows)
+    layer_pieces = put_pieces(0, own, layer_out)
+    load("middle3", grad_middle_out, middle)
+    x_copies = [
+        pltpu.make_async_copy(x_in.at[:, pl.ds(a, size)], part_core.at[rows(1), pl.ds(b, size)], piece_sem.at[1, n])
+        for n, (a, b, size) in enumerate(pieces)
+    ]
+    for copy in x_copies:
+        copy.start()
     finish(0, output_out)
     finish(1, gate_out)
     to_line(3)
     big_finish(2, right_out)
     finish(2, value_out)
     to_line(4)
-    for copy in (out_next, out_pair, grad_next, grad_pair):
-        copy.wait_recv()
+    for copy in layer_pieces:
+        copy.wait()
+    given(grad_given)
+    grad_next.wait_recv()
+    grad_pair.wait_recv()
+    load("grad_own", grad_own, own)
+    load("grad_near", grad_near, part_core.at[rows(0)])
+    load("grad_far", grad_far, part_far)
+    for copy in x_copies:
+        copy.wait()
+    ready("middle3", "grad_own", "grad_near", "grad_far")
+    loops(quarter // 32, input_rows)
+    grad_pieces = put_pieces(2, middle, input_grad_out)
     finish(3, query_out)
     finish(4, key_out)
-    for copy in (branch_near, branch_far, branch_pass, out_pair, core_copy, far_copy, grad_diag, grad_next, grad_pair):
+    for copy in grad_pieces:
+        copy.wait()
+    for copy in (branch_pass, out_pair, core_copy, far_copy, grad_diag, grad_next, grad_pair):
         copy.wait_send()
     for i in range(5):
         for j in range(6):
@@ -1223,7 +1283,12 @@
     many = features // 2 if wide > 16 else 16
     far_rows = max(q, many)
     part = (quarter, features)
-    outs = [((rb, 2 * small), F32)] * 5 + [((rb, 2 * large), F32)] * 3 + [(part, F32)] + [(part, BF16)] * 7 + [
+    outs = [((rb, 2 * small), F32)] * 5 + [((rb, 2 * large), F32)] * 3 + [
+        (part, BF16),
+        (part, F32),
+        (part, F32),
+        *[(part, BF16)] * 7,
+
         ((tokens, features), BF16),
         ((3, features, large), BF16),
         ((3, 2, q // 2, large), BF16),
@@ -1256,8 +1321,8 @@
         ((rb, 2 * large), F32),
     ]
     sems = [
-        (52,), (5, 6), (5, 6), (5, 3), (5, 3), (3, 6), (3, 6), (3, 3), (3, 3), (14,), (14,), (6,), (10,), (5, extra),
-        (5, extra), (2, 4), (3, extra), (3, extra),
+        (60,), (5, 6), (5, 6), (5, 3), (5, 3), (3, 6), (3, 6), (3, 3), (3, 3), (14,), (14,), (6,), (10,), (5, extra),
+        (5, extra), (2, 4), (3, extra), (3, extra), (3, len(pieces_of(wide, features))),
     ]
     return pl.pallas_call(
         functools.partial(backward_kernel, wide, small, large),
@@ -1265,6 +1330,7 @@
         in_specs=[anywhere] * len(arrays),
         out_specs=[anywhere] * len(outs),
         scratch_shapes=[pltpu.VMEM(s, t) for s, t in held] + [dma(s) for s in sems],
+        input_output_aliases={24: 19},
         compiler_params=pltpu.CompilerParams(
             has_side_effects=True, collective_id=2, vmem_limit_bytes=60 << 20
         ),
@@ -1272,14 +1338,6 @@
     )(*arrays)
 
 
-def ends_of(lengths, places):
-    total, ends = 0, 0
-    for c in range(lengths.shape[1]):
-        ends = ends + jnp.where(places >= total, lengths[0, c], 0)
-        total = total + lengths[0, c]
-    return jnp.broadcast_to(ends.astype(F32)[None], (8, places.shape[0]))
-
-
 def sigmoid(z):
     return 1.0 / (1.0 + jnp.exp(-z))
 
@@ -1287,48 +1345,29 @@
 def on_device(
     layer_input, doc_lengths, w_query, w_key, w_value, w_gate, w_output, w_left, w_right, w_down, cotangent, *, wide
 ):
-    net = Net(wide)
-    core = lax.axis_index("narrow")
-    half = (net.me >> 2) & 1
     features = layer_input.shape[1]
-
-    x = net.permute(layer_input)
-    inputs = x.astype(F32)
-    norm_one = norm_scale_of(inputs)
-    cot = net.permute(cotangent)
-    quarter = inputs.shape[0]
-    tokens = 4 * quarter
-    row_len = 2 * quarter
-    own = jnp.arange(quarter, dtype=jnp.int32)
-    places = jnp.concatenate([own + core * quarter, own + (1 - core) * quarter])
+    cut = len(pieces_of(wide, features)) == 1
+    x = to_kept(layer_input, wide) if cut else layer_input
+    cot = to_kept(cotangent, wide) if cut else cotangent
+    weights = [w_query, w_key, w_value, w_gate, w_output, w_left, w_right, w_down]
     (
         qk_w, vg_w, output_w, left_w, right_w, down_w, normed, cot_all, query_pre, key_pre, gate, queries, keys, values,
-        mixed, probs, middle, mid, left, right, product, squares, ends,
-    ) = forward(
-        wide,
-        [w_query, w_key, w_value, w_gate, w_output, w_left, w_right, w_down],
-        (inputs * norm_one).astype(BF16),
-        cot,
-        x,
-        ends_of(doc_lengths, places),
-    )
-
+        mixed, probs, middle, mid, left, right, product, squares, ends, big_grad,
+    ) = forward(wide, weights, cot, x, doc_lengths)
     (
-        grad_output, grad_gate, grad_value, grad_query, grad_key, grad_left, grad_right, grad_down, grad_middle,
-        out_own, out_near, out_far, _, grad_own, grad_near, grad_far, *_
+        grad_output, grad_gate, grad_value, grad_query, grad_key, grad_left, grad_right, grad_down, layer_output,
+        input_grad, *_
     ) = backward(
         wide,
         [
             cot_all, product, left, right, mid, middle, normed, gate, mixed, query_pre, key_pre, queries, keys, values,
-            probs, squares, ends, output_w, vg_w, qk_w, left_w, right_w, down_w,
+            probs, squares, ends, output_w, vg_w, qk_w, left_w, right_w, down_w, x, big_grad,
         ],
         queries.shape[1],
         left.shape[1],
     )
-    layer_output = middle + out_own.astype(F32) + out_near.astype(F32) + out_far.astype(F32)
-    layer_output = net.restore(layer_output.astype(BF16))
-    grad_normed = grad_own.astype(F32) + grad_near.astype(F32) + grad_far.astype(F32)
-    input_grad = net.restore(grad_middle + norm_back(inputs, norm_one, grad_normed))
+    if cut:
+        layer_output, input_grad = from_kept(layer_output, wide), from_kept(input_grad, wide)
     return (
         layer_output,
         input_grad,

time: 606 us -> 552 us (0.911)
  local copies, waits for them, and re-layouts: 30.5 us -> 11.1 us
  Pallas kernels: 549 us -> 530 us
  other arithmetic: 11.8 us -> 0 us
    reshape x10 -> x0, local copies, waits for them, and re-layouts: 14.5 us -> none  [the longest x2 4.45 us: restore(): return value.transpose(0, 1, 3, 2, 4).reshape(tokens, cols)]
    pallas_call x1, Pallas kernels: 278 us -> 265 us  [backward(): pl.pallas_call(functools.partial(backward_kernel, wide, small, large), ou...]
    pallas_call x1, Pallas kernels: 272 us -> 265 us  [forward(): pl.pallas_call(functools.partial(forward_kernel, wide, small, large), out...]
    convert_element_type x3 -> x0, other arithmetic: 6.31 us -> none  [the longest x1 2.6 us: ends_of(): return jnp.broadcast_to(ends.astype(F32)[None], (8, places.shape[0]))]
where the time goes in v6:
time: 552 us; the launch traced here: 542 us
  Pallas kernels  530 us (96%)
  local copies, waits for them, and re-layouts  11.1 us (2%)
    pallas_call x1, Pallas kernels, backward(): pl.pallas_call(functools.partial(backward_kernel, wide, small, large), ou...  265 us
    pallas_call x1, Pallas kernels, forward(): pl.pallas_call(functools.partial(forward_kernel, wide, small, large), out...  265 us
    unnamed x28, local copies, waits for them, and re-layouts  11.1 us

profile of v6, /device:TPU:25, one launch (start us, length us, event | category | flops | bytes accessed | tf_op | source)
XLA Modules:
  0.0 541.8 jit_solution(15933671422087024345)
XLA Ops:
  0.6 264.7 %shard_map.186 = (bf16[2048,1024]{1,0:T(8,128)(2,1)}, bf16[2048,1024]{1,0:T(8,128)(2,1)}, bf16[2048,512]{1,0:T(8,128)(2,1)}, bf16[2048,1408]{1,0:T(8,128)(2,1)},...) custom-call(bf16[128,1024]{1,0:T(8,128)(2,1)} %refs_0_.1, ...), custom_call_target="tpu_custom_call" | custom-call | bytes 314572800 | tf_op jit(solution)/shard_map/pallas_call | solution.py:569
  265.3 264.9 %shard_map.187 = (f32[128,1024]{1,0:T(8,128)}, f32[128,1024]{1,0:T(8,128)}, f32[128,1024]{1,0:T(8,128)}, f32[128,1024]{1,0:T(8,128)}, f32[128,1024]{1,0:T(8,128)...) custom-call(bf16[1024,2048]{1,0:T(8,128)(2,1)} %get-tuple-element.44, ...), custom_call_target="tpu_custom_call", output_to_operand_aliasing={{19}: (24, {})} | custom-call | bytes 314572800 | tf_op jit(solution)/shard_map/pallas_call | solution.py:1327
  530.2 0.0 copy-start
  530.2 0.0 copy-start.8
  530.3 0.0 copy-start.7
  530.3 2.5 copy.33
  532.7 0.0 copy-done
  532.7 0.0 copy-start.6
  532.7 0.0 copy-start.5
  532.7 0.0 copy-start.4
  532.7 1.3 copy.34
  534.1 0.0 copy-done.8
  534.1 0.0 copy-start.3
  534.1 0.8 copy.35
  534.9 0.0 copy-done.7
  534.9 0.8 copy.36
  535.6 0.0 copy-done.6
  535.7 0.0 copy-start.2
  535.7 0.8 copy.37
  536.4 0.0 copy-done.5
  536.4 0.8 copy.38
  537.2 0.0 copy-done.4
  537.2 0.0 copy-start.1
  537.2 0.8 copy.39
  538.0 0.0 copy-done.3
  538.0 1.1 copy.40
  539.1 0.0 copy-done.2
  539.1 1.1 copy.41
  540.2 0.0 copy-done.1
  540.2 1.1 copy.42
Async XLA Ops:
  530.2 2.5 copy-start
  530.2 3.8 copy-start.8
  530.3 4.6 copy-start.7
  532.7 2.9 copy-start.6
  532.7 3.7 copy-start.5
  532.7 4.5 copy-start.4
  534.1 4.0 copy-start.3
  535.7 3.5 copy-start.2
  537.2 3.0 copy-start.1

commit v7 on v6

--- a/solution.py
+++ b/solution.py
@@ -9,6 +9,7 @@
 
 HEAD_DIM = 128
 LINE = 4
+LATE = 2
 EPS = 1e-06
 DECAY = 2.0
 F32 = jnp.float32
@@ -62,10 +63,10 @@
                 probs_out, middle_out, mid_out, left_out, right_out, product_out, square_out, ends_out, big_grad),
         (normed, wide_w, query_pre, key_pre, gate, query, key, value, mixed, probs, blended, part, part_core, part_far,
          square, square_core, square_far, square_all, ends_far, mid, middle, large_w, left, right, product, x_own, ends_own,
-         filled),
+         filled, cot_own, small_own, large_own),
         (line_send, line_recv, own_sem, plane_send, plane_recv, load_sem, save_sem, token_sem, token_send, token_recv,
          small_send, small_recv, piece_sem),
-    ) = split_refs(refs, (8, 3, 6, 18, 28, 13))
+    ) = split_refs(refs, (8, 3, 6, 18, 31, 13))
     me, core, z, on_line, flip = place_of(wide)
     extra = list(range(4, wide.bit_length() - 1))
     plane_at = (me // 16) * 4 + me % 4
@@ -77,9 +78,7 @@
         for n, (a, b, size) in enumerate(pieces)
     ]
     cot_loads = [
-        pltpu.make_async_copy(
-            cot_in.at[:, pl.ds(a, size)], cot_out.at[pl.ds(0, quarter), pl.ds(b, size)], piece_sem.at[1, n]
-        )
+        pltpu.make_async_copy(cot_in.at[:, pl.ds(a, size)], cot_own.at[:, pl.ds(b, size)], piece_sem.at[1, n])
         for n, (a, b, size) in enumerate(pieces)
     ]
     for copy in x_loads + cot_loads:
@@ -118,8 +117,14 @@
             line_send.at[i, k - 1], line_recv.at[i, k - 1], (device, core),
         )
 
-    def own_copy(i):
-        return pltpu.make_async_copy(mine(i, z), part_of(i, block(0) + z * rb, rb), own_sem.at[i])
+    def own_held(i):
+        return small_own.at[i] if i < 5 else large_own.at[i - 5]
+
+    def own_load(i):
+        return pltpu.make_async_copy(mine(i, z), own_held(i), own_sem.at[0, i])
+
+    def own_store(i):
+        return pltpu.make_async_copy(own_held(i), part_of(i, block(0) + z * rb, rb), own_sem.at[1, i])
 
     def plane(i, j, start, size, bit):
         place = part_of(i, start, size)
@@ -137,7 +142,7 @@
         return plane(i, 8, block(1), h, 1), plane(i, 9, block(2) + h, h, 0)
 
     def start_line(i):
-        own_copy(i).start()
+        own_load(i).start()
         for k in (1, 2, 3):
             line_copy(i, k).start()
 
@@ -146,8 +151,9 @@
             copy.start()
 
     def start_plane(i):
-        own_copy(i).wait()
-        for k in (1, 3, 2):
+        own_load(i).wait()
+        own_store(i).start()
+        for k in (1, 2, 3):
             line_copy(i, k).wait_recv()
             for copy in first(i, k):
                 copy.start()
@@ -159,6 +165,7 @@
             onward.start()
 
     def complete(i):
+        own_store(i).wait()
         for copy in second(i):
             copy.wait_recv()
         for e, bit in enumerate(extra):
@@ -201,7 +208,7 @@
         saves.append(copy)
 
     normed_copies = token_copies(0, normed.at[rows(0)], normed)
-    cot_copies = token_copies(1, cot_out.at[rows(0)], cot_out)
+    cot_copies = token_copies(1, cot_own, cot_out)
     mid_copies = token_copies(2, mid.at[rows(0)], mid)
     square_copies = token_copies(3, square_all.at[rows(0)], square_all)
     ends_copy = remote(ends_own, ends_far, small_send.at[0], small_recv.at[0], far_device)
@@ -303,8 +310,9 @@
         values = x_own[here].astype(F32)
         normed[here] = (values * lax.rsqrt(jnp.mean(values * values, axis=1, keepdims=True) + EPS)).astype(BF16)
 
+    start_line(1)
     start_tokens(normed_copies)
-    start_line(1)
+    start_line(2)
     total, ends = 0, jnp.zeros(ends_own.shape, jnp.int32)
     places = lax.broadcasted_iota(jnp.int32, ends_own.shape, 1) + core * quarter
     places = jnp.where(places >= row_len, places - row_len, places)
@@ -314,13 +322,13 @@
     ends_own[...] = ends.astype(F32)
     ends_copy.start()
     start_plane(0)
-    start_line(2)
+    start_line(3)
     start_plane(1)
-    start_line(3)
+    start_line(4)
     pass_tokens(normed_copies)
     forward_plane(0)
     start_plane(2)
-    start_line(4)
+    start_line(5)
     forward_plane(1)
     end_tokens(normed_copies)
     save(normed, normed_out)
@@ -329,14 +337,13 @@
     save(query_pre, query_pre_out)
     save(query, query_out)
     start_plane(3)
-    start_line(5)
+    start_line(6)
     forward_plane(2)
     complete(1)
     project(1, 1, keep_key)
     save(key_pre, key_pre_out)
     save(key, key_out)
     start_plane(4)
-    start_line(6)
     forward_plane(3)
     complete(2)
     project(2, 0, keep_value)
@@ -421,6 +428,8 @@
     start_own(7)
     for copy in cot_loads:
         copy.wait()
+    cot_kept = pltpu.make_async_copy(cot_own, cot_out.at[rows(0)], token_sem.at[2])
+    cot_kept.start()
     start_tokens(cot_copies)
     forward_plane(6)
     pass_tokens(square_copies)
@@ -449,6 +458,7 @@
     pass_tokens(cot_copies)
     forward_plane(7)
     end_tokens(cot_copies)
+    cot_kept.wait()
     saves[0].wait()
     sent_tokens(normed_copies)
     copy = pltpu.make_async_copy(cot_out, normed, token_sem.at[0])
@@ -561,9 +571,12 @@
         ((quarter, features), BF16),
         ((8, row_len), F32),
         ((row_len, large), BF16),
+        ((quarter, features), BF16),
+        ((5, features // wide, small), BF16),
+        ((3, features // wide, large), BF16),
     ]
     sems = [
-        (8, 3), (8, 3), (8,), (8, 6 + steps), (8, 6 + steps), (8,), (17,), (2,), (4, 3), (4, 3), (7,), (7,),
+        (8, 3), (8, 3), (2, 8), (8, 6 + steps), (8, 6 + steps), (8,), (17,), (3,), (4, 3), (4, 3), (7,), (7,),
         (2, len(pieces_of(wide, features))),
     ]
     return pl.pallas_call(
@@ -679,23 +692,33 @@
 
 
     def rows_at(i, start, size):
-        return held.at[i, pl.ds(pl.multiple_of(start, min(size, h)), size)]
+        return held.at[i, pl.ds(pl.multiple_of(start, min(size, rb)), size)]
 
     def step(i, j, start, size, target, bit):
         return remote(rows_at(i, start, size), target, send.at[i, j], recv.at[i, j], (flip(bit), core))
 
+    apart = pl.multiple_of((1 - z // 2) * h, h)
+    beside = pl.multiple_of(z // 2 * h + (1 - z % 2) * rb, rb)
+    at_z = pl.multiple_of(z * rb, rb)
+
     def copies(i, j):
         if j == 0:
-            return step(i, 0, block(3), h, near.at[i, 0], 1)
+            return step(i, 0, block(3) + apart, h, near.at[i, 0], 1)
         if j == 1:
-            return step(i, 1, block(3) + h, h, near.at[i, 1], 0)
+            return step(i, 1, block(3) + beside, rb, near.at[i, 1, pl.ds(0, rb)], 0)
         if j == 2:
-            return step(i, 2, block(1) + h, h, far.at[i, 0, pl.ds(h, h)], 0)
+            return step(i, 2, block(1) + beside, rb, far.at[i, 0, pl.ds(beside, rb)], 0)
         if j == 3:
-            return step(i, 3, block(2), h, far.at[i, 1, pl.ds(0, h)], 1)
+            return step(i, 3, block(2) + apart, h, far.at[i, 1, pl.ds(apart, h)], 1)
         if j == 4:
-            return step(i, 4, block(1), h, far.at[i, 0, pl.ds(0, h)], 0)
-        return step(i, 5, block(2) + h, h, far.at[i, 1, pl.ds(h, h)], 1)
+            return step(i, 4, block(1) + apart, h, far.at[i, 0, pl.ds(apart, h)], 0)
+        if j == 5:
+            return step(i, 5, block(2) + beside, rb, far.at[i, 1, pl.ds(beside, rb)], 1)
+        if j == 6:
+            return step(i, 6, block(3) + at_z, rb, near.at[i, 1, pl.ds(rb, rb)], 0)
+        if j == 7:
+            return step(i, 7, block(1) + at_z, rb, far.at[i, 0, pl.ds(at_z, rb)], 0)
+        return step(i, 8, block(2) + at_z, rb, far.at[i, 1, pl.ds(at_z, rb)], 1)
 
     def line_copy(i, k):
         device, there = on_line(k)
@@ -704,7 +727,7 @@
             line_send.at[i, k - 1], line_recv.at[i, k - 1], (device, core),
         )
 
-    tile = min(64, h)
+    tile = min(64, rb)
 
     def add(target, start, size, *sources):
         def body(n):
@@ -736,6 +759,8 @@
                 add(held.at[i], half * size, size, branch_more(i, e, size))
             for j in range(4):
                 copies(i, j).start()
+            if i < LATE:
+                begin_own(i)
         else:
             fill(3)
             copies(i, 0).start()
@@ -744,6 +769,8 @@
             copies(i, 2).start()
             fill(2)
             copies(i, 3).start()
+            if i < LATE:
+                begin_own(i)
             fill(0)
 
     def branch_more(i, e, size):
@@ -751,27 +778,42 @@
 
     def fold(i):
         copies(i, 0).wait_recv()
-        add(held.at[i], block(1), h, near.at[i, 0])
+        add(held.at[i], block(1) + apart, h, near.at[i, 0])
         copies(i, 4).start()
         copies(i, 1).wait_recv()
-        add(held.at[i], block(2) + h, h, near.at[i, 1])
+        add(held.at[i], block(2) + beside, rb, near.at[i, 1, pl.ds(0, rb)])
         copies(i, 5).start()
+
+    def begin_own(i):
+        copies(i, 6).start()
+        copies(i, 7).start()
+
+    def fold_own(i):
+        copies(i, 6).wait_recv()
+        add(held.at[i], block(2) + at_z, rb, near.at[i, 1, pl.ds(rb, rb)])
+        copies(i, 8).start()
 
     def to_line(i):
         for j in range(2, 6):
             copies(i, j).wait_recv()
-        add(held.at[i], block(0), q, far.at[i, 0], far.at[i, 1])
+        for start, size in ((apart, h), (beside, rb)):
+            here = pl.ds(start, size)
+            add(held.at[i], block(0) + start, size, far.at[i, 0, here], far.at[i, 1, here])
         for k in (1, 2, 3):
             line_copy(i, k).start()
 
     def finish(i, out):
+        for j in (7, 8):
+            copies(i, j).wait_recv()
+        here = pl.ds(at_z, rb)
+        add(held.at[i], block(0) + at_z, rb, far.at[i, 0, here], far.at[i, 1, here])
         for k in (1, 2, 3):
             line_copy(i, k).wait_recv()
-        own = held[i, pl.ds(block(0) + pl.multiple_of(z * rb, rb), rb)].astype(F32) + line[i, 1].astype(F32)
+        own_sum = held[i, pl.ds(pl.multiple_of(block(0) + at_z, rb), rb)].astype(F32) + line[i, 1].astype(F32)
         other = line[i, 0].astype(F32) + line[i, 2].astype(F32)
         if small_done:
             given(small_done[-1])
-        put(small_result, own, other, small)
+        put(small_result, own_sum, other, small)
         small_done.append(give(small_result, out))
 
     small_done = []
@@ -1184,9 +1226,11 @@
         ready(*("probs%d%d" % (r, n) for n in range(heads)))
     attend_back(1)
     fold(0)
+    fold_own(0)
     attend_back(0)
     begin(2, normed, lambda: vg_grad[:, pl.ds(0, small)])
     fold(1)
+    fold_own(1)
     begin(3, normed, lambda: qk_grad[:, pl.ds(0, small)])
     begin(4, normed, lambda: qk_grad[:, pl.ds(small, small)])
     big_to_line(2)
@@ -1212,6 +1256,8 @@
     grad_pair.start()
     fold(3)
     fold(4)
+    for i in range(LATE, 5):
+        begin_own(i)
     big_finish(1, left_out)
     given(middle_given)
     branch_near.wait_send()
@@ -1236,9 +1282,11 @@
     finish(0, output_out)
     finish(1, gate_out)
     to_line(3)
+    fold_own(2)
     big_finish(2, right_out)
-    finish(2, value_out)
     to_line(4)
+    fold_own(3)
+    fold_own(4)
     for copy in layer_pieces:
         copy.wait()
     given(grad_given)
@@ -1252,6 +1300,7 @@
     ready("middle3", "grad_own", "grad_near", "grad_far")
     loops(quarter // 32, input_rows)
     grad_pieces = put_pieces(2, middle, input_grad_out)
+    finish(2, value_out)
     finish(3, query_out)
     finish(4, key_out)
     for copy in grad_pieces:
@@ -1259,7 +1308,7 @@
     for copy in (branch_pass, out_pair, core_copy, far_copy, grad_diag, grad_next, grad_pair):
         copy.wait_send()
     for i in range(5):
-        for j in range(6):
+        for j in range(9):
             copies(i, j).wait_send()
         for k in (1, 2, 3):
             line_copy(i, k).wait_send()
@@ -1321,7 +1370,7 @@
         ((rb, 2 * large), F32),
     ]
     sems = [
-        (60,), (5, 6), (5, 6), (5, 3), (5, 3), (3, 6), (3, 6), (3, 3), (3, 3), (14,), (14,), (6,), (10,), (5, extra),
+        (60,), (5, 9), (5, 9), (5, 3), (5, 3), (3, 6), (3, 6), (3, 3), (3, 3), (14,), (14,), (6,), (10,), (5, extra),
         (5, extra), (2, 4), (3, extra), (3, extra), (3, len(pieces_of(wide, features))),
     ]
     return pl.pallas_call(

time: 552 us -> 544 us (0.986)
  Pallas kernels: 530 us -> 522 us
    pallas_call x1, Pallas kernels: 265 us -> 249 us  [forward(): pl.pallas_call(functools.partial(forward_kernel, wide, small, large), out...]
    pallas_call x1, Pallas kernels: 265 us -> 273 us  [backward(): pl.pallas_call(functools.partial(backward_kernel, wide, small, large), ou...]
where the time goes in v7:
time: 544 us; the launch traced here: 534 us
  Pallas kernels  522 us (96%)
  local copies, waits for them, and re-layouts  11.1 us (2%)
    pallas_call x1, Pallas kernels, backward(): pl.pallas_call(functools.partial(backward_kernel, wide, small, large), ou...  273 us
    pallas_call x1, Pallas kernels, forward(): pl.pallas_call(functools.partial(forward_kernel, wide, small, large), out...  249 us
    unnamed x28, local copies, waits for them, and re-layouts  11.1 us

profile of v7, /device:TPU:25, one launch (start us, length us, event | category | flops | bytes accessed | tf_op | source)
XLA Modules:
  0.0 534.2 jit_solution(6270336917515305263)
XLA Ops:
  0.6 248.8 %shard_map.186 = (bf16[2048,1024]{1,0:T(8,128)(2,1)}, bf16[2048,1024]{1,0:T(8,128)(2,1)}, bf16[2048,512]{1,0:T(8,128)(2,1)}, bf16[2048,1408]{1,0:T(8,128)(2,1)},...) custom-call(bf16[128,1024]{1,0:T(8,128)(2,1)} %refs_0_.1, ...), custom_call_target="tpu_custom_call" | custom-call | bytes 314572800 | tf_op jit(solution)/shard_map/pallas_call | solution.py:582
  249.4 273.2 %shard_map.187 = (f32[128,1024]{1,0:T(8,128)}, f32[128,1024]{1,0:T(8,128)}, f32[128,1024]{1,0:T(8,128)}, f32[128,1024]{1,0:T(8,128)}, f32[128,1024]{1,0:T(8,128)...) custom-call(bf16[1024,2048]{1,0:T(8,128)(2,1)} %get-tuple-element.44, ...), custom_call_target="tpu_custom_call", output_to_operand_aliasing={{19}: (24, {})} | custom-call | bytes 314572800 | tf_op jit(solution)/shard_map/pallas_call | solution.py:1376
  522.6 0.0 copy-start
  522.7 0.0 copy-start.8
  522.7 0.0 copy-start.7
  522.7 2.5 copy.33
  525.1 0.0 copy-done
  525.1 0.0 copy-start.6
  525.1 0.0 copy-start.5
  525.1 0.0 copy-start.4
  525.1 1.3 copy.34
  526.5 0.0 copy-done.8
  526.5 0.0 copy-start.3
  526.5 0.8 copy.35
  527.3 0.0 copy-done.7
  527.3 0.8 copy.36
  528.1 0.0 copy-done.6
  528.1 0.0 copy-start.2
  528.1 0.8 copy.37
  528.9 0.0 copy-done.5
  528.9 0.8 copy.38
  529.7 0.0 copy-done.4
  529.7 0.0 copy-start.1
  529.7 0.8 copy.39
  530.5 0.0 copy-done.3
  530.5 1.1 copy.40
  531.6 0.0 copy-done.2
  531.6 1.1 copy.41
  532.7 0.0 copy-done.1
  532.7 1.1 copy.42
Async XLA Ops:
  522.6 2.5 copy-start
  522.7 3.8 copy-start.8
  522.7 4.6 copy-start.7
  525.1 2.9 copy-start.6
  525.1 3.7 copy-start.5
  525.1 4.5 copy-start.4
  526.5 4.0 copy-start.3
  528.1 3.5 copy-start.2
  529.7 3.0 copy-start.1

commit v8 on v7

--- a/solution.py
+++ b/solution.py
@@ -1415,20 +1415,42 @@
         queries.shape[1],
         left.shape[1],
     )
+    results = copied(
+        [
+            layer_output, input_grad, grad_query, grad_key, grad_value, grad_gate, grad_output, grad_left, grad_right,
+            grad_down,
+        ]
+    )
     if cut:
-        layer_output, input_grad = from_kept(layer_output, wide), from_kept(input_grad, wide)
-    return (
-        layer_output,
-        input_grad,
-        grad_query,
-        grad_key,
-        grad_value,
-        grad_gate,
-        grad_output,
-        grad_left,
-        grad_right,
-        grad_down,
-    )
+        return tuple(from_kept(value, wide) for value in results[:2]) + tuple(results[2:])
+    return tuple(results)
+
+
+def copy_kernel(count, *refs):
+    sources, targets, held = refs[:count], refs[count : 2 * count], refs[2 * count : 3 * count]
+    load_sem, store_sem = refs[3 * count :]
+    loads = [pltpu.make_async_copy(sources[i], held[i], load_sem.at[i]) for i in range(count)]
+    stores = [pltpu.make_async_copy(held[i], targets[i], store_sem.at[i]) for i in range(count)]
+    for copy in loads:
+        copy.start()
+    for load, store in zip(loads, stores):
+        load.wait()
+        store.start()
+    for copy in stores:
+        copy.wait()
+
+
+def copied(arrays):
+    anywhere = pl.BlockSpec(memory_space=pl.ANY)
+    count = len(arrays)
+    return pl.pallas_call(
+        functools.partial(copy_kernel, count),
+        out_shape=[jax.ShapeDtypeStruct(a.shape, a.dtype) for a in arrays],
+        in_specs=[anywhere] * count,
+        out_specs=[anywhere] * count,
+        scratch_shapes=[pltpu.VMEM(a.shape, a.dtype) for a in arrays] + [pltpu.SemaphoreType.DMA((count,))] * 2,
+        compiler_params=pltpu.CompilerParams(vmem_limit_bytes=60 << 20),
+    )(*arrays)
 
 
 def solution(mesh):

time: 544 us -> 540 us (level)
  local copies, waits for them, and re-layouts: 11.1 us -> 0 us
  Pallas kernels: 522 us -> 529 us
    unnamed x28 -> x0, local copies, waits for them, and re-layouts: 11.1 us -> none
    pallas_call x0 -> x1, Pallas kernels: none -> 7.43 us  [copied(): pl.pallas_call(functools.partial(copy_kernel, count), out_shape=[jax.Shap...]
where the time goes in v8:
time: 540 us; the launch traced here: 531 us
  Pallas kernels  529 us (98%)
    pallas_call x1, Pallas kernels, backward(): pl.pallas_call(functools.partial(backward_kernel, wide, small, large), ou...  273 us
    pallas_call x1, Pallas kernels, forward(): pl.pallas_call(functools.partial(forward_kernel, wide, small, large), out...  249 us

profile of v8, /device:TPU:25, one launch (start us, length us, event | category | flops | bytes accessed | tf_op | source)
XLA Modules:
  0.0 530.6 jit_solution(3257585474153029612)
XLA Ops:
  0.6 248.8 %shard_map.186 = (bf16[2048,1024]{1,0:T(8,128)(2,1)}, bf16[2048,1024]{1,0:T(8,128)(2,1)}, bf16[2048,512]{1,0:T(8,128)(2,1)}, bf16[2048,1408]{1,0:T(8,128)(2,1)},...) custom-call(bf16[128,1024]{1,0:T(8,128)(2,1)} %refs_0_.1, ...), custom_call_target="tpu_custom_call" | custom-call | bytes 314572800 | tf_op jit(solution)/shard_map/pallas_call | solution.py:582
  249.4 273.2 %shard_map.187 = (f32[128,1024]{1,0:T(8,128)}, f32[128,1024]{1,0:T(8,128)}, f32[128,1024]{1,0:T(8,128)}, f32[128,1024]{1,0:T(8,128)}, f32[128,1024]{1,0:T(8,128)...) custom-call(bf16[1024,2048]{1,0:T(8,128)(2,1)} %get-tuple-element.44, ...), custom_call_target="tpu_custom_call", output_to_operand_aliasing={{19}: (24, {})} | custom-call | bytes 314572800 | tf_op jit(solution)/shard_map/pallas_call | solution.py:1376
  522.7 7.4 %shard_map.188 = (bf16[256,2048]{1,0:T(8,128)(2,1)}, f32[256,2048]{1,0:T(8,128)}, f32[128,1024]{1,0:T(8,128)}, f32[128,1024]{1,0:T(8,128)}, f32[128,1024]{1,0:T(...) custom-call(bf16[256,2048]{1,0:T(8,128)(2,1)} %get-tuple-element.68., ...), custom_call_target="tpu_custom_call" | custom-call | tf_op jit(solution)/shard_map/pallas_call | solution.py:1446
